TPU v7x, 32 devices: a whole 2x2x4 slice. The times are simulated.
32 devices in a mesh: row: 4 (over x, core), col: 8 (over z, y).
Axes of the slice: x: 2, y: 2, z: 4, core: 2. Of those that a mesh axis runs over, the one named last changes fastest.
Arguments:
- block_input: bfloat16 [2, 32, 128, 192], P(None, 'row', 'col'), may hold values from -40 to 40
- cotangent: bfloat16 [2, 32, 128, 192], P(None, 'row', 'col'), may hold values from -6 to 6
- qkv_weight: bfloat16 [2, 192, 576], replicated, may hold values from -0.4375 to 0.4375
- proj_weight: bfloat16 [2, 192, 192], replicated, may hold values from -0.4375 to 0.4375
- expand_weight: bfloat16 [2, 192, 768], replicated, may hold values from -0.4375 to 0.4375
- reduce_weight: bfloat16 [2, 768, 192], replicated, may hold values from -0.21875 to 0.21875
- bias_table: float32 [2, 6, 225], replicated, may hold values from -6 to 320
Outputs:
- input_grad: float32 [2, 32, 128, 192], P(None, 'row', 'col')
- qkv_grad: float32 [2, 192, 576], replicated
- proj_grad: float32 [2, 192, 192], replicated
- expand_grad: float32 [2, 192, 768], replicated
- reduce_grad: float32 [2, 768, 192], replicated
- table_grad: float32 [2, 6, 225], replicated
All inputs are finite; a program needn't handle non-finite values.
Results may differ from a plain program's by a relative error of at most 0.02.
Values may be sent and summed in bfloat16 or wider, within the bound.
No kernel may reach another device: no remote copies, remote signals or barrier semaphores. Data moves between devices by JAX's collectives and lax.ppermute only.
A program may use at most 64 MiB of HBM per device.

v0:
```python
import math

import jax
import jax.numpy as jnp
from jax import lax
from jax.sharding import PartitionSpec as P

WIN = 8
SHIFT = 4


def from_behind(block, axis, distance):
    devices = range(lax.axis_size(axis))
    route = [((i - distance) % len(devices), i) for i in devices]
    return lax.ppermute(block, axis, route)


def layer_norm(field):
    center = field - jnp.mean(field, axis=-1, keepdims=True)
    spread = jnp.mean(center * center, axis=-1, keepdims=True)
    return center * lax.rsqrt(spread + 1e-05)


def to_windows(field):
    frames, rows, cols, width = field.shape
    shaped = field.reshape(frames, rows // WIN, WIN, cols // WIN, WIN, width)
    return shaped.transpose(0, 1, 3, 2, 4, 5).reshape(-1, WIN * WIN, width)


def from_windows(windows, frames, rows, cols):
    shaped = windows.reshape(frames, rows // WIN, cols // WIN, WIN, WIN, -1)
    return shaped.transpose(0, 1, 3, 2, 4, 5).reshape(frames, rows, cols, -1)


def offset_onehot():
    places = jnp.arange(WIN * WIN, dtype=jnp.int32)
    prow = places // WIN
    pcol = places % WIN
    index = (prow[:, None] - prow[None, :] + WIN - 1) * (2 * WIN - 1) + (
        pcol[:, None] - pcol[None, :] + WIN - 1
    )
    entries = jnp.arange((2 * WIN - 1) ** 2, dtype=jnp.int32)
    return (entries[:, None] == index.reshape(-1)[None, :]).astype(jnp.float32)


def window_mask(row_start, col_start, rows, cols, height, breadth):
    row_ids = row_start + jnp.arange(rows, dtype=jnp.int32)
    col_ids = col_start + jnp.arange(cols, dtype=jnp.int32)
    label = (row_ids >= height - WIN // 2).astype(jnp.int32)[:, None] * 2 + (
        col_ids >= breadth - WIN // 2
    ).astype(jnp.int32)[None, :]
    label = (
        label.reshape(rows // WIN, WIN, cols // WIN, WIN)
        .transpose(0, 2, 1, 3)
        .reshape(-1, WIN * WIN)
    )
    return jnp.where(label[:, :, None] == label[:, None, :], 0.0, -10000.0).astype(jnp.float32)


def block_tile(field, weights, masking):
    frames, rows, cols, width = field.shape
    qkv_w, proj_w, expand_w, reduce_w, table = weights
    heads = table.shape[0]
    head = width // heads
    windows = to_windows(field)
    count = windows.shape[0]
    normed = layer_norm(windows).astype(jnp.bfloat16).reshape(-1, width)
    mixed = jnp.dot(normed, qkv_w, preferred_element_type=jnp.float32).reshape(
        count, WIN * WIN, 3, heads, head
    )
    query = (mixed[:, :, 0] * head ** (-0.5)).astype(jnp.bfloat16)
    keys = mixed[:, :, 1].astype(jnp.bfloat16)
    values = mixed[:, :, 2].astype(jnp.bfloat16)
    scores = jnp.einsum("nqhd,nkhd->nhqk", query, keys, preferred_element_type=jnp.float32)
    bias = jnp.dot(table, offset_onehot(), precision=lax.Precision.HIGHEST).reshape(
        heads, WIN * WIN, WIN * WIN
    )
    scores = scores + bias[None]
    if masking is not None:
        scores = (
            scores.reshape(frames, -1, heads, WIN * WIN, WIN * WIN) + masking[None, :, None]
        ).reshape(count, heads, WIN * WIN, WIN * WIN)
    top = lax.stop_gradient(jnp.max(scores, axis=-1, keepdims=True))
    expos = jnp.exp(scores - top)
    probs = (expos / jnp.sum(expos, axis=-1, keepdims=True)).astype(jnp.bfloat16)
    attended = jnp.einsum("nhqk,nkhd->nqhd", probs, values, preferred_element_type=jnp.float32)
    attended = attended.reshape(-1, width).astype(jnp.bfloat16)
    resid = windows + jnp.dot(attended, proj_w, preferred_element_type=jnp.float32).reshape(
        count, WIN * WIN, width
    )
    normed_two = layer_norm(resid).astype(jnp.bfloat16).reshape(-1, width)
    hidden = jax.nn.gelu(
        jnp.dot(normed_two, expand_w, preferred_element_type=jnp.float32), approximate=False
    ).astype(jnp.bfloat16)
    result = resid + jnp.dot(hidden, reduce_w, preferred_element_type=jnp.float32).reshape(
        count, WIN * WIN, width
    )
    return from_windows(result, frames, rows, cols)


def advance(field):
    frames, rows, cols, width = field.shape
    upper = field[:, :SHIFT].reshape(frames, SHIFT, cols * width)
    below = (
        from_behind(upper.astype(jnp.bfloat16), "row", -1)
        .astype(upper.dtype)
        .reshape(frames, SHIFT, cols, width)
    )
    field = jnp.concatenate([field[:, SHIFT:], below], axis=1)
    leftmost = field[:, :, :SHIFT].reshape(frames, rows, SHIFT * width)
    beyond = (
        from_behind(leftmost.astype(jnp.bfloat16), "col", -1)
        .astype(leftmost.dtype)
        .reshape(frames, rows, SHIFT, width)
    )
    return jnp.concatenate([field[:, :, SHIFT:], beyond], axis=2)


def advance_cotangent(field):
    frames, rows, cols, width = field.shape
    upper = field[:, :SHIFT].reshape(frames, SHIFT, cols * width)
    below = from_behind(upper, "row", -1).reshape(frames, SHIFT, cols, width)
    field = jnp.concatenate([field[:, SHIFT:], below], axis=1)
    leftmost = field[:, :, :SHIFT].reshape(frames, rows, SHIFT * width)
    beyond = from_behind(leftmost, "col", -1).reshape(frames, rows, SHIFT, width)
    return jnp.concatenate([field[:, :, SHIFT:], beyond], axis=2)


def retreat(field):
    frames, rows, cols, width = field.shape
    lowest = field[:, rows - SHIFT :].reshape(frames, SHIFT, cols * width)
    above = (
        from_behind(lowest.astype(jnp.bfloat16), "row", 1)
        .astype(lowest.dtype)
        .reshape(frames, SHIFT, cols, width)
    )
    field = jnp.concatenate([above, field[:, : rows - SHIFT]], axis=1)
    rightmost = field[:, :, cols - SHIFT :].reshape(frames, rows, SHIFT * width)
    before = (
        from_behind(rightmost.astype(jnp.bfloat16), "col", 1)
        .astype(rightmost.dtype)
        .reshape(frames, rows, SHIFT, width)
    )
    return jnp.concatenate([before, field[:, :, : cols - SHIFT]], axis=2)


def local(
    block_input, cotangent, qkv_weight, proj_weight, expand_weight, reduce_weight, bias_table
):
    frames, rows, cols, width = block_input.shape
    height = rows * lax.axis_size("row")
    breadth = cols * lax.axis_size("col")
    plain = (qkv_weight[0], proj_weight[0], expand_weight[0], reduce_weight[0], bias_table[0])
    shifted = (qkv_weight[1], proj_weight[1], expand_weight[1], reduce_weight[1], bias_table[1])
    first_out, first_back = jax.vjp(
        lambda field, weights: block_tile(field, weights, None),
        block_input.astype(jnp.float32),
        plain,
    )
    moved = advance(first_out)
    masking = window_mask(
        lax.axis_index("row") * rows, lax.axis_index("col") * cols, rows, cols, height, breadth
    )
    second_out, second_back = jax.vjp(
        lambda field, weights: block_tile(field, weights, masking), moved, shifted
    )
    turned = advance_cotangent(cotangent).astype(jnp.float32)
    rolled_grad, shift_grads = second_back(turned)
    shift_grads = tuple((piece.astype(jnp.float32) for piece in shift_grads))
    middle = retreat(rolled_grad)
    input_grad, plain_grads = first_back(middle)
    plain_grads = tuple((piece.astype(jnp.float32) for piece in plain_grads))
    summed = lax.psum(
        (
            plain_grads[0],
            plain_grads[1],
            plain_grads[2],
            plain_grads[3],
            plain_grads[4],
            shift_grads[0],
            shift_grads[1],
            shift_grads[2],
            shift_grads[3],
            shift_grads[4],
        ),
        ("row", "col"),
    )
    plain_grads = summed[:5]
    shift_grads = summed[5:]
    factor = 1.0 / math.sqrt(frames * height * breadth)
    stacked = [
        jnp.stack([plain_grads[member], shift_grads[member]]) * factor for member in range(5)
    ]
    return (input_grad, stacked[0], stacked[1], stacked[2], stacked[3], stacked[4])


def solution(mesh):
    in_specs = (P(None, "row", "col", None), P(None, "row", "col", None), P(), P(), P(), P(), P())
    out_specs = (P(None, "row", "col", None), P(), P(), P(), P(), P())
    return jax.shard_map(local, mesh=mesh, in_specs=in_specs, out_specs=out_specs, check_vma=False)
```

profile of v0, /device:TPU:0, one launch (start us, length us, event | category | flops | bytes accessed | tf_op | source)
XLA Modules:
  0.0 241.1 jit_solution(12141002322793085635)
XLA Ops:
  8.3 2.4 %collective-permute-start = (bf16[2,4,3072]{2,1,0:T(4,128)(2,1)S(1)}, bf16[2,4,3072]{2,1,0:T(4,128)(2,1)S(1)}, u32[]{:S(2)}, u32[]{:S(2)}) collective-permute-start(bf16[2,4,3072]{2,1,0:T(4,128)(2,1)S(1)} %reshape.668), channel_id=1, source_target_pairs={{8,0},{16,8},{24,16},{0,24},{9,1},{17,9},{25,17},{1,25},{10,2},{18... | collective-permute-start | bytes 147464 | tf_op jit(solution)/shard_map/ppermute | solution.py:15
  13.5 1.1 multiply_reduce_fusion.7
  15.0 1.3 convolution_bitcast_fusion.1
  19.8 2.8 %multiply_convert_fusion.1 = (bf16[256,768]{1,0:T(8,128)(2,1)S(1)}, f32[256,768]{1,0:T(8,128)}, f32[256,768]{1,0:T(8,128)}) fusion(bf16[256,192]{1,0:T(8,128)(2,1)S(1)} %bitcast.405, bf16[2,192,768]{2,1,0:T(8,128)(2,1)S(1)} %copy-done.24), kind=kOutput, calls=%fused_computation.107 | convolution fusion | flops 88276992 | bytes 2392064 | tf_op jit(solution)/shard_map/jvp()/dot_general | solution.py:93
  24.9 1.3 convolution_bitcast_fusion
  31.9 4.6 %collective-permute-start.3 = (bf16[2,8,768]{2,1,0:T(8,128)(2,1)S(1)}, bf16[2,8,768]{2,1,0:T(8,128)(2,1)S(1)}, u32[]{:S(2)}, u32[]{:S(2)}) collective-permute-start(bf16[2,8,768]{2,1,0:T(8,128)(2,1)S(1)} %convert_element_type.349), channel_id=1, source_target_pairs={{1,0},{2,1},{3,2},{4,3},{5,4},{6,5},{7,6},{0,7},{9,8},{10,9},{11,1... | collective-permute-start | bytes 73736 | tf_op jit(solution)/shard_map/ppermute | solution.py:15
  44.7 1.2 convolution_convert_fusion.12
  46.0 1.3 fusion.145
  47.7 2.2 fusion.44
  50.3 1.1 fusion.18
  51.7 1.1 fusion.14
  53.4 1.1 fusion.76
  55.0 1.3 fusion.31
  56.3 1.3 multiply_reduce_fusion.1
  57.9 1.3 fusion.29
  59.2 1.2 fusion.24
  61.4 1.2 fusion.35
  64.2 1.1 fusion.28
  65.6 1.8 collective-permute-done.4
  67.7 1.3 collective-permute-start.5
  70.1 4.7 %collective-permute-done.5 = bf16[2,8,768]{2,1,0:T(8,128)(2,1)S(1)} collective-permute-done((bf16[2,8,768]{2,1,0:T(8,128)(2,1)S(1)}, bf16[2,8,768]{2,1,0:T(8,128)(2,1)S(1)}, u32[]{:S(2)}, u32[]{:S(2)}) %collective-permute-start.5) | collective-permute-done | bytes 24608 | tf_op jit(solution)/shard_map/ppermute | solution.py:15
  75.0 1.9 multiply_add_fusion
  77.2 1.1 fusion.12
  78.3 1.1 fusion.16
  82.2 1.3 fusion.30
  87.5 1.8 fusion.42
  90.4 1.8 fusion.41
  92.2 37.3 %all-reduce.6 = (f32[1,6,225]{2,1,0:T(8,128)S(1)}, f32[1,6,225]{2,1,0:T(8,128)S(1)}) all-reduce(f32[1,6,225]{2,1,0:T(8,128)S(1)} %fusion.42, f32[1,6,225]{2,1,0:T(8,128)S(1)} %fusion.41), channel_id=1, replica_groups=mesh['row'=4,'col'=8] {'row','col'}, use_global_device_ids=true, to_apply=%region_33.34 | all-reduce | flops 2700 | bytes 21600 | tf_op jit(solution)/shard_map/psum | solution.py:173
  131.2 97.1 %all-reduce.10.cloned.1.call-done = (f32[1,192,576]{2,1,0:T(8,128)}, f32[1,192,576]{2,1,0:T(8,128)}, f32[1,192,192]{2,1,0:T(8,128)}, f32[1,192,192]{2,1,0:T(8,12...) async-done(((f32[1,192,576]{2,1,0:T(8,128)}, f32[1,192,576]{2,1,0:T(8,128)}, f32[1,192,192]{2,1,0:T(8,128)}, ...) | async-done | bytes 3538960 | tf_op jit(solution)/shard_map/psum | solution.py:173
  228.3 2.3 maximum_multiply_fusion.2
  231.4 1.1 maximum_multiply_fusion
  233.1 1.1 maximum_multiply_fusion.1
  (310 shorter events, 40.9 us)
Async XLA Ops:
  7.2 7.6 %copy-start.3 = (bf16[2,8,16,192]{3,2,1,0:T(8,128)(2,1)S(1)}, bf16[2,8,16,192]{3,2,1,0:T(8,128)(2,1)}, u32[]{:S(2)}) copy-start(bf16[2,8,16,192]{3,2,1,0:T(8,128)(2,1)} %param.7) | copy-start | bytes 294916
  7.2 221.1 %all-reduce.10.cloned.1.call-start = ((), (), s32[]{:S(2)}) async-start(), calls=%async_computation | async-start | bytes 7471104 | tf_op jit(solution)/shard_map/psum | solution.py:173
  8.3 28.2 %collective-permute-start = (bf16[2,4,3072]{2,1,0:T(4,128)(2,1)S(1)}, bf16[2,4,3072]{2,1,0:T(4,128)(2,1)S(1)}, u32[]{:S(2)}, u32[]{:S(2)}) collective-permute-start(bf16[2,4,3072]{2,1,0:T(4,128)(2,1)S(1)} %reshape.668), channel_id=1, source_target_pairs={{8,0},{16,8},{24,16},{0,24},{9,1},{17,9},{25,17},{1,25},{10,2},{18... | collective-permute-start | bytes 147464 | tf_op jit(solution)/shard_map/ppermute | solution.py:15
  14.8 10.1 %copy-start.59 = (s32[4096]{0:T(1024)}, s32[4096]{0:T(1024)S(1)}, u32[]{:S(2)}) copy-start(s32[4096]{0:T(1024)S(1)} %add.254) | copy-start | bytes 49156
  18.1 8.1 %copy-start.36 = (f32[4,6,64]{2,1,0:T(8,128)}, f32[4,6,64]{2,1,0:T(8,128)S(1)}, u32[]{:S(2)}) copy-start(f32[4,6,64]{2,1,0:T(8,128)S(1)} %fusion.55) | copy-start | bytes 18436
  18.4 4.3 %copy-start = (bf16[4,6,64,64]{2,3,1,0:T(8,128)(2,1)}, bf16[4,6,64,64]{2,3,1,0:T(8,128)(2,1)S(1)}, u32[]{:S(2)}) copy-start(bf16[4,6,64,64]{2,3,1,0:T(8,128)(2,1)S(1)} %divide_convert_fusion.1) | copy-start | bytes 589828
  19.4 3.2 %copy-start.49 = (f32[4,64]{1,0:T(4,128)}, f32[4,64]{1,0:T(4,128)S(1)}, u32[]{:S(2)}) copy-start(f32[4,64]{1,0:T(4,128)S(1)} %broadcast_multiply_fusion.1) | copy-start | bytes 3076
  19.6 3.1 %copy-start.57 = (f32[4,64]{1,0:T(4,128)}, f32[4,64]{1,0:T(4,128)S(1)}, u32[]{:S(2)}) copy-start(f32[4,64]{1,0:T(4,128)S(1)} %multiply_reduce_fusion.6) | copy-start | bytes 3076
  19.6 3.0 %copy-start.54 = (f32[4,64]{1,0:T(4,128)}, f32[4,64]{1,0:T(4,128)S(1)}, u32[]{:S(2)}) copy-start(f32[4,64]{1,0:T(4,128)S(1)} %fusion.121) | copy-start | bytes 3076
  19.8 2.9 %copy-start.31 = (bf16[4,64,192]{2,1,0:T(8,128)(2,1)}, bf16[4,64,192]{2,1,0:T(8,128)(2,1)S(1)}, u32[]{:S(2)}) copy-start(bf16[4,64,192]{2,1,0:T(8,128)(2,1)S(1)} %multiply_convert_fusion.5) | copy-start | bytes 294916
  19.8 3.6 %copy-start.46 = (bf16[2,768,192]{1,2,0:T(8,128)(2,1)S(1)}, bf16[2,768,192]{1,2,0:T(8,128)(2,1)}, u32[]{:S(2)}) copy-start(bf16[2,768,192]{1,2,0:T(8,128)(2,1)} %param.12) | copy-start | bytes 1769476
  23.9 7.7 %collective-permute-start.2 = (bf16[2,4,3072]{2,1,0:T(4,128)(2,1)S(1)}, bf16[2,4,3072]{2,1,0:T(4,128)(2,1)S(1)}, u32[]{:S(2)}, u32[]{:S(2)}) collective-permute-start(bf16[2,4,3072]{2,1,0:T(4,128)(2,1)S(1)} %convert_element_type.348), channel_id=1, source_target_pairs={{8,0},{16,8},{24,16},{0,24},{9,1},{17,9},{25,17},{1,25},{10,2},{18... | collective-permute-start | bytes 147464 | tf_op jit(solution)/shard_map/ppermute | solution.py:15
  31.9 6.1 %collective-permute-start.3 = (bf16[2,8,768]{2,1,0:T(8,128)(2,1)S(1)}, bf16[2,8,768]{2,1,0:T(8,128)(2,1)S(1)}, u32[]{:S(2)}, u32[]{:S(2)}) collective-permute-start(bf16[2,8,768]{2,1,0:T(8,128)(2,1)S(1)} %convert_element_type.349), channel_id=1, source_target_pairs={{1,0},{2,1},{3,2},{4,3},{5,4},{6,5},{7,6},{0,7},{9,8},{10,9},{11,1... | collective-permute-start | bytes 73736 | tf_op jit(solution)/shard_map/ppermute | solution.py:15
  36.8 7.0 %collective-permute-start.1 = (bf16[2,8,768]{2,1,0:T(8,128)(2,1)S(1)}, bf16[2,8,768]{2,1,0:T(8,128)(2,1)}, u32[]{:S(2)}, u32[]{:S(2)}) collective-permute-start(bf16[2,8,768]{2,1,0:T(8,128)(2,1)S(1)} %reshape.670), channel_id=1, source_target_pairs={{1,0},{2,1},{3,2},{4,3},{5,4},{6,5},{7,6},{0,7},{9,8},{10,9},{11,1... | collective-permute-start | bytes 73736 | tf_op jit(solution)/shard_map/ppermute | solution.py:15
  39.7 3.4 %copy-start.33 = (f32[4,6,64]{2,1,0:T(8,128)}, f32[4,6,64]{2,1,0:T(8,128)S(1)}, u32[]{:S(2)}) copy-start(f32[4,6,64]{2,1,0:T(8,128)S(1)} %get-tuple-element.93) | copy-start | bytes 18436
  40.3 2.8 %copy-start.38 = (f32[4,6,64]{2,1,0:T(8,128)}, f32[4,6,64]{2,1,0:T(8,128)S(1)}, u32[]{:S(2)}) copy-start(f32[4,6,64]{2,1,0:T(8,128)S(1)} %fusion.56) | copy-start | bytes 18436
  40.4 5.5 %copy-start.2 = (bf16[4,6,64,64]{2,3,1,0:T(8,128)(2,1)}, bf16[4,6,64,64]{2,3,1,0:T(8,128)(2,1)S(1)}, u32[]{:S(2)}) copy-start(bf16[4,6,64,64]{2,3,1,0:T(8,128)(2,1)S(1)} %divide_convert_fusion) | copy-start | bytes 589828
  44.7 5.6 %copy-start.19 = (bf16[2,1,8,2,8,192]{5,4,2,3,0,1:T(8,128)(2,1)}, bf16[2,1,8,2,8,192]{5,4,2,3,0,1:T(8,128)(2,1)S(1)}, u32[]{:S(2)}) copy-start(bf16[2,1,8,2,8,192]{5,4,2,3,0,1:T(8,128)(2,1)S(1)} %copy.298) | copy-start | bytes 294916
  44.7 2.9 %copy-start.25 = (bf16[2,192,768]{2,1,0:T(8,128)(2,1)S(1)}, bf16[2,192,768]{2,1,0:T(8,128)(2,1)}, u32[]{:S(2)}) copy-start(bf16[2,192,768]{2,1,0:T(8,128)(2,1)} %param.11) | copy-start | bytes 1769476
  46.0 3.9 %copy-start.11 = (bf16[4,6,32,64]{3,2,1,0:T(8,128)(2,1)}, bf16[4,6,32,64]{3,2,1,0:T(8,128)(2,1)S(1)}, u32[]{:S(2)}) copy-start(bf16[4,6,32,64]{3,2,1,0:T(8,128)(2,1)S(1)} %convolution_convert_fusion.12) | copy-start | bytes 294916
  47.3 5.9 %copy-start.51 = (f32[4,64]{1,0:T(4,128)}, f32[4,64]{1,0:T(4,128)S(1)}, u32[]{:S(2)}) copy-start(f32[4,64]{1,0:T(4,128)S(1)} %broadcast_multiply_fusion) | copy-start | bytes 3076
  47.5 5.7 %copy-start.56 = (f32[4,64]{1,0:T(4,128)}, f32[4,64]{1,0:T(4,128)S(1)}, u32[]{:S(2)}) copy-start(f32[4,64]{1,0:T(4,128)S(1)} %fusion.122) | copy-start | bytes 3076
  63.9 3.6 %collective-permute-start.4 = (bf16[2,4,3072]{2,1,0:T(4,128)(2,1)S(1)}, bf16[2,4,3072]{2,1,0:T(4,128)(2,1)S(1)}, u32[]{:S(2)}, u32[]{:S(2)}) collective-permute-start(bf16[2,4,3072]{2,1,0:T(4,128)(2,1)S(1)} %convert_element_type.382), channel_id=1, source_target_pairs={{24,0},{0,8},{8,16},{16,24},{25,1},{1,9},{9,17},{17,25},{26,2},{2,... | collective-permute-start | bytes 147464 | tf_op jit(solution)/shard_map/ppermute | solution.py:15
  67.7 7.3 %copy-start.48 = (bf16[2,768,192]{1,2,0:T(8,128)(2,1)S(1)}, bf16[2,768,192]{1,2,0:T(8,128)(2,1)}, u32[]{:S(2)}) copy-start(bf16[2,768,192]{1,2,0:T(8,128)(2,1)} %param.12) | copy-start | bytes 1769476
  67.7 7.1 %collective-permute-start.5 = (bf16[2,8,768]{2,1,0:T(8,128)(2,1)S(1)}, bf16[2,8,768]{2,1,0:T(8,128)(2,1)S(1)}, u32[]{:S(2)}, u32[]{:S(2)}) collective-permute-start(bf16[2,8,768]{2,1,0:T(8,128)(2,1)S(1)} %convert_element_type.383), channel_id=1, source_target_pairs={{7,0},{0,1},{1,2},{2,3},{3,4},{4,5},{5,6},{6,7},{15,8},{8,9},{9,10... | collective-permute-start | bytes 73736 | tf_op jit(solution)/shard_map/ppermute | solution.py:15
  89.7 40.3 %copy-start.67 = (f32[256]{0:T(256)S(1)}, f32[256]{0:T(256)}, u32[]{:S(2)}) copy-start(f32[256]{0:T(256)} %add.281) | copy-start | bytes 3076
  89.7 40.3 %copy-start.23 = (f32[256,192]{0,1:T(8,128)S(1)}, f32[256,192]{0,1:T(8,128)}, u32[]{:S(2)}) copy-start(f32[256,192]{0,1:T(8,128)} %copy.349) | copy-start | bytes 589828
  89.7 40.3 %copy-start.65 = (f32[256]{0:T(256)S(1)}, f32[256]{0:T(256)}, u32[]{:S(2)}) copy-start(f32[256]{0:T(256)} %div.189) | copy-start | bytes 3076
  89.9 40.3 %copy-start.63 = (f32[4,64]{1,0:T(4,128)S(1)}, f32[4,64]{1,0:T(4,128)}, u32[]{:S(2)}) copy-start(f32[4,64]{1,0:T(4,128)} %add.280) | copy-start | bytes 3076
  90.0 40.3 %copy-start.61 = (f32[4,64]{1,0:T(4,128)S(1)}, f32[4,64]{1,0:T(4,128)}, u32[]{:S(2)}) copy-start(f32[4,64]{1,0:T(4,128)} %div.186) | copy-start | bytes 3076
  228.3 3.1 %copy-start.29 = (f32[1,192,768]{2,1,0:T(8,128)S(1)}, f32[1,192,768]{2,1,0:T(8,128)}, u32[]{:S(2)}) copy-start(f32[1,192,768]{2,1,0:T(8,128)} %get-tuple-element.54) | copy-start | bytes 1769476
  228.3 3.1 %copy-start.30 = (f32[1,192,768]{2,1,0:T(8,128)S(1)}, f32[1,192,768]{2,1,0:T(8,128)}, u32[]{:S(2)}) copy-start(f32[1,192,768]{2,1,0:T(8,128)} %get-tuple-element.55) | copy-start | bytes 1769476
  (44 other events, 66.0 us)
Sparse Core Ops, SparseCore 0:
  86.9 141.3 all-reduce.9
where the time goes:
time: 242 us; the launch traced here: 241 us
  waiting for transfers between devices  104 us (43%)
  blocking collectives  37.3 us (15%)
  matrix products  36.2 us (15%)
  local copies, waits for them, and re-layouts  21.9 us (9%)
  other arithmetic  16.1 us (7%)
  between operations  15.6 us (6%)
  starting transfers between devices  9.9 us (4%)
    psum x1, waiting for transfers between devices, local(): lax.psum((plain_grads[0], plain_grads[1], plain_grads[2], plain_grads[3],...  97.1 us
    psum x1, blocking collectives, local(): lax.psum((plain_grads[0], plain_grads[1], plain_grads[2], plain_grads[3],...  37.3 us
    ppermute x6, starting transfers between devices, from_behind(): return lax.ppermute(block, axis, route)  9.87 us
    dot_general x6, matrix products, block_tile(): jnp.dot(normed_two, expand_w, preferred_element_type=jnp.float32)  7.79 us
    ppermute x6, waiting for transfers between devices, from_behind(): return lax.ppermute(block, axis, route)  7.04 us
    dot_general x4, matrix products, block_tile(): jnp.dot(table, offset_onehot(), precision=lax.Precision.HIGHEST)  6.18 us
    unnamed x139, local copies, waits for them, and re-layouts  5.4 us
    mul x5, other arithmetic, local(): jnp.stack([plain_grads[member], shift_grads[member]]) * factor  5.36 us
  transfers between devices with their start and end apart: 7, of which 4 were waited for; matrix products, arithmetic and copies ran while one was open for 13% of the time, Pallas kernels for 0%

commit v1 on v0

v1 whole, which is shorter than its diff:
```python
import functools
import math

import jax
import jax.numpy as jnp
from jax import lax
from jax.experimental import pallas as pl
from jax.experimental.pallas import tpu as pltpu
from jax.sharding import PartitionSpec as P

WIN = 8
SHIFT = 4
BF = jnp.bfloat16
F32 = jnp.float32
LIMIT = 48 * 1024 * 1024
ROOT_HALF = 0.7071067811865476
DENSITY = 0.3989422804014327


def dot(a, b):
    return lax.dot_general(a, b, (((1,), (0,)), ((), ())), preferred_element_type=F32)


def dot_nt(a, b):
    return lax.dot_general(a, b, (((1,), (1,)), ((), ())), preferred_element_type=F32)


def dot_tn(a, b):
    return lax.dot_general(a, b, (((0,), (0,)), ((), ())), preferred_element_type=F32)


def iota(shape, axis):
    return lax.broadcasted_iota(jnp.int32, shape, axis)


def norm(field):
    center = field - jnp.mean(field, axis=0, keepdims=True)
    spread = jnp.mean(center * center, axis=0, keepdims=True)
    scale = lax.rsqrt(spread + 1e-05)
    return center * scale, scale


def norm_back(grad, normed, scale):
    along = jnp.mean(grad * normed, axis=0, keepdims=True)
    return scale * (grad - jnp.mean(grad, axis=0, keepdims=True) - normed * along)


def first_half(shape):
    return iota(shape, 1) < 64


def head_masks(heads, head):
    tall = (heads * 64, heads * head)
    wide = (heads * head, heads * 64)
    over = (iota(tall, 0) // 64 == iota(tall, 1) // head).astype(F32).astype(BF)
    across = (iota(wide, 0) // head == iota(wide, 1) // 64).astype(F32).astype(BF)
    return over, across


def spread_bias(table, heads):
    entries = table.shape[1]
    side = 2 * WIN - 1
    lanes = iota((entries, 256), 1)
    rows = iota((entries, 256), 0)
    place = lanes % 128
    down = place // 8 - 8
    right = place % 8 - jnp.where(lanes >= 128, 8, 0)
    wanted = (down + WIN - 1) * side + right + WIN - 1
    fits = (down >= 1 - WIN) & (right >= 1 - WIN)
    pick = (fits & (wanted == rows)).astype(F32)
    vectors = lax.dot_general(
        table, pick, (((1,), (0,)), ((), ())), precision=lax.Precision.HIGHEST, preferred_element_type=F32
    )
    ahead = jnp.broadcast_to(vectors[:, None, :128], (heads, 8, 128)).reshape(heads * 8, 128)
    behind = jnp.broadcast_to(vectors[:, None, 128:], (heads, 8, 128)).reshape(heads * 8, 128)
    shape = (heads * 8, 128)
    col_j = iota(shape, 0) % 8
    col_i = iota(shape, 1) % 8
    built = jnp.zeros(shape, F32)
    for c in range(8):
        line = jnp.where(col_i >= c, pltpu.roll(ahead, 64 + c, 1), pltpu.roll(behind, 56 + c, 1))
        built = jnp.where(col_j == c, line, built)
    rolled = [built] + [pltpu.roll(built, 8 * r, 1) for r in range(1, 8)]
    rolled = [jnp.where(first_half(shape), one, pltpu.roll(one, 64, 1)) for one in rolled]
    parts = []
    for h in range(heads):
        for r in range(8):
            parts.append(rolled[r][8 * h : 8 * h + 8])
    return jnp.concatenate(parts, axis=0)


def fold_bias(grad, heads):
    folded = jnp.where(first_half(grad.shape), grad + pltpu.roll(grad, 64, 1), 0.0)
    split = folded.reshape(heads, 8, 8, 128)
    total = jnp.zeros((heads * 8, 128), F32)
    for r in range(8):
        piece = split[:, r].reshape(heads * 8, 128)
        total = total + pltpu.roll(piece, 64 - 8 * r, 1)
    shape = (heads * 8, 128)
    col_j = iota(shape, 0) % 8
    col_i = iota(shape, 1) % 8
    ahead = jnp.zeros(shape, F32)
    behind = jnp.zeros(shape, F32)
    for c in range(8):
        mine = jnp.where((col_j == c) & (col_i >= c), total, 0.0)
        ahead = ahead + (pltpu.roll(mine, 128 - c, 1) if c else mine)
        rest = jnp.where((col_j == c) & (col_i < c), total, 0.0)
        behind = behind + pltpu.roll(rest, 8 - c, 1)
    ahead = jnp.sum(ahead.reshape(heads, 8, 128), axis=1)
    behind = jnp.sum(behind.reshape(heads, 8, 128), axis=1)
    return ahead, behind


def shift_mask(shape, last_row, last_col):
    j = iota(shape, 0) % 64
    lane = iota(shape, 1)
    i = lane % 64
    low = (j // 8 >= SHIFT) != (i // 8 >= SHIFT)
    side = (j % 8 >= SHIFT) != (i % 8 >= SHIFT)
    differ = (low & last_row) | (side & (lane >= 64) & last_col)
    return jnp.where(differ, -10000.0, 0.0)


def heads_of(weights, field, bias, heads):
    width, tokens = field.shape
    head = width // heads
    qkv_w, proj_w = weights[0][...], weights[1][...]
    over, across = head_masks(heads, head)
    normed, scale = norm(field)
    normed = normed.astype(BF)
    mixed = dot_tn(qkv_w, normed)
    query = (mixed[:width] * head ** (-0.5)).astype(BF)
    natural = mixed[width:].T.astype(BF)
    parts, probs, attended = [], [], []
    half = first_half((width, 128))
    for p in range(tokens // 128):
        lanes = slice(128 * p, 128 * p + 128)
        keys, values = mixed[width : 2 * width, lanes], mixed[2 * width :, lanes]
        pieces = []
        for field_t in (keys, values):
            swapped = pltpu.roll(field_t, 64, 1)
            pieces.append(
                [
                    jnp.concatenate([one.astype(BF)] * (heads // 2), axis=1) * across
                    for one in (jnp.where(half, field_t, swapped), jnp.where(half, swapped, field_t))
                ]
            )
        talls = []
        for which in range(2):
            talls.append(
                [
                    jnp.concatenate(
                        [natural[128 * p + 64 * w : 128 * p + 64 * w + 64, which * width : which * width + width]]
                        * heads,
                        axis=0,
                    )
                    * over
                    for w in range(2)
                ]
            )
        q = query[:, lanes]
        scores = jnp.where(first_half((heads * 64, 128)), dot(talls[0][0], q), dot(talls[0][1], q)) + bias
        scores = scores.reshape(heads, 64, 128)
        expos = jnp.exp(scores - jnp.max(scores, axis=1, keepdims=True))
        prob = (expos / jnp.sum(expos, axis=1, keepdims=True)).reshape(heads * 64, 128)
        prob_b = prob.astype(BF)
        attended.append(jnp.where(half, dot(pieces[1][0], prob_b), dot(pieces[1][1], prob_b)))
        probs.append(prob)
        parts.append((q, pieces[0], talls[1]))
    attended = jnp.concatenate(attended, axis=1).astype(BF)
    resid = field + dot_tn(proj_w, attended)
    return normed, scale, parts, probs, attended, resid


def forward(weights, field, bias, heads):
    expand_w, reduce_w = weights[2][...], weights[3][...]
    normed, scale, parts, probs, attended, resid = heads_of(weights, field, bias, heads)
    normed_two, scale_two = norm(resid)
    normed_two = normed_two.astype(BF)
    pre = dot_tn(expand_w, normed_two)
    bell = 0.5 * (1.0 + lax.erf(pre * ROOT_HALF))
    hidden = (pre * bell).astype(BF)
    result = resid + dot_tn(reduce_w, hidden)
    saved = (normed, scale, parts, probs, attended, resid, normed_two, scale_two, pre, bell, hidden)
    return result, saved


def backward(weights, field, saved, grad, heads):
    qkv_w, proj_w, expand_w, reduce_w = (w[...] for w in weights)
    normed, scale, parts, probs, attended, resid, normed_two, scale_two, pre, bell, hidden = saved
    width, tokens = field.shape
    head = width // heads
    over, across = head_masks(heads, head)
    grad_b = grad.astype(BF)
    grad_hidden = dot(reduce_w, grad_b).astype(BF).astype(F32)
    slope = bell + pre * (DENSITY * jnp.exp(-0.5 * pre * pre))
    grad_pre = (grad_hidden * slope).astype(BF)
    grad_two = dot(expand_w, grad_pre).astype(BF).astype(F32)
    center_two = resid - jnp.mean(resid, axis=0, keepdims=True)
    grad_resid = grad + norm_back(grad_two, center_two * scale_two, scale_two)
    grad_resid_b = grad_resid.astype(BF)
    grad_att = dot(proj_w, grad_resid_b)
    half = first_half((width, 128))
    tall_half = first_half((heads * 64, 128))
    grad_q, grad_k, grad_v = [], [], []
    grad_bias = jnp.zeros((heads * 64, 128), F32)
    for p in range(tokens // 128):
        query, keys_wide, values_tall = parts[p]
        prob = probs[p]
        prob_b = prob.astype(BF)
        att = grad_att[:, 128 * p : 128 * p + 128]
        att_b = att.astype(BF)
        zero = jnp.zeros_like(att)
        att_w = (jnp.where(half, att, zero).astype(BF), jnp.where(half, zero, att).astype(BF))
        query_f = query.astype(F32)
        query_w = (jnp.where(half, query_f, zero).astype(BF), jnp.where(half, zero, query_f).astype(BF))
        grad_prob = jnp.where(tall_half, dot(values_tall[0], att_b), dot(values_tall[1], att_b))
        grad_prob = grad_prob.astype(BF).astype(F32)
        along = jnp.sum((prob * grad_prob).reshape(heads, 64, 128), axis=1, keepdims=True)
        grad_score = prob * (grad_prob.reshape(heads, 64, 128) - along).reshape(heads * 64, 128)
        grad_bias = grad_bias + grad_score
        score_b = grad_score.astype(BF)
        grad_q.append(jnp.where(half, dot(keys_wide[0], score_b), dot(keys_wide[1], score_b)))
        for store, lhs, rhs in ((grad_k, query_w, score_b), (grad_v, att_w, prob_b)):
            both = []
            for w in range(2):
                full = dot_nt(lhs[w], rhs) * across.astype(F32)
                folded = sum(full[:, 128 * n : 128 * n + 128] for n in range(heads // 2))
                both.append(folded + pltpu.roll(folded, 64, 1))
            store.append(jnp.where(half, both[0], both[1]))
    grad_q = jnp.concatenate(grad_q, axis=1).astype(BF).astype(F32) * head ** (-0.5)
    grad_k = jnp.concatenate(grad_k, axis=1)
    grad_v = jnp.concatenate(grad_v, axis=1)
    grad_mixed = jnp.concatenate([grad_q, grad_k, grad_v], axis=0).astype(BF)
    grad_normed = dot(qkv_w, grad_mixed).astype(BF).astype(F32)
    center = field - jnp.mean(field, axis=0, keepdims=True)
    grad_field = grad_resid + norm_back(grad_normed, center * scale, scale)
    operands = (normed, grad_mixed, attended, grad_resid_b, normed_two, grad_pre, hidden, grad_b)
    return grad_field, operands, grad_bias


def pack_grads(operands, ahead, behind, buffer):
    normed, grad_mixed, attended, grad_resid, normed_two, grad_pre, hidden, grad = operands
    width = normed.shape[0]
    qkv = dot_nt(normed, grad_mixed)
    proj = dot_nt(attended, grad_resid)
    expand = dot_nt(normed_two, grad_pre)
    reduce = dot_nt(hidden, grad)
    inner = hidden.shape[0]
    at = 0

    def put(block):
        nonlocal at
        buffer[at : at + block.shape[0], :] = block.astype(BF)
        at += block.shape[0]

    full = 3 * width // 128
    for n in range(full):
        put(qkv[:, 128 * n : 128 * n + 128])
    put(jnp.concatenate([qkv[:, 128 * full :], proj[:, 128:]], axis=1))
    put(proj[:, :128])
    for n in range(inner // 128):
        put(expand[:, 128 * n : 128 * n + 128])
    put(reduce[:, :128])
    put(jnp.concatenate([reduce[: inner // 2, 128:], reduce[inner // 2 :, 128:]], axis=1))
    heads = ahead.shape[0]
    put(jnp.concatenate([ahead, behind, jnp.zeros((16 - 2 * heads, 128), F32)], axis=0))
    rest = buffer.shape[0] - at
    if rest:
        put(jnp.zeros((rest, 128), F32))


def unpack_grads(buffer, outs, block, factor):
    qkv, proj, expand, reduce, table = outs
    width, inner = qkv.shape[1], expand.shape[2]
    heads, entries = table.shape[1:]
    at = 0

    def take(rows):
        nonlocal at
        piece = buffer[at : at + rows, :].astype(F32) * factor
        at += rows
        return piece

    full = 3 * width // 128
    for n in range(full):
        qkv[block, :, 128 * n : 128 * n + 128] = take(width)
    shared = take(width)
    qkv[block, :, 128 * full :] = shared[:, :64]
    proj[block, :, 128:] = shared[:, 64:]
    proj[block, :, :128] = take(width)
    for n in range(inner // 128):
        expand[block, :, 128 * n : 128 * n + 128] = take(width)
    reduce[block, :, :128] = take(inner)
    shared = take(inner // 2)
    reduce[block, : inner // 2, 128:] = shared[:, :64]
    reduce[block, inner // 2 :, 128:] = shared[:, 64:]
    vectors = buffer[at : at + 16, :]
    side = 2 * WIN - 1
    shape = (128, entries)
    rows, lanes = iota(shape, 0), iota(shape, 1)
    down, right = lanes // side - (WIN - 1), lanes % side - (WIN - 1)
    base = 8 * (down + 8) + right
    ahead = ((right >= 0) & (base == rows)).astype(F32).astype(BF)
    behind = ((right < 0) & (base + 8 == rows)).astype(F32).astype(BF)
    table[block] = (dot(vectors, ahead)[:heads] + dot(vectors, behind)[heads : 2 * heads]) * factor


def tokens_of(read):
    flat = [read(f, c).reshape(64, -1) for f in range(2) for c in range(2)]
    return jnp.concatenate(flat, axis=0).T


def plain_forward(x_ref, qkv, proj, expand, reduce, table, first, top, left, corner, tight):
    heads = table.shape[0]
    field = tokens_of(lambda f, c: x_ref[f, :, 8 * c : 8 * c + 8, :].astype(F32))
    result, _ = forward((qkv, proj, expand, reduce), field, spread_bias(table[...], heads), heads)
    natural = result.T
    for f in range(2):
        for c in range(2):
            n = 64 * (2 * f + c)
            first[f, :, 8 * c : 8 * c + 8, :] = natural[n : n + 64].reshape(8, 8, -1)
    top[...] = first[:, :SHIFT].astype(BF)
    for f in range(2):
        for r in range(4):
            n = 16 * f + 4 * r
            tight[n : n + 4, :] = first[f, r, :4, :]
            tight[32 + n : 36 + n, :] = first[f, 4 + r, :4, :]
    corner[...] = tight[:32].astype(BF)
    left[...] = tight[32:].astype(BF)


def shifted_block(
    n_row, n_col, first, below, beside, across, cot, cot_below, cot_beside, cot_across, qkv, proj, expand, reduce, table,
    own, bottom, right, corner, normed, grad_mixed, attended, grad_resid, normed_two, grad_pre, hidden, grad, lines,
    moved, turned, tight,
):
    heads = table.shape[0]
    moved[:, :4, :16, :] = first[:, 4:, :, :]
    moved[:, 4:, :16, :] = below[...].astype(F32)
    turned[:, :4, :16, :] = cot[:, 4:, :, :].astype(F32)
    turned[:, 4:, :16, :] = cot_below[:, :4, :, :].astype(F32)
    turned[:, :4, 16:, :] = cot_beside[:, 4:, :8, :].astype(F32)
    turned[:, 4:, 16:, :] = cot_across[:, :4, :8, :].astype(F32)
    tight[:32] = across[...].astype(F32)
    tight[32:] = beside[...].astype(F32)
    for f in range(2):
        for r in range(4):
            n = 16 * f + 4 * r
            moved[f, 4 + r, 16:20, :] = tight[n : n + 4, :]
            moved[f, r, 16:20, :] = tight[32 + n : 36 + n, :]
    field = tokens_of(lambda f, c: moved[f, :, 4 + 8 * c : 12 + 8 * c, :])
    cotangent = tokens_of(lambda f, c: turned[f, :, 4 + 8 * c : 12 + 8 * c, :])
    last_row = lax.axis_index("row") == n_row - 1
    last_col = lax.axis_index("col") == n_col - 1
    bias = spread_bias(table[...], heads)
    bias = bias + shift_mask(bias.shape, last_row, last_col)
    weights = (qkv, proj, expand, reduce)
    _, saved = forward(weights, field, bias, heads)
    grad_field, operands, grad_bias = backward(weights, field, saved, cotangent, heads)
    natural = grad_field.T
    for f in range(2):
        for c in range(2):
            n = 64 * (2 * f + c)
            moved[f, :, 4 + 8 * c : 12 + 8 * c, :] = natural[n : n + 64].reshape(8, 8, -1)
    own[...] = moved[:, :4, :16, :]
    bottom[...] = moved[:, 4:, :16, :].astype(BF)
    for f in range(2):
        for r in range(4):
            n = 16 * f + 4 * r
            tight[n : n + 4, :] = moved[f, 4 + r, 16:20, :]
            tight[32 + n : 36 + n, :] = moved[f, r, 16:20, :]
    corner[...] = tight[:32].astype(BF)
    right[...] = tight[32:].astype(BF)
    for ref, value in zip(
        (normed, grad_mixed, attended, grad_resid, normed_two, grad_pre, hidden, grad), operands, strict=True
    ):
        ref[...] = value
    lines[...] = grad_bias


def split_core(buffer, keep, send):
    rows = keep.shape[0]
    core = lax.axis_index("row") % 2
    keep[...] = buffer[pl.ds(pl.multiple_of(core * rows, 16), rows), :]
    send[...] = buffer[pl.ds(pl.multiple_of((1 - core) * rows, 16), rows), :]


def shifted_grads(heads, normed, grad_mixed, attended, grad_resid, normed_two, grad_pre, hidden, grad, lines, keep, send, buffer):
    operands = tuple(
        ref[...] for ref in (normed, grad_mixed, attended, grad_resid, normed_two, grad_pre, hidden, grad)
    )
    ahead, behind = fold_bias(lines[...], heads)
    pack_grads(operands, ahead, behind, buffer)
    split_core(buffer, keep, send)


def plain_backward(
    x_ref, own, above, beside, across, qkv, proj, expand, reduce, table, out, keep, send, middle, tight, buffer
):
    heads = table.shape[0]
    field = tokens_of(lambda f, c: x_ref[f, :, 8 * c : 8 * c + 8, :].astype(F32))
    middle[:, 4:] = own[...]
    middle[:, :4] = above[...].astype(F32)
    tight[:32] = across[...].astype(F32)
    tight[32:] = beside[...].astype(F32)
    for f in range(2):
        for r in range(4):
            n = 16 * f + 4 * r
            middle[f, r, :4, :] = tight[n : n + 4, :]
            middle[f, 4 + r, :4, :] = tight[32 + n : 36 + n, :]
    cotangent = tokens_of(lambda f, c: middle[f, :, 8 * c : 8 * c + 8, :])
    weights = (qkv, proj, expand, reduce)
    _, saved = forward(weights, field, spread_bias(table[...], heads), heads)
    grad_field, operands, grad_bias = backward(weights, field, saved, cotangent, heads)
    natural = grad_field.T
    for f in range(2):
        for c in range(2):
            n = 64 * (2 * f + c)
            out[f, :, 8 * c : 8 * c + 8, :] = natural[n : n + 64].reshape(8, 8, -1)
    ahead, behind = fold_bias(grad_bias, heads)
    pack_grads(operands, ahead, behind, buffer)
    split_core(buffer, keep, send)


def near_place():
    return lax.axis_index("row") // 2 * 2 + lax.axis_index("col") % 2


def add_core(keep, came, own, *rest):
    sends, total = rest[:-1], rest[-1]
    total[...] = keep[...].astype(F32) + came[...].astype(F32)
    rows = own.shape[0]
    me = near_place()
    own[...] = total[pl.ds(pl.multiple_of(me * rows, 16), rows), :]
    for d, send in enumerate(sends):
        send[...] = total[pl.ds(pl.multiple_of((me ^ (d + 1)) * rows, 16), rows), :].astype(BF)


def add_near(count, *refs):
    ins, own, sends, total = refs[:4], refs[4], refs[5 : 4 + count], refs[-1]
    total[...] = ins[0][...] + sum(one[...].astype(F32) for one in ins[1:])
    rows = own.shape[0]
    me = lax.axis_index("col") // 2
    own[...] = total[pl.ds(pl.multiple_of(me * rows, 16), rows), :]
    for d, send in enumerate(sends):
        send[...] = total[pl.ds(pl.multiple_of((me ^ (d + 1)) * rows, 16), rows), :].astype(BF)


def add_far(*refs):
    ins, out = refs[:-1], refs[-1]
    out[...] = (ins[0][...] + sum(one[...].astype(F32) for one in ins[1:])).astype(BF)


def join_far(*refs):
    ins, out = refs[:-1], refs[-1]
    rows = ins[0].shape[0]
    me = lax.axis_index("col") // 2
    for d, piece in enumerate(ins):
        out[pl.ds(pl.multiple_of((me ^ d) * rows, 16), rows), :] = piece[...]


def finish(factor, *refs):
    ins, outs, buffer = refs[:16], refs[16:21], refs[21]
    rows = ins[0].shape[0]
    me = near_place()
    core = lax.axis_index("row") % 2
    for block in range(2):
        for n in range(8):
            where = (core ^ (n // 4)) * 4 + (me ^ (n % 4))
            buffer[pl.ds(pl.multiple_of(where * rows, 16), rows), :] = ins[8 * block + n][...]
        unpack_grads(buffer, outs, block, factor)


def call(kernel, outs, scratch, args, block=None, weights=0):
    specs = []
    for n, arg in enumerate(args):
        if n >= len(args) - weights:
            specs.append(pl.BlockSpec((None,) + arg.shape[1:], lambda _, k=arg.ndim: (block,) + (0,) * (k - 1)))
        else:
            specs.append(pl.BlockSpec(arg.shape, lambda _, k=arg.ndim: (0,) * k))
    return pl.pallas_call(
        kernel,
        grid=(1,),
        in_specs=specs,
        out_specs=[pl.BlockSpec(s, lambda _, k=len(s): (0,) * k) for s, _ in outs],
        out_shape=[jax.ShapeDtypeStruct(s, d) for s, d in outs],
        scratch_shapes=[pltpu.VMEM(s, d) for s, d in scratch],
        compiler_params=pltpu.CompilerParams(vmem_limit_bytes=LIMIT),
    )(*args)


def local(block_input, cotangent, qkv_weight, proj_weight, expand_weight, reduce_weight, bias_table):
    frames, rows, cols, width = block_input.shape
    n_row, n_col = lax.axis_size("row"), lax.axis_size("col")
    inner = expand_weight.shape[2]
    heads = bias_table.shape[1]
    tokens = frames * rows * cols
    weights = (qkv_weight, proj_weight, expand_weight, reduce_weight, bias_table)
    axes = ("row", "col")

    def send(block, down, right):
        route = [
            (r * n_col + c, (r + down) % n_row * n_col + (c + right) % n_col)
            for r in range(n_row)
            for c in range(n_col)
        ]
        return lax.ppermute(block, axes, route)

    def swap(block, row_bits, col_bits):
        route = [
            (r * n_col + c, (r ^ row_bits) * n_col + (c ^ col_bits)) for r in range(n_row) for c in range(n_col)
        ]
        return lax.ppermute(block, axes, route)

    cots = [cotangent, send(cotangent, -1, 0), send(cotangent, 0, -1), send(cotangent, -1, -1)]
    tile = (frames, rows, cols, width)
    strip = (frames, SHIFT, cols, width)
    small = (frames * SHIFT * SHIFT, width)
    tight = ((2 * small[0], width), F32)
    first, top, left, corner = call(
        plain_forward, [(tile, F32), (strip, BF), (small, BF), (small, BF)], [tight], [block_input, *weights], 0, 5
    )
    halo = [first, send(top, -1, 0), send(left, 0, -1), send(corner, -1, -1)]
    kinds = [(n, tokens) for n in (width, 3 * width, width, width, width, inner, inner, width)]
    outs = call(
        functools.partial(shifted_block, n_row, n_col),
        [(strip, F32), (strip, BF), (small, BF), (small, BF)]
        + [(kind, BF) for kind in kinds]
        + [((heads * 64, 128), F32)],
        [((frames, rows, cols + 8, width), F32)] * 2 + [tight],
        [*halo, *cots, *weights],
        1,
        5,
    )
    back = [outs[0], send(outs[1], 1, 0), send(outs[2], 0, 1), send(outs[3], 1, 1)]

    far = n_col // 2
    unit = 8 * far * 16
    used = (3 * width + width + inner) * width // 128 + inner * width // 128 + 16
    size = -(-used // unit) * unit
    chunk = size // (8 * far)
    halves = [((size // 2, 128), BF)] * 2
    buffer = ((size, 128), BF)

    def reduce_all(keep, came_from):
        came = swap(came_from, 1, 0)
        quarter = (size // 8, 128)
        own, *sends = call(add_core, [(quarter, F32)] + [(quarter, BF)] * 3, [((size // 2, 128), F32)], [keep, came])
        near = [own] + [swap(one, (d & 2), d & 1) for d, one in enumerate(sends, 1)]
        own, *sends = call(
            functools.partial(add_near, far),
            [((chunk, 128), F32)] + [((chunk, 128), BF)] * (far - 1),
            [(quarter, F32)],
            near,
        )
        distant = [own] + [swap(one, 0, 2 * d) for d, one in enumerate(sends, 1)]
        (done,) = call(add_far, [((chunk, 128), BF)], [], distant)
        distant = [done] + [swap(done, 0, 2 * d) for d in range(1, far)]
        (joined,) = call(join_far, [(quarter, BF)], [], distant)
        near = [joined] + [swap(joined, (d & 2), d & 1) for d in range(1, 4)]
        return near + [swap(one, 1, 0) for one in near]

    keep, away = call(functools.partial(shifted_grads, heads), halves, [buffer], list(outs[4:]))
    shifted = reduce_all(keep, away)
    input_grad, keep, away = call(
        plain_backward,
        [(tile, F32), *halves],
        [(tile, F32), tight, buffer],
        [block_input, *back, *weights],
        0,
        5,
    )
    plain = reduce_all(keep, away)
    factor = 1.0 / math.sqrt(frames * rows * n_row * cols * n_col)
    grads = call(
        functools.partial(finish, factor), [(w.shape, F32) for w in weights], [buffer], plain + shifted
    )
    return (input_grad, *grads)


def solution(mesh):
    in_specs = (P(None, "row", "col", None), P(None, "row", "col", None), P(), P(), P(), P(), P())
    out_specs = (P(None, "row", "col", None), P(), P(), P(), P(), P())
    return jax.shard_map(local, mesh=mesh, in_specs=in_specs, out_specs=out_specs, check_vma=False)
```

time: 242 us -> 104 us (0.43)
  waiting for transfers between devices: 104 us -> 36.7 us
  blocking collectives: 37.3 us -> 0 us
  matrix products: 36.2 us -> 0 us
  starting transfers between devices: 9.9 us -> 46.1 us
  local copies, waits for them, and re-layouts: 21.9 us -> 5.04 us
  other arithmetic: 16.1 us -> 0 us
  Pallas kernels: 0 us -> 15.1 us
  between operations: 15.6 us -> 0.86 us
    psum x1 -> x0, waiting for transfers between devices: 97.1 us -> none  [local(): lax.psum((plain_grads[0], plain_grads[1], plain_grads[2], plain_grads[3],...]
    psum x1 -> x0, blocking collectives: 37.3 us -> none  [local(): lax.psum((plain_grads[0], plain_grads[1], plain_grads[2], plain_grads[3],...]
    ppermute x6 -> x43, starting transfers between devices: 9.87 us -> 46.1 us  [the longest x34 31.6 us: swap(): return lax.ppermute(block, axes, route)]
    dot_general x39 -> x0, matrix products: 36.2 us -> none  [the longest x6 7.79 us: block_tile(): jnp.dot(normed_two, expand_w, preferred_element_type=jnp.float32)]
    ppermute x6 -> x43, waiting for transfers between devices: 7.04 us -> 36.7 us  [the longest x34 26.6 us: swap(): return lax.ppermute(block, axes, route)]
    pallas_call x0 -> x13, Pallas kernels: none -> 15.1 us  [call(): pl.pallas_call(kernel, grid=(1,), in_specs=specs, out_specs=[pl.BlockSpec...]
    mul x6 -> x0, other arithmetic: 5.36 us -> none  [the longest x5 5.36 us: local(): jnp.stack([plain_grads[member], shift_grads[member]]) * factor]
    reduce_sum x18 -> x0, other arithmetic: 5.09 us -> none  [the longest x6 1.8 us: layer_norm(): center = field - jnp.mean(field, axis=-1, keepdims=True)]
  transfers between devices with their start and end apart: 7 -> 43, of which waited for: 4 -> 17; matrix products, arithmetic and copies ran while one was open for 13% -> 2% of each run, Pallas kernels for 0% -> 8%
where the time goes in v1:
time: 104 us
  starting transfers between devices  46.1 us (44%)
  waiting for transfers between devices  36.7 us (35%)
  Pallas kernels  15.1 us (15%)
  local copies, waits for them, and re-layouts  5.04 us (5%)
    ppermute x34, starting transfers between devices, swap(): return lax.ppermute(block, axes, route)  31.6 us
    ppermute x34, waiting for transfers between devices, swap(): return lax.ppermute(block, axes, route)  26.6 us
    pallas_call x13, Pallas kernels, call(): pl.pallas_call(kernel, grid=(1,), in_specs=specs, out_specs=[pl.BlockSpec...  15.1 us
    ppermute x9, starting transfers between devices, send(): return lax.ppermute(block, axes, route)  14.5 us
    ppermute x9, waiting for transfers between devices, send(): return lax.ppermute(block, axes, route)  10.1 us
    unnamed x16, local copies, waits for them, and re-layouts  5.04 us
  transfers between devices with their start and end apart: 43, of which 17 were waited for; matrix products, arithmetic and copies ran while one was open for 2% of the time, Pallas kernels for 8%

profile of v1, /device:TPU:0, one launch (start us, length us, event | category | flops | bytes accessed | tf_op | source)
XLA Modules:
  0.0 103.8 jit_solution(15294301493644645708)
XLA Ops:
  0.7 6.1 %collective-permute-start.4 = (bf16[2,8,16,192]{3,2,1,0:T(8,128)(2,1)}, bf16[2,8,16,192]{3,2,1,0:T(8,128)(2,1)S(1)}, u32[]{:S(2)}, u32[]{:S(2)}) collective-permute-start(bf16[2,8,16,192]{3,2,1,0:T(8,128)(2,1)} %cot.1), channel_id=1, source_target_pairs={{0,7},{1,0},{2,1},{3,2},{4,3},{5,4},{6,5},{7,6},{8,15},{9,8},{10,9... | collective-permute-start | bytes 294920 | tf_op jit(solution)/shard_map/ppermute | solution.py:508
  9.0 1.3 %copy.13.reduce = bf16[2,768,192]{2,1,0:T(8,128)(2,1)S(1)} copy(bf16[2,768,192]{1,2,0:T(8,128)(2,1)} %param.12) | data formatting | bytes 1179648 | tf_op args[5]
  11.3 2.3 %shard_map.118 = (f32[2,8,16,192]{3,2,1,0:T(8,128)S(1)}, bf16[2,4,16,192]{3,2,1,0:T(8,128)(2,1)S(1)}, bf16[32,192]{1,0:T(8,128)(2,1)S(1)}, bf16[32,192]{1,0:T(8,128)(2,1)S(1)}) custom-call(bf16[2,8,16,192]{3,2,1,0:T(8,128)(2,1)S(1)} %copy-done.3, bf16[2,192,576]{2,1,0:T(8,128)(2,1)S(1)} %copy-done.1, bf16[2,192,192]{2,1,0:T(8,128)(2,1)S(1)} %copy-done.2, ...), custom_call_target="tpu_custom_call" | custom-call | tf_op jit(solution)/shard_map/pallas_call | solution.py:482
  13.8 1.4 %collective-permute-start.1 = (bf16[32,192]{1,0:T(8,128)(2,1)S(1)}, bf16[32,192]{1,0:T(8,128)(2,1)S(1)}, u32[]{:S(2)}, u32[]{:S(2)}) collective-permute-start(bf16[32,192]{1,0:T(8,128)(2,1)S(1)} %get-tuple-element.51), channel_id=1, source_target_pairs={{0,7},{1,0},{2,1},{3,2},{4,3},{5,4},{6,5},{7,6},{8,15},{9,8},{10,9... | collective-permute-start | bytes 36872 | tf_op jit(solution)/shard_map/ppermute | solution.py:508
  15.2 2.3 %collective-permute-done.1.beside = bf16[32,192]{1,0:T(8,128)(2,1)S(1)} collective-permute-done((bf16[32,192]{1,0:T(8,128)(2,1)S(1)}, bf16[32,192]{1,0:T(8,128)(2,1)S(1)}, u32[]{:S(2)}, u32[]{:S(2)}) %collective-permute-start.1) | collective-permute-done | bytes 12320 | tf_op jit(solution)/shard_map/ppermute | solution.py:508
  17.5 2.9 %collective-permute-start.2 = (bf16[32,192]{1,0:T(8,128)(2,1)S(1)}, bf16[32,192]{1,0:T(8,128)(2,1)S(1)}, u32[]{:S(2)}, u32[]{:S(2)}) collective-permute-start(bf16[32,192]{1,0:T(8,128)(2,1)S(1)} %get-tuple-element.52), channel_id=1, source_target_pairs={{0,31},{1,24},{2,25},{3,26},{4,27},{5,28},{6,29},{7,30},{8,7},{9,0... | collective-permute-start | bytes 36872 | tf_op jit(solution)/shard_map/ppermute | solution.py:508
  20.4 1.4 %collective-permute-done.2.across = bf16[32,192]{1,0:T(8,128)(2,1)S(1)} collective-permute-done((bf16[32,192]{1,0:T(8,128)(2,1)S(1)}, bf16[32,192]{1,0:T(8,128)(2,1)S(1)}, u32[]{:S(2)}, u32[]{:S(2)}) %collective-permute-start.2) | collective-permute-done | bytes 12320 | tf_op jit(solution)/shard_map/ppermute | solution.py:508
  21.8 4.4 %shard_map.119 = (f32[2,4,16,192]{3,2,1,0:T(8,128)S(1)}, bf16[2,4,16,192]{3,2,1,0:T(8,128)(2,1)S(1)}, bf16[32,192]{1,0:T(8,128)(2,1)S(1)}, bf16[32,192]{1,0:T(8,...) custom-call(f32[2,8,16,192]{3,2,1,0:T(8,128)S(1)} %get-tuple-element, ...), custom_call_target="tpu_custom_call" | custom-call | tf_op jit(solution)/shard_map/pallas_call | solution.py:482
  28.0 1.8 %collective-permute-start.7 = (bf16[32,192]{1,0:T(8,128)(2,1)S(1)}, bf16[32,192]{1,0:T(8,128)(2,1)S(1)}, u32[]{:S(2)}, u32[]{:S(2)}) collective-permute-start(bf16[32,192]{1,0:T(8,128)(2,1)S(1)} %get-tuple-element.55), channel_id=1, source_target_pairs={{0,1},{1,2},{2,3},{3,4},{4,5},{5,6},{6,7},{7,0},{8,9},{9,10},{10,1... | collective-permute-start | bytes 36872 | tf_op jit(solution)/shard_map/ppermute | solution.py:508
  30.3 4.7 %collective-permute-done.7.beside = bf16[32,192]{1,0:T(8,128)(2,1)S(1)} collective-permute-done((bf16[32,192]{1,0:T(8,128)(2,1)S(1)}, bf16[32,192]{1,0:T(8,128)(2,1)S(1)}, u32[]{:S(2)}, u32[]{:S(2)}) %collective-permute-start.7) | collective-permute-done | bytes 12320 | tf_op jit(solution)/shard_map/ppermute | solution.py:508
  35.0 1.6 %collective-permute-done.8.across = bf16[32,192]{1,0:T(8,128)(2,1)S(1)} collective-permute-done((bf16[32,192]{1,0:T(8,128)(2,1)S(1)}, bf16[32,192]{1,0:T(8,128)(2,1)S(1)}, u32[]{:S(2)}, u32[]{:S(2)}) %collective-permute-start.8) | collective-permute-done | bytes 12320 | tf_op jit(solution)/shard_map/ppermute | solution.py:508
  36.7 5.2 %shard_map.120 = (f32[2,8,16,192]{3,2,1,0:T(8,128)}, bf16[1792,128]{1,0:T(8,128)(2,1)S(1)}, bf16[1792,128]{1,0:T(8,128)(2,1)S(1)}) custom-call(bf16[2,8,16,192]{3,2,1,0:T(8,128)(2,1)S(1)} %copy-done.4, f32[2,4,16,192]{3,2,1,0:T(8,128)S(1)} %get-tuple-element.53.own, bf16[2,4,16,192]{3,2,1,0:T(8,128)(2,1)S(1)} %collective-permute-done.6.above, ...), custom_call_target="tpu_custom_call" | custom-call | tf_op jit(solution)/shard_map/pallas_call | solution.py:482
  42.1 1.2 %collective-permute-start.28 = (bf16[448,128]{1,0:T(8,128)(2,1)S(1)}, bf16[448,128]{1,0:T(8,128)(2,1)S(1)}, u32[]{:S(2)}, u32[]{:S(2)}) collective-permute-start(bf16[448,128]{1,0:T(8,128)(2,1)S(1)} %get-tuple-element.81), channel_id=1, source_target_pairs={{0,16},{1,17},{2,18},{3,19},{4,20},{5,21},{6,22},{7,23},{8,24},{9,... | collective-permute-start | bytes 344072 | tf_op jit(solution)/shard_map/ppermute | solution.py:514
  43.3 2.3 %collective-permute-start.29 = (bf16[448,128]{1,0:T(8,128)(2,1)S(1)}, bf16[448,128]{1,0:T(8,128)(2,1)S(1)}, u32[]{:S(2)}, u32[]{:S(2)}) collective-permute-start(bf16[448,128]{1,0:T(8,128)(2,1)S(1)} %get-tuple-element.82), channel_id=1, source_target_pairs={{0,17},{1,16},{2,19},{3,18},{4,21},{5,20},{6,23},{7,22},{8,25},{9,... | collective-permute-start | bytes 344072 | tf_op jit(solution)/shard_map/ppermute | solution.py:514
  47.7 1.7 %collective-permute-start.12 = (bf16[448,128]{1,0:T(8,128)(2,1)S(1)}, bf16[448,128]{1,0:T(8,128)(2,1)S(1)}, u32[]{:S(2)}, u32[]{:S(2)}) collective-permute-start(bf16[448,128]{1,0:T(8,128)(2,1)S(1)} %get-tuple-element.63), channel_id=1, source_target_pairs={{0,17},{1,16},{2,19},{3,18},{4,21},{5,20},{6,23},{7,22},{8,25},{9,... | collective-permute-start | bytes 344072 | tf_op jit(solution)/shard_map/ppermute | solution.py:514
  49.4 2.7 %collective-permute-done.29.refs_3_ = bf16[448,128]{1,0:T(8,128)(2,1)S(1)} collective-permute-done((bf16[448,128]{1,0:T(8,128)(2,1)S(1)}, bf16[448,128]{1,0:T(8,128)(2,1)S(1)}, u32[]{:S(2)}, u32[]{:S(2)}) %collective-permute-start.29) | collective-permute-done | bytes 114720 | tf_op jit(solution)/shard_map/ppermute | solution.py:514
  52.2 2.8 %collective-permute-start.31 = (bf16[112,128]{1,0:T(8,128)(2,1)S(1)}, bf16[112,128]{1,0:T(8,128)(2,1)S(1)}, u32[]{:S(2)}, u32[]{:S(2)}) collective-permute-start(bf16[112,128]{1,0:T(8,128)(2,1)S(1)} %get-tuple-element.85), channel_id=1, source_target_pairs={{0,4},{1,5},{2,6},{3,7},{4,0},{5,1},{6,2},{7,3},{8,12},{9,13},{10,... | collective-permute-start | bytes 86024 | tf_op jit(solution)/shard_map/ppermute | solution.py:514
  56.1 2.3 %collective-permute-start.32 = (bf16[112,128]{1,0:T(8,128)(2,1)S(1)}, bf16[112,128]{1,0:T(8,128)(2,1)S(1)}, u32[]{:S(2)}, u32[]{:S(2)}) collective-permute-start(bf16[112,128]{1,0:T(8,128)(2,1)S(1)} %get-tuple-element.86), channel_id=1, source_target_pairs={{0,6},{1,7},{2,4},{3,5},{4,2},{5,3},{6,0},{7,1},{8,14},{9,15},{10,... | collective-permute-start | bytes 86024 | tf_op jit(solution)/shard_map/ppermute | solution.py:514
  58.3 3.4 %collective-permute-done.32.refs_3_ = bf16[112,128]{1,0:T(8,128)(2,1)S(1)} collective-permute-done((bf16[112,128]{1,0:T(8,128)(2,1)S(1)}, bf16[112,128]{1,0:T(8,128)(2,1)S(1)}, u32[]{:S(2)}, u32[]{:S(2)}) %collective-permute-start.32) | collective-permute-done | bytes 28704 | tf_op jit(solution)/shard_map/ppermute | solution.py:514
  61.8 2.3 %collective-permute-start.35 = (bf16[112,128]{1,0:T(8,128)(2,1)S(1)}, bf16[112,128]{1,0:T(8,128)(2,1)S(1)}, u32[]{:S(2)}, u32[]{:S(2)}) collective-permute-start(bf16[112,128]{1,0:T(8,128)(2,1)S(1)} %shard_map.128.refs_0_), channel_id=1, source_target_pairs={{0,6},{1,7},{2,4},{3,5},{4,2},{5,3},{6,0},{7,1},{8,14},{9,15},{10,... | collective-permute-start | bytes 86024 | tf_op jit(solution)/shard_map/ppermute | solution.py:514
  64.1 2.1 %collective-permute-start.33 = (bf16[112,128]{1,0:T(8,128)(2,1)S(1)}, bf16[112,128]{1,0:T(8,128)(2,1)S(1)}, u32[]{:S(2)}, u32[]{:S(2)}) collective-permute-start(bf16[112,128]{1,0:T(8,128)(2,1)S(1)} %shard_map.128.refs_0_), channel_id=1, source_target_pairs={{0,2},{1,3},{2,0},{3,1},{4,6},{5,7},{6,4},{7,5},{8,10},{9,11},{10,... | collective-permute-start | bytes 86024 | tf_op jit(solution)/shard_map/ppermute | solution.py:514
  66.4 2.8 %collective-permute-start.14 = (bf16[112,128]{1,0:T(8,128)(2,1)S(1)}, bf16[112,128]{1,0:T(8,128)(2,1)S(1)}, u32[]{:S(2)}, u32[]{:S(2)}) collective-permute-start(bf16[112,128]{1,0:T(8,128)(2,1)S(1)} %get-tuple-element.66), channel_id=1, source_target_pairs={{0,4},{1,5},{2,6},{3,7},{4,0},{5,1},{6,2},{7,3},{8,12},{9,13},{10,... | collective-permute-start | bytes 86024 | tf_op jit(solution)/shard_map/ppermute | solution.py:514
  69.2 1.6 %collective-permute-start.15 = (bf16[112,128]{1,0:T(8,128)(2,1)S(1)}, bf16[112,128]{1,0:T(8,128)(2,1)S(1)}, u32[]{:S(2)}, u32[]{:S(2)}) collective-permute-start(bf16[112,128]{1,0:T(8,128)(2,1)S(1)} %get-tuple-element.67), channel_id=1, source_target_pairs={{0,6},{1,7},{2,4},{3,5},{4,2},{5,3},{6,0},{7,1},{8,14},{9,15},{10,... | collective-permute-start | bytes 86024 | tf_op jit(solution)/shard_map/ppermute | solution.py:514
  72.7 1.8 %collective-permute-start.36 = (bf16[448,128]{1,0:T(8,128)(2,1)S(1)}, bf16[448,128]{1,0:T(8,128)(2,1)S(1)}, u32[]{:S(2)}, u32[]{:S(2)}) collective-permute-start(bf16[448,128]{1,0:T(8,128)(2,1)S(1)} %shard_map.129.refs_8_), channel_id=1, source_target_pairs={{0,1},{1,0},{2,3},{3,2},{4,5},{5,4},{6,7},{7,6},{8,9},{9,8},{10,11... | collective-permute-start | bytes 344072 | tf_op jit(solution)/shard_map/ppermute | solution.py:514
  74.9 1.9 %collective-permute-start.18 = (bf16[112,128]{1,0:T(8,128)(2,1)S(1)}, bf16[112,128]{1,0:T(8,128)(2,1)S(1)}, u32[]{:S(2)}, u32[]{:S(2)}) collective-permute-start(bf16[112,128]{1,0:T(8,128)(2,1)S(1)} %shard_map.123.refs_0_), channel_id=1, source_target_pairs={{0,6},{1,7},{2,4},{3,5},{4,2},{5,3},{6,0},{7,1},{8,14},{9,15},{10,... | collective-permute-start | bytes 86024 | tf_op jit(solution)/shard_map/ppermute | solution.py:514
  76.8 3.8 %collective-permute-done.18.refs_3_ = bf16[112,128]{1,0:T(8,128)(2,1)S(1)} collective-permute-done((bf16[112,128]{1,0:T(8,128)(2,1)S(1)}, bf16[112,128]{1,0:T(8,128)(2,1)S(1)}, u32[]{:S(2)}, u32[]{:S(2)}) %collective-permute-start.18) | collective-permute-done | bytes 28704 | tf_op jit(solution)/shard_map/ppermute | solution.py:514
  80.6 4.9 %collective-permute-done.17.refs_2_ = bf16[112,128]{1,0:T(8,128)(2,1)S(1)} collective-permute-done((bf16[112,128]{1,0:T(8,128)(2,1)S(1)}, bf16[112,128]{1,0:T(8,128)(2,1)S(1)}, u32[]{:S(2)}, u32[]{:S(2)}) %collective-permute-start.17) | collective-permute-done | bytes 28704 | tf_op jit(solution)/shard_map/ppermute | solution.py:514
  85.5 3.9 %collective-permute-done.16.refs_1_ = bf16[112,128]{1,0:T(8,128)(2,1)S(1)} collective-permute-done((bf16[112,128]{1,0:T(8,128)(2,1)S(1)}, bf16[112,128]{1,0:T(8,128)(2,1)S(1)}, u32[]{:S(2)}, u32[]{:S(2)}) %collective-permute-start.16) | collective-permute-done | bytes 28704 | tf_op jit(solution)/shard_map/ppermute | solution.py:514
  91.3 1.8 %collective-permute-start.19 = (bf16[448,128]{1,0:T(8,128)(2,1)S(1)}, bf16[448,128]{1,0:T(8,128)(2,1)S(1)}, u32[]{:S(2)}, u32[]{:S(2)}) collective-permute-start(bf16[448,128]{1,0:T(8,128)(2,1)S(1)} %shard_map.124.refs_0_), channel_id=1, source_target_pairs={{0,1},{1,0},{2,3},{3,2},{4,5},{5,4},{6,7},{7,6},{8,9},{9,8},{10,11... | collective-permute-start | bytes 344072 | tf_op jit(solution)/shard_map/ppermute | solution.py:514
  93.6 2.9 %collective-permute-done.21.refs_3_ = bf16[448,128]{1,0:T(8,128)(2,1)S(1)} collective-permute-done((bf16[448,128]{1,0:T(8,128)(2,1)S(1)}, bf16[448,128]{1,0:T(8,128)(2,1)S(1)}, u32[]{:S(2)}, u32[]{:S(2)}) %collective-permute-start.21) | collective-permute-done | bytes 114720 | tf_op jit(solution)/shard_map/ppermute | solution.py:514
  99.9 1.9 %shard_map.130 = (f32[2,192,576]{2,1,0:T(8,128)}, f32[2,192,192]{2,1,0:T(8,128)}, f32[2,192,768]{2,1,0:T(8,128)}, f32[2,768,192]{2,1,0:T(8,128)S(1)}, f32[2,6,225]{2,1,0:T(8,128)S(1)}) custom-call(bf16[448,128]{1,0:T(8,128)(2,1)S(1)} %shard_map.124.refs_0_, bf16[448,128]{1,0:T(8,128)(2,1)S(1)} %collective-permute-done.19.refs_1_, ...), custom_call_target="tpu_custom_call" | custom-call | tf_op jit(solution)/shard_map/pallas_call | solution.py:482
  102.3 1.5 %copy.19 = f32[2,768,192]{1,2,0:T(8,128)} copy(f32[2,768,192]{2,1,0:T(8,128)S(1)} %get-tuple-element.96) | data formatting | bytes 2359296
  (83 shorter events, 18.2 us)
Async XLA Ops:
  0.7 21.2 %collective-permute-start.4 = (bf16[2,8,16,192]{3,2,1,0:T(8,128)(2,1)}, bf16[2,8,16,192]{3,2,1,0:T(8,128)(2,1)S(1)}, u32[]{:S(2)}, u32[]{:S(2)}) collective-permute-start(bf16[2,8,16,192]{3,2,1,0:T(8,128)(2,1)} %cot.1), channel_id=1, source_target_pairs={{0,7},{1,0},{2,1},{3,2},{4,3},{5,4},{6,5},{7,6},{8,15},{9,8},{10,9... | collective-permute-start | bytes 294920 | tf_op jit(solution)/shard_map/ppermute | solution.py:508
  6.7 15.1 %collective-permute-start.3 = (bf16[2,8,16,192]{3,2,1,0:T(8,128)(2,1)}, bf16[2,8,16,192]{3,2,1,0:T(8,128)(2,1)S(1)}, u32[]{:S(2)}, u32[]{:S(2)}) collective-permute-start(bf16[2,8,16,192]{3,2,1,0:T(8,128)(2,1)} %cot.1), channel_id=1, source_target_pairs={{0,24},{1,25},{2,26},{3,27},{4,28},{5,29},{6,30},{7,31},{8,0},{9,1... | collective-permute-start | bytes 294920 | tf_op jit(solution)/shard_map/ppermute | solution.py:508
  7.4 14.5 %collective-permute-start.5 = (bf16[2,8,16,192]{3,2,1,0:T(8,128)(2,1)}, bf16[2,8,16,192]{3,2,1,0:T(8,128)(2,1)S(1)}, u32[]{:S(2)}, u32[]{:S(2)}) collective-permute-start(bf16[2,8,16,192]{3,2,1,0:T(8,128)(2,1)} %cot.1), channel_id=1, source_target_pairs={{0,31},{1,24},{2,25},{3,26},{4,27},{5,28},{6,29},{7,30},{8,7},{9,0... | collective-permute-start | bytes 294920 | tf_op jit(solution)/shard_map/ppermute | solution.py:508
  13.5 8.3 %collective-permute-start = (bf16[2,4,16,192]{3,2,1,0:T(8,128)(2,1)S(1)}, bf16[2,4,16,192]{3,2,1,0:T(8,128)(2,1)S(1)}, u32[]{:S(2)}, u32[]{:S(2)}) collective-permute-start(bf16[2,4,16,192]{3,2,1,0:T(8,128)(2,1)S(1)} %get-tuple-element.50), channel_id=1, source_target_pairs={{0,24},{1,25},{2,26},{3,27},{4,28},{5,29},{6,30},{7,31},{8,0},{9,1... | collective-permute-start | bytes 147464 | tf_op jit(solution)/shard_map/ppermute | solution.py:508
  27.1 14.8 %collective-permute-start.26 = (bf16[1792,128]{1,0:T(8,128)(2,1)S(1)}, bf16[1792,128]{1,0:T(8,128)(2,1)S(1)}, u32[]{:S(2)}, u32[]{:S(2)}) collective-permute-start(bf16[1792,128]{1,0:T(8,128)(2,1)S(1)} %get-tuple-element.78), channel_id=1, source_target_pairs={{0,8},{1,9},{2,10},{3,11},{4,12},{5,13},{6,14},{7,15},{8,0},{9,1},... | collective-permute-start | bytes 1376264 | tf_op jit(solution)/shard_map/ppermute | solution.py:514
  27.9 8.7 %collective-permute-start.6 = (bf16[2,4,16,192]{3,2,1,0:T(8,128)(2,1)S(1)}, bf16[2,4,16,192]{3,2,1,0:T(8,128)(2,1)S(1)}, u32[]{:S(2)}, u32[]{:S(2)}) collective-permute-start(bf16[2,4,16,192]{3,2,1,0:T(8,128)(2,1)S(1)} %get-tuple-element.54), channel_id=1, source_target_pairs={{0,8},{1,9},{2,10},{3,11},{4,12},{5,13},{6,14},{7,15},{8,16},{9,17... | collective-permute-start | bytes 147464 | tf_op jit(solution)/shard_map/ppermute | solution.py:508
  28.0 7.0 %collective-permute-start.7 = (bf16[32,192]{1,0:T(8,128)(2,1)S(1)}, bf16[32,192]{1,0:T(8,128)(2,1)S(1)}, u32[]{:S(2)}, u32[]{:S(2)}) collective-permute-start(bf16[32,192]{1,0:T(8,128)(2,1)S(1)} %get-tuple-element.55), channel_id=1, source_target_pairs={{0,1},{1,2},{2,3},{3,4},{4,5},{5,6},{6,7},{7,0},{8,9},{9,10},{10,1... | collective-permute-start | bytes 36872 | tf_op jit(solution)/shard_map/ppermute | solution.py:508
  29.8 6.8 %collective-permute-start.8 = (bf16[32,192]{1,0:T(8,128)(2,1)S(1)}, bf16[32,192]{1,0:T(8,128)(2,1)S(1)}, u32[]{:S(2)}, u32[]{:S(2)}) collective-permute-start(bf16[32,192]{1,0:T(8,128)(2,1)S(1)} %get-tuple-element.56), channel_id=1, source_target_pairs={{0,9},{1,10},{2,11},{3,12},{4,13},{5,14},{6,15},{7,8},{8,17},{9,18... | collective-permute-start | bytes 36872 | tf_op jit(solution)/shard_map/ppermute | solution.py:508
  42.0 5.6 %collective-permute-start.27 = (bf16[448,128]{1,0:T(8,128)(2,1)S(1)}, bf16[448,128]{1,0:T(8,128)(2,1)S(1)}, u32[]{:S(2)}, u32[]{:S(2)}) collective-permute-start(bf16[448,128]{1,0:T(8,128)(2,1)S(1)} %get-tuple-element.80), channel_id=1, source_target_pairs={{0,1},{1,0},{2,3},{3,2},{4,5},{5,4},{6,7},{7,6},{8,9},{9,8},{10,11... | collective-permute-start | bytes 344072 | tf_op jit(solution)/shard_map/ppermute | solution.py:514
  42.1 7.2 %collective-permute-start.28 = (bf16[448,128]{1,0:T(8,128)(2,1)S(1)}, bf16[448,128]{1,0:T(8,128)(2,1)S(1)}, u32[]{:S(2)}, u32[]{:S(2)}) collective-permute-start(bf16[448,128]{1,0:T(8,128)(2,1)S(1)} %get-tuple-element.81), channel_id=1, source_target_pairs={{0,16},{1,17},{2,18},{3,19},{4,20},{5,21},{6,22},{7,23},{8,24},{9,... | collective-permute-start | bytes 344072 | tf_op jit(solution)/shard_map/ppermute | solution.py:514
  43.3 8.7 %collective-permute-start.29 = (bf16[448,128]{1,0:T(8,128)(2,1)S(1)}, bf16[448,128]{1,0:T(8,128)(2,1)S(1)}, u32[]{:S(2)}, u32[]{:S(2)}) collective-permute-start(bf16[448,128]{1,0:T(8,128)(2,1)S(1)} %get-tuple-element.82), channel_id=1, source_target_pairs={{0,17},{1,16},{2,19},{3,18},{4,21},{5,20},{6,23},{7,22},{8,25},{9,... | collective-permute-start | bytes 344072 | tf_op jit(solution)/shard_map/ppermute | solution.py:514
  45.8 18.3 %collective-permute-start.10 = (bf16[448,128]{1,0:T(8,128)(2,1)S(1)}, bf16[448,128]{1,0:T(8,128)(2,1)S(1)}, u32[]{:S(2)}, u32[]{:S(2)}) collective-permute-start(bf16[448,128]{1,0:T(8,128)(2,1)S(1)} %get-tuple-element.61), channel_id=1, source_target_pairs={{0,1},{1,0},{2,3},{3,2},{4,5},{5,4},{6,7},{7,6},{8,9},{9,8},{10,11... | collective-permute-start | bytes 344072 | tf_op jit(solution)/shard_map/ppermute | solution.py:514
  45.9 20.3 %collective-permute-start.11 = (bf16[448,128]{1,0:T(8,128)(2,1)S(1)}, bf16[448,128]{1,0:T(8,128)(2,1)S(1)}, u32[]{:S(2)}, u32[]{:S(2)}) collective-permute-start(bf16[448,128]{1,0:T(8,128)(2,1)S(1)} %get-tuple-element.62), channel_id=1, source_target_pairs={{0,16},{1,17},{2,18},{3,19},{4,20},{5,21},{6,22},{7,23},{8,24},{9,... | collective-permute-start | bytes 344072 | tf_op jit(solution)/shard_map/ppermute | solution.py:514
  47.7 18.6 %collective-permute-start.12 = (bf16[448,128]{1,0:T(8,128)(2,1)S(1)}, bf16[448,128]{1,0:T(8,128)(2,1)S(1)}, u32[]{:S(2)}, u32[]{:S(2)}) collective-permute-start(bf16[448,128]{1,0:T(8,128)(2,1)S(1)} %get-tuple-element.63), channel_id=1, source_target_pairs={{0,17},{1,16},{2,19},{3,18},{4,21},{5,20},{6,23},{7,22},{8,25},{9,... | collective-permute-start | bytes 344072 | tf_op jit(solution)/shard_map/ppermute | solution.py:514
  52.2 6.1 %collective-permute-start.31 = (bf16[112,128]{1,0:T(8,128)(2,1)S(1)}, bf16[112,128]{1,0:T(8,128)(2,1)S(1)}, u32[]{:S(2)}, u32[]{:S(2)}) collective-permute-start(bf16[112,128]{1,0:T(8,128)(2,1)S(1)} %get-tuple-element.85), channel_id=1, source_target_pairs={{0,4},{1,5},{2,6},{3,7},{4,0},{5,1},{6,2},{7,3},{8,12},{9,13},{10,... | collective-permute-start | bytes 86024 | tf_op jit(solution)/shard_map/ppermute | solution.py:514
  56.1 5.7 %collective-permute-start.32 = (bf16[112,128]{1,0:T(8,128)(2,1)S(1)}, bf16[112,128]{1,0:T(8,128)(2,1)S(1)}, u32[]{:S(2)}, u32[]{:S(2)}) collective-permute-start(bf16[112,128]{1,0:T(8,128)(2,1)S(1)} %get-tuple-element.86), channel_id=1, source_target_pairs={{0,6},{1,7},{2,4},{3,5},{4,2},{5,3},{6,0},{7,1},{8,14},{9,15},{10,... | collective-permute-start | bytes 86024 | tf_op jit(solution)/shard_map/ppermute | solution.py:514
  61.8 7.4 %collective-permute-start.35 = (bf16[112,128]{1,0:T(8,128)(2,1)S(1)}, bf16[112,128]{1,0:T(8,128)(2,1)S(1)}, u32[]{:S(2)}, u32[]{:S(2)}) collective-permute-start(bf16[112,128]{1,0:T(8,128)(2,1)S(1)} %shard_map.128.refs_0_), channel_id=1, source_target_pairs={{0,6},{1,7},{2,4},{3,5},{4,2},{5,3},{6,0},{7,1},{8,14},{9,15},{10,... | collective-permute-start | bytes 86024 | tf_op jit(solution)/shard_map/ppermute | solution.py:514
  64.1 6.7 %collective-permute-start.34 = (bf16[112,128]{1,0:T(8,128)(2,1)S(1)}, bf16[112,128]{1,0:T(8,128)(2,1)S(1)}, u32[]{:S(2)}, u32[]{:S(2)}) collective-permute-start(bf16[112,128]{1,0:T(8,128)(2,1)S(1)} %shard_map.128.refs_0_), channel_id=1, source_target_pairs={{0,4},{1,5},{2,6},{3,7},{4,0},{5,1},{6,2},{7,3},{8,12},{9,13},{10,... | collective-permute-start | bytes 86024 | tf_op jit(solution)/shard_map/ppermute | solution.py:514
  64.1 6.7 %collective-permute-start.33 = (bf16[112,128]{1,0:T(8,128)(2,1)S(1)}, bf16[112,128]{1,0:T(8,128)(2,1)S(1)}, u32[]{:S(2)}, u32[]{:S(2)}) collective-permute-start(bf16[112,128]{1,0:T(8,128)(2,1)S(1)} %shard_map.128.refs_0_), channel_id=1, source_target_pairs={{0,2},{1,3},{2,0},{3,1},{4,6},{5,7},{6,4},{7,5},{8,10},{9,11},{10,... | collective-permute-start | bytes 86024 | tf_op jit(solution)/shard_map/ppermute | solution.py:514
  66.3 5.3 %collective-permute-start.13 = (bf16[112,128]{1,0:T(8,128)(2,1)S(1)}, bf16[112,128]{1,0:T(8,128)(2,1)S(1)}, u32[]{:S(2)}, u32[]{:S(2)}) collective-permute-start(bf16[112,128]{1,0:T(8,128)(2,1)S(1)} %get-tuple-element.65), channel_id=1, source_target_pairs={{0,2},{1,3},{2,0},{3,1},{4,6},{5,7},{6,4},{7,5},{8,10},{9,11},{10,... | collective-permute-start | bytes 86024 | tf_op jit(solution)/shard_map/ppermute | solution.py:514
  66.4 6.3 %collective-permute-start.14 = (bf16[112,128]{1,0:T(8,128)(2,1)S(1)}, bf16[112,128]{1,0:T(8,128)(2,1)S(1)}, u32[]{:S(2)}, u32[]{:S(2)}) collective-permute-start(bf16[112,128]{1,0:T(8,128)(2,1)S(1)} %get-tuple-element.66), channel_id=1, source_target_pairs={{0,4},{1,5},{2,6},{3,7},{4,0},{5,1},{6,2},{7,3},{8,12},{9,13},{10,... | collective-permute-start | bytes 86024 | tf_op jit(solution)/shard_map/ppermute | solution.py:514
  69.2 5.7 %collective-permute-start.15 = (bf16[112,128]{1,0:T(8,128)(2,1)S(1)}, bf16[112,128]{1,0:T(8,128)(2,1)S(1)}, u32[]{:S(2)}, u32[]{:S(2)}) collective-permute-start(bf16[112,128]{1,0:T(8,128)(2,1)S(1)} %get-tuple-element.67), channel_id=1, source_target_pairs={{0,6},{1,7},{2,4},{3,5},{4,2},{5,3},{6,0},{7,1},{8,14},{9,15},{10,... | collective-permute-start | bytes 86024 | tf_op jit(solution)/shard_map/ppermute | solution.py:514
  70.8 18.7 %collective-permute-start.39 = (bf16[448,128]{1,0:T(8,128)(2,1)S(1)}, bf16[448,128]{1,0:T(8,128)(2,1)S(1)}, u32[]{:S(2)}, u32[]{:S(2)}) collective-permute-start(bf16[448,128]{1,0:T(8,128)(2,1)S(1)} %shard_map.129.refs_8_), channel_id=1, source_target_pairs={{0,8},{1,9},{2,10},{3,11},{4,12},{5,13},{6,14},{7,15},{8,0},{9,1},... | collective-permute-start | bytes 344072 | tf_op jit(solution)/shard_map/ppermute | solution.py:514
  70.9 19.2 %collective-permute-start.38 = (bf16[448,128]{1,0:T(8,128)(2,1)S(1)}, bf16[448,128]{1,0:T(8,128)(2,1)S(1)}, u32[]{:S(2)}, u32[]{:S(2)}) collective-permute-start(bf16[448,128]{1,0:T(8,128)(2,1)S(1)} %shard_map.129.refs_8_), channel_id=1, source_target_pairs={{0,17},{1,16},{2,19},{3,18},{4,21},{5,20},{6,23},{7,22},{8,25},{9,... | collective-permute-start | bytes 344072 | tf_op jit(solution)/shard_map/ppermute | solution.py:514
  71.6 19.7 %collective-permute-start.37 = (bf16[448,128]{1,0:T(8,128)(2,1)S(1)}, bf16[448,128]{1,0:T(8,128)(2,1)S(1)}, u32[]{:S(2)}, u32[]{:S(2)}) collective-permute-start(bf16[448,128]{1,0:T(8,128)(2,1)S(1)} %shard_map.129.refs_8_), channel_id=1, source_target_pairs={{0,16},{1,17},{2,18},{3,19},{4,20},{5,21},{6,22},{7,23},{8,24},{9,... | collective-permute-start | bytes 344072 | tf_op jit(solution)/shard_map/ppermute | solution.py:514
  72.7 20.4 %collective-permute-start.36 = (bf16[448,128]{1,0:T(8,128)(2,1)S(1)}, bf16[448,128]{1,0:T(8,128)(2,1)S(1)}, u32[]{:S(2)}, u32[]{:S(2)}) collective-permute-start(bf16[448,128]{1,0:T(8,128)(2,1)S(1)} %shard_map.129.refs_8_), channel_id=1, source_target_pairs={{0,1},{1,0},{2,3},{3,2},{4,5},{5,4},{6,7},{7,6},{8,9},{9,8},{10,11... | collective-permute-start | bytes 344072 | tf_op jit(solution)/shard_map/ppermute | solution.py:514
  74.9 5.7 %collective-permute-start.18 = (bf16[112,128]{1,0:T(8,128)(2,1)S(1)}, bf16[112,128]{1,0:T(8,128)(2,1)S(1)}, u32[]{:S(2)}, u32[]{:S(2)}) collective-permute-start(bf16[112,128]{1,0:T(8,128)(2,1)S(1)} %shard_map.123.refs_0_), channel_id=1, source_target_pairs={{0,6},{1,7},{2,4},{3,5},{4,2},{5,3},{6,0},{7,1},{8,14},{9,15},{10,... | collective-permute-start | bytes 86024 | tf_op jit(solution)/shard_map/ppermute | solution.py:514
  89.5 6.9 %collective-permute-start.21 = (bf16[448,128]{1,0:T(8,128)(2,1)S(1)}, bf16[448,128]{1,0:T(8,128)(2,1)S(1)}, u32[]{:S(2)}, u32[]{:S(2)}) collective-permute-start(bf16[448,128]{1,0:T(8,128)(2,1)S(1)} %shard_map.124.refs_0_), channel_id=1, source_target_pairs={{0,17},{1,16},{2,19},{3,18},{4,21},{5,20},{6,23},{7,22},{8,25},{9,... | collective-permute-start | bytes 344072 | tf_op jit(solution)/shard_map/ppermute | solution.py:514
  90.1 7.1 %collective-permute-start.20 = (bf16[448,128]{1,0:T(8,128)(2,1)S(1)}, bf16[448,128]{1,0:T(8,128)(2,1)S(1)}, u32[]{:S(2)}, u32[]{:S(2)}) collective-permute-start(bf16[448,128]{1,0:T(8,128)(2,1)S(1)} %shard_map.124.refs_0_), channel_id=1, source_target_pairs={{0,16},{1,17},{2,18},{3,19},{4,20},{5,21},{6,22},{7,23},{8,24},{9,... | collective-permute-start | bytes 344072 | tf_op jit(solution)/shard_map/ppermute | solution.py:514
  91.3 7.1 %collective-permute-start.19 = (bf16[448,128]{1,0:T(8,128)(2,1)S(1)}, bf16[448,128]{1,0:T(8,128)(2,1)S(1)}, u32[]{:S(2)}, u32[]{:S(2)}) collective-permute-start(bf16[448,128]{1,0:T(8,128)(2,1)S(1)} %shard_map.124.refs_0_), channel_id=1, source_target_pairs={{0,1},{1,0},{2,3},{3,2},{4,5},{5,4},{6,7},{7,6},{8,9},{9,8},{10,11... | collective-permute-start | bytes 344072 | tf_op jit(solution)/shard_map/ppermute | solution.py:514
  93.0 5.4 %collective-permute-start.42 = (bf16[448,128]{1,0:T(8,128)(2,1)S(1)}, bf16[448,128]{1,0:T(8,128)(2,1)S(1)}, u32[]{:S(2)}, u32[]{:S(2)}) collective-permute-start(bf16[448,128]{1,0:T(8,128)(2,1)S(1)} %collective-permute-done.38.refs_11_), channel_id=1, source_target_pairs={{0,8},{1,9},{2,10},{3,11},{4,12},{5,13},{6,14},{7,15},{8,0},{9,1},... | collective-permute-start | bytes 344072 | tf_op jit(solution)/shard_map/ppermute | solution.py:514
  93.0 5.9 %collective-permute-start.41 = (bf16[448,128]{1,0:T(8,128)(2,1)S(1)}, bf16[448,128]{1,0:T(8,128)(2,1)S(1)}, u32[]{:S(2)}, u32[]{:S(2)}) collective-permute-start(bf16[448,128]{1,0:T(8,128)(2,1)S(1)} %collective-permute-done.37.refs_10_), channel_id=1, source_target_pairs={{0,8},{1,9},{2,10},{3,11},{4,12},{5,13},{6,14},{7,15},{8,0},{9,1},... | collective-permute-start | bytes 344072 | tf_op jit(solution)/shard_map/ppermute | solution.py:514
  (17 other events, 86.1 us)

commit v2 on v1

v2 whole, which is shorter than its diff:
```python
import functools
import math

import jax
import jax.numpy as jnp
from jax import lax
from jax.experimental import pallas as pl
from jax.experimental.pallas import tpu as pltpu
from jax.sharding import PartitionSpec as P

WIN = 8
SHIFT = 4
BF = jnp.bfloat16
F32 = jnp.float32
LIMIT = 48 * 1024 * 1024
FULL = 62 * 1024 * 1024
ROOT_HALF = 0.7071067811865476
DENSITY = 0.3989422804014327


def dot(a, b):
    return lax.dot_general(a, b, (((1,), (0,)), ((), ())), preferred_element_type=F32)


def dot_nt(a, b):
    return lax.dot_general(a, b, (((1,), (1,)), ((), ())), preferred_element_type=F32)


def dot_tn(a, b):
    return lax.dot_general(a, b, (((0,), (0,)), ((), ())), preferred_element_type=F32)


def iota(shape, axis):
    return lax.broadcasted_iota(jnp.int32, shape, axis)


def norm(field):
    center = field - jnp.mean(field, axis=0, keepdims=True)
    spread = jnp.mean(center * center, axis=0, keepdims=True)
    scale = lax.rsqrt(spread + 1e-05)
    return center * scale, scale


def norm_back(grad, normed, scale):
    along = jnp.mean(grad * normed, axis=0, keepdims=True)
    return scale * (grad - jnp.mean(grad, axis=0, keepdims=True) - normed * along)


class Late:
    def __init__(self, copy, here):
        self.copy, self.here = copy, here

    def __getitem__(self, index):
        if self.copy is not None:
            self.copy.wait()
            self.copy = None
        return self.here[index]


def first_half(shape):
    return iota(shape, 1) < 64


def head_masks(heads, head):
    tall = (heads * 64, heads * head)
    wide = (heads * head, heads * 64)
    over = (iota(tall, 0) // 64 == iota(tall, 1) // head).astype(F32).astype(BF)
    across = (iota(wide, 0) // head == iota(wide, 1) // 64).astype(F32).astype(BF)
    return over, across


def spread_bias(table, heads):
    entries = table.shape[1]
    side = 2 * WIN - 1
    lanes = iota((entries, 256), 1)
    rows = iota((entries, 256), 0)
    place = lanes % 128
    down = place // 8 - 8
    right = place % 8 - jnp.where(lanes >= 128, 8, 0)
    wanted = (down + WIN - 1) * side + right + WIN - 1
    fits = (down >= 1 - WIN) & (right >= 1 - WIN)
    pick = (fits & (wanted == rows)).astype(F32)
    vectors = lax.dot_general(
        table, pick, (((1,), (0,)), ((), ())), precision=lax.Precision.HIGHEST, preferred_element_type=F32
    )
    ahead = jnp.broadcast_to(vectors[:, None, :128], (heads, 8, 128)).reshape(heads * 8, 128)
    behind = jnp.broadcast_to(vectors[:, None, 128:], (heads, 8, 128)).reshape(heads * 8, 128)
    shape = (heads * 8, 128)
    col_j = iota(shape, 0) % 8
    col_i = iota(shape, 1) % 8
    built = jnp.zeros(shape, F32)
    for c in range(8):
        line = jnp.where(col_i >= c, pltpu.roll(ahead, 64 + c, 1), pltpu.roll(behind, 56 + c, 1))
        built = jnp.where(col_j == c, line, built)
    rolled = [built] + [pltpu.roll(built, 8 * r, 1) for r in range(1, 8)]
    rolled = [jnp.where(first_half(shape), one, pltpu.roll(one, 64, 1)) for one in rolled]
    parts = []
    for h in range(heads):
        for r in range(8):
            parts.append(rolled[r][8 * h : 8 * h + 8])
    return jnp.concatenate(parts, axis=0)


def fold_bias(grad, heads):
    folded = jnp.where(first_half(grad.shape), grad + pltpu.roll(grad, 64, 1), 0.0)
    split = folded.reshape(heads, 8, 8, 128)
    total = jnp.zeros((heads * 8, 128), F32)
    for r in range(8):
        piece = split[:, r].reshape(heads * 8, 128)
        total = total + pltpu.roll(piece, 64 - 8 * r, 1)
    shape = (heads * 8, 128)
    col_j = iota(shape, 0) % 8
    col_i = iota(shape, 1) % 8
    ahead = jnp.zeros(shape, F32)
    behind = jnp.zeros(shape, F32)
    for c in range(8):
        mine = jnp.where((col_j == c) & (col_i >= c), total, 0.0)
        ahead = ahead + (pltpu.roll(mine, 128 - c, 1) if c else mine)
        rest = jnp.where((col_j == c) & (col_i < c), total, 0.0)
        behind = behind + pltpu.roll(rest, 8 - c, 1)
    ahead = jnp.sum(ahead.reshape(heads, 8, 128), axis=1)
    behind = jnp.sum(behind.reshape(heads, 8, 128), axis=1)
    return ahead, behind


def shift_mask(shape, last_row, last_col):
    j = iota(shape, 0) % 64
    lane = iota(shape, 1)
    i = lane % 64
    low = (j // 8 >= SHIFT) != (i // 8 >= SHIFT)
    side = (j % 8 >= SHIFT) != (i % 8 >= SHIFT)
    differ = (low & last_row) | (side & (lane >= 64) & last_col)
    return jnp.where(differ, -10000.0, 0.0)


def wide_of(field, heads, across):
    field = field.astype(F32)
    half = first_half(field.shape)
    swapped = pltpu.roll(field, 64, 1)
    return [
        jnp.concatenate([one.astype(BF)] * (heads // 2), axis=1) * across
        for one in (jnp.where(half, field, swapped), jnp.where(half, swapped, field))
    ]


def tall_of(natural, heads, over):
    return [jnp.concatenate([natural[64 * w : 64 * w + 64]] * heads, axis=0) * over for w in range(2)]


def forward(weights, field, bias, heads):
    width, tokens = field.shape
    head = width // heads
    over, across = head_masks(heads, head)
    center, scale = norm(field)
    normed = center.astype(BF)
    mixed = dot_tn(weights[0][...], normed)
    query = (mixed[:width] * head ** (-0.5)).astype(BF)
    keys = mixed[width : 2 * width].astype(BF)
    natural = mixed[width:].T.astype(BF)
    values = natural[:, width:]
    probs, attended = [], []
    half = first_half((width, 128))
    tall_half = first_half((heads * 64, 128))
    for p in range(tokens // 128):
        lanes = slice(128 * p, 128 * p + 128)
        wide = wide_of(mixed[2 * width :, lanes], heads, across)
        tall = tall_of(natural[lanes, :width], heads, over)
        q = query[:, lanes]
        scores = jnp.where(tall_half, dot(tall[0], q), dot(tall[1], q)) + bias
        scores = scores.reshape(heads, 64, 128)
        expos = jnp.exp(scores - jnp.max(scores, axis=1, keepdims=True))
        prob = (expos / jnp.sum(expos, axis=1, keepdims=True)).reshape(heads * 64, 128)
        prob_b = prob.astype(BF)
        attended.append(jnp.where(half, dot(wide[0], prob_b), dot(wide[1], prob_b)))
        probs.append(prob)
    attended = jnp.concatenate(attended, axis=1).astype(BF)
    prob = jnp.concatenate(probs, axis=1)
    resid = field + dot_tn(weights[1][...], attended)
    center_two, scale_two = norm(resid)
    normed_two = center_two.astype(BF)
    pre = dot_tn(weights[2][...], normed_two)
    bell = 0.5 * (1.0 + lax.erf(pre * ROOT_HALF))
    hidden = (pre * bell).astype(BF)
    saved = (center, scale, query, keys, values, prob, attended, center_two, scale_two, hidden)
    return resid, hidden, pre, bell, saved


def slope_of(pre, bell):
    return bell + pre * (DENSITY * jnp.exp(-0.5 * pre * pre))


def backward(weights, saved, slope, grad, heads):
    qkv_w, proj_w, expand_w, reduce_w = (w[...] for w in weights)
    center, scale, query, keys, values, prob, attended, center_two, scale_two, hidden = saved
    width, tokens = grad.shape
    head = width // heads
    over, across = head_masks(heads, head)
    grad_b = grad.astype(BF)
    grad_hidden = dot_tn(reduce_w, grad_b).astype(BF).astype(F32)
    grad_pre = (grad_hidden * slope).astype(BF)
    grad_two = dot(expand_w, grad_pre).astype(BF).astype(F32)
    grad_resid = grad + norm_back(grad_two, center_two, scale_two)
    grad_resid_b = grad_resid.astype(BF)
    grad_att = dot(proj_w, grad_resid_b)
    half = first_half((width, 128))
    tall_half = first_half((heads * 64, 128))
    across_f = across.astype(F32)
    grad_q, grad_k, grad_v = [], [], []
    grad_bias = jnp.zeros((heads * 64, 128), F32)
    for p in range(tokens // 128):
        lanes = slice(128 * p, 128 * p + 128)
        tall = tall_of(values[lanes], heads, over)
        wide = wide_of(keys[:, lanes], heads, across)
        p_f = prob[:, lanes]
        p_b = p_f.astype(BF)
        att = grad_att[:, lanes]
        att_b = att.astype(BF)
        zero = jnp.zeros_like(att)
        att_w = (jnp.where(half, att, zero).astype(BF), jnp.where(half, zero, att).astype(BF))
        query_f = query[:, lanes].astype(F32)
        query_w = (jnp.where(half, query_f, zero).astype(BF), jnp.where(half, zero, query_f).astype(BF))
        grad_prob = jnp.where(tall_half, dot(tall[0], att_b), dot(tall[1], att_b))
        grad_prob = grad_prob.astype(BF).astype(F32)
        along = jnp.sum((p_f * grad_prob).reshape(heads, 64, 128), axis=1, keepdims=True)
        grad_score = p_f * (grad_prob.reshape(heads, 64, 128) - along).reshape(heads * 64, 128)
        grad_bias = grad_bias + grad_score
        score_b = grad_score.astype(BF)
        grad_q.append(jnp.where(half, dot(wide[0], score_b), dot(wide[1], score_b)))
        for store, lhs, rhs in ((grad_k, query_w, score_b), (grad_v, att_w, p_b)):
            both = []
            for w in range(2):
                full = dot_nt(lhs[w], rhs) * across_f
                folded = sum(full[:, 128 * n : 128 * n + 128] for n in range(heads // 2))
                both.append(folded + pltpu.roll(folded, 64, 1))
            store.append(jnp.where(half, both[0], both[1]))
    grad_q = jnp.concatenate(grad_q, axis=1).astype(BF).astype(F32) * head ** (-0.5)
    grad_k = jnp.concatenate(grad_k, axis=1)
    grad_v = jnp.concatenate(grad_v, axis=1)
    grad_mixed = jnp.concatenate([grad_q, grad_k, grad_v], axis=0).astype(BF)
    grad_normed = dot(qkv_w, grad_mixed).astype(BF).astype(F32)
    grad_field = grad_resid + norm_back(grad_normed, center, scale)
    operands = (center.astype(BF), grad_mixed, attended, grad_resid_b, center_two.astype(BF), grad_pre, hidden, grad_b)
    return grad_field, operands, grad_bias


def pack_grads(operands, ahead, behind, buffer):
    normed, grad_mixed, attended, grad_resid, normed_two, grad_pre, hidden, grad = operands
    width = normed.shape[0]
    qkv = dot_nt(normed, grad_mixed)
    proj = dot_nt(attended, grad_resid)
    expand = dot_nt(normed_two, grad_pre)
    reduce = dot_nt(grad, hidden)
    inner = hidden.shape[0]
    at = 0

    def put(block):
        nonlocal at
        buffer[at : at + block.shape[0], :] = block.astype(BF)
        at += block.shape[0]

    full = 3 * width // 128
    for n in range(full):
        put(qkv[:, 128 * n : 128 * n + 128])
    put(jnp.concatenate([qkv[:, 128 * full :], proj[:, 128:]], axis=1))
    put(proj[:, :128])
    for one in (expand, reduce):
        for n in range(inner // 128):
            put(one[:, 128 * n : 128 * n + 128])
    heads = ahead.shape[0]
    put(jnp.concatenate([ahead, behind, jnp.zeros((16 - 2 * heads, 128), F32)], axis=0))
    rest = buffer.shape[0] - at
    if rest:
        put(jnp.zeros((rest, 128), F32))


def unpack_grads(buffer, outs, block, factor):
    qkv, proj, expand, reduce, table = outs
    width, inner = expand.shape[1:]
    heads, _, entries = table.shape
    at = 0

    def take(rows):
        nonlocal at
        piece = buffer[at : at + rows, :].astype(F32) * factor
        at += rows
        return piece

    full = 3 * width // 128
    for n in range(full):
        qkv[block, :, 128 * n : 128 * n + 128] = take(width)
    shared = take(width)
    qkv[block, :, 128 * full :] = shared[:, :64]
    proj[block, :, 128:] = shared[:, 64:]
    proj[block, :, :128] = take(width)
    for one in (expand, reduce):
        for n in range(inner // 128):
            one[block, :, 128 * n : 128 * n + 128] = take(width)
    vectors = buffer[at : at + 16, :]
    side = 2 * WIN - 1
    shape = (128, entries)
    rows, lanes = iota(shape, 0), iota(shape, 1)
    down, right = lanes // side - (WIN - 1), lanes % side - (WIN - 1)
    base = 8 * (down + 8) + right
    ahead = ((right >= 0) & (base == rows)).astype(F32).astype(BF)
    behind = ((right < 0) & (base + 8 == rows)).astype(F32).astype(BF)
    table[:, block, :] = (dot(vectors, ahead)[:heads] + dot(vectors, behind)[heads : 2 * heads]) * factor


def tokens_of(read):
    flat = [read(f, c).reshape(64, -1) for f in range(2) for c in range(2)]
    return jnp.concatenate(flat, axis=0).T


def tile_of(field, write):
    natural = field.T
    for f in range(2):
        for c in range(2):
            n = 64 * (2 * f + c)
            write(f, c, natural[n : n + 64].reshape(8, 8, -1))


def corners():
    return [(f, r, 16 * f + 4 * r) for f in range(2) for r in range(4)]


def plain_forward(x_far, cot_far, table_far, *refs):
    far, (first, top, left, corner, tight), near, done = refs[:4], refs[4:9], refs[9:17], refs[17]
    heads = table_far.shape[0]
    qkv_far, *rest = (there.at[0] for there in far)
    pairs = [(x_far, near[0]), (qkv_far, near[1]), *zip(rest, near[2:5], strict=True)]
    pairs[1:1] = [(table_far, near[7])]
    pairs.append((cot_far, near[5]))
    copies = [pltpu.make_async_copy(there, here, done.at[n]) for n, (there, here) in enumerate(pairs)]
    for copy in copies:
        copy.start()
    x_ref, table, qkv, proj, expand, reduce, cot = (
        Late(copy, here) for copy, (_, here) in zip(copies, pairs, strict=True)
    )
    whole = near[6]

    def write(f, c, piece):
        whole[f, :, 8 * c : 8 * c + 8, :] = piece

    bias = spread_bias(table[:, 0, :], heads)
    field = tokens_of(lambda f, c: x_ref[f, :, 8 * c : 8 * c + 8, :].astype(F32))
    resid, hidden, _, _, _ = forward((qkv, proj, expand), field, bias, heads)
    tile_of(resid + dot(reduce[...], hidden), write)
    first[...] = whole[:, SHIFT:]
    top[0] = whole[:, :SHIFT].astype(BF)
    top[1] = cot[:, :SHIFT]
    for f, r, n in corners():
        tight[n : n + 4, :] = whole[f, r, :4, :]
        tight[32 + n : 36 + n, :] = cot[f, r, :8, :].astype(F32)[:4]
        tight[64 + n : 68 + n, :] = whole[f, 4 + r, :4, :]
        tight[96 + n : 100 + n, :] = cot[f, 4 + r, :8, :].astype(F32)[:4]
    corner[...] = tight[:64].astype(BF)
    left[...] = tight[64:].astype(BF)


def keep_plain(n_row, n_col, x_ref, table, qkv, proj, expand, bias_out, slope_out, *outs):
    heads = table.shape[0]
    field = tokens_of(lambda f, c: x_ref[f, :, 8 * c : 8 * c + 8, :].astype(F32))
    _, _, pre, bell, saved = forward((qkv, proj, expand), field, spread_bias(table[:, 0, :], heads), heads)
    slope_out[...] = slope_of(pre, bell)
    for ref, value in zip(outs, saved, strict=True):
        ref[...] = value
    last_row = lax.axis_index("row") == n_row - 1
    last_col = lax.axis_index("col") == n_col - 1
    bias_out[...] = spread_bias(table[:, 1, :], heads) + shift_mask(bias_out.shape, last_row, last_col)


def shifted_block(
    first, cot, below, beside, across, bias, qkv, proj, expand, reduce,
    own, bottom, right, corner, keep, send, moved, turned, tight, buffer,
):
    heads = bias.shape[0] // 64
    moved[:, :4, :16, :] = first[...]
    moved[:, 4:, :16, :] = below[0].astype(F32)
    turned[:, :4, :16, :] = cot[:, 4:, :, :].astype(F32)
    turned[:, 4:, :16, :] = below[1].astype(F32)
    tight[:64] = across[...].astype(F32)
    tight[64:] = beside[...].astype(F32)
    for f, r, n in corners():
        moved[f, 4 + r, 16:20, :] = tight[n : n + 4, :]
        turned[f, 4 + r, 16:20, :] = tight[32 + n : 36 + n, :]
        moved[f, r, 16:20, :] = tight[64 + n : 68 + n, :]
        turned[f, r, 16:20, :] = tight[96 + n : 100 + n, :]
    field = tokens_of(lambda f, c: moved[f, :, 4 + 8 * c : 12 + 8 * c, :])
    cotangent = tokens_of(lambda f, c: turned[f, :, 4 + 8 * c : 12 + 8 * c, :])
    weights = (qkv, proj, expand, reduce)
    _, _, pre, bell, saved = forward(weights, field, bias[...], heads)
    grad_field, operands, grad_bias = backward(weights, saved, slope_of(pre, bell), cotangent, heads)

    def write(f, c, piece):
        moved[f, :, 4 + 8 * c : 12 + 8 * c, :] = piece

    tile_of(grad_field, write)
    own[...] = moved[:, :4, :16, :]
    bottom[...] = moved[:, 4:, :16, :].astype(BF)
    for f, r, n in corners():
        tight[n : n + 4, :] = moved[f, 4 + r, 16:20, :]
        tight[32 + n : 36 + n, :] = moved[f, r, 16:20, :]
    corner[...] = tight[:32].astype(BF)
    right[...] = tight[32:64].astype(BF)
    ahead, behind = fold_bias(grad_bias, heads)
    pack_grads(operands, ahead, behind, buffer)
    split_core(buffer, keep, send)


def split_core(buffer, keep, send):
    rows = keep.shape[0]
    core = lax.axis_index("row") % 2
    keep[...] = buffer[pl.ds(pl.multiple_of(core * rows, 16), rows), :]
    send[...] = buffer[pl.ds(pl.multiple_of((1 - core) * rows, 16), rows), :]


def plain_backward(own, above, beside, across, slope, *refs):
    saved, weights = refs[:10], refs[10:14]
    out, lines, outs, middle, tight = refs[14], refs[15], refs[16:21], refs[21], refs[22]
    heads = saved[5].shape[0] // 64
    middle[:, 4:] = own[...]
    middle[:, :4] = above[...].astype(F32)
    tight[:32] = across[...].astype(F32)
    tight[32:64] = beside[...].astype(F32)
    for f, r, n in corners():
        middle[f, r, :4, :] = tight[n : n + 4, :]
        middle[f, 4 + r, :4, :] = tight[32 + n : 36 + n, :]
    cotangent = tokens_of(lambda f, c: middle[f, :, 8 * c : 8 * c + 8, :])
    saved = tuple(ref[...] for ref in saved)
    grad_field, operands, grad_bias = backward(weights, saved, slope[...], cotangent, heads)

    def write(f, c, piece):
        out[f, :, 8 * c : 8 * c + 8, :] = piece

    tile_of(grad_field, write)
    lines[...] = grad_bias
    for ref, n in zip(outs, (0, 1, 3, 5, 7), strict=True):
        ref[...] = operands[n]


def plain_grads(normed, mixed, attended, resid, two, pre, hidden, grad, lines, mine, one, *refs):
    two_came, three_came, keep, send, done, buffer = refs
    kept = (normed, mixed, attended, resid, two, pre, hidden, grad)
    ahead, behind = fold_bias(lines[...], lines.shape[0] // 64)
    pack_grads(tuple(ref[...].astype(BF) for ref in kept), ahead, behind, buffer)
    split_core(buffer, keep, send)
    done[...] = mine[...] + one[...].astype(F32) + two_came[...].astype(F32) + three_came[...].astype(F32)


def near_place():
    return lax.axis_index("row") // 2 * 2 + lax.axis_index("col") % 2


def cut(total, me, own, sends, here=slice(None)):
    rows = total.shape[0] // (len(sends) + 1)
    own[here, :] = total[pl.ds(pl.multiple_of(me * rows, 16), rows), :]
    for d, send in enumerate(sends, 1):
        send[here, :] = total[pl.ds(pl.multiple_of((me ^ d) * rows, 16), rows), :].astype(BF)


def add_core(keep, came, own, *rest):
    sends, total = rest[:-1], rest[-1]
    total[...] = keep[...].astype(F32) + came[...].astype(F32)
    cut(total, near_place(), own, sends)


def add_near(count, mine, one, two, three, other, own, *rest):
    sends, total = rest[: count - 1], rest[-1]
    rows = own.shape[0] // 2
    place = lax.axis_index("col") // 2
    total[...] = mine[...] + one[...].astype(F32) + two[...].astype(F32) + three[...].astype(F32)
    cut(total, place, own, sends, slice(0, rows))
    cut(other, place, own, sends, slice(rows, 2 * rows))


def add_far(*refs):
    ins, out = refs[:-1], refs[-1]
    out[...] = (ins[0][...] + sum(one[...].astype(F32) for one in ins[1:])).astype(BF)


def join_far(*refs):
    ins, out = refs[:-1], refs[-1]
    rows, length = ins[0].shape[0] // 2, out.shape[0] // 2
    me = lax.axis_index("col") // 2
    for d, piece in enumerate(ins):
        for block in range(2):
            there = pl.multiple_of(block * length + (me ^ d) * rows, 16)
            out[pl.ds(there, rows), :] = piece[block * rows : block * rows + rows, :]


def finish(factor, *refs):
    ins, outs, buffer, done, stage = refs[:8], refs[8:13], refs[13], refs[14], refs[15:20]
    rows = ins[0].shape[0] // 2
    me = near_place()
    core = lax.axis_index("row") % 2
    copies = []
    for block in range(2):
        for n in range(8):
            where = (core ^ (n // 4)) * 4 + (me ^ (n % 4))
            piece = ins[n][block * rows : block * rows + rows, :]
            buffer[pl.ds(pl.multiple_of(where * rows, 16), rows), :] = piece
        unpack_grads(buffer, stage, block, factor)
        for n in range(4):
            copies.append(pltpu.make_async_copy(stage[n].at[block], outs[n].at[block], done.at[4 * block + n]))
            copies[-1].start()
    copies.append(pltpu.make_async_copy(stage[4], outs[4], done.at[8]))
    copies[-1].start()
    for copy in copies:
        copy.wait()


class Whole:
    def __init__(self, ref, block):
        self.ref, self.block = ref, block

    def __getitem__(self, index):
        return self.ref[self.block]


def call(kernel, outs, scratch, args, stacked=(), distant=(), micros=0.5, limit=LIMIT, far_outs=False):
    here, there = pl.BlockSpec(memory_space=pltpu.VMEM), pl.BlockSpec(memory_space=pltpu.HBM)
    count = len(args)

    def body(*refs):
        weights = [Whole(ref, block) for ref, (_, block) in zip(refs[count:], stacked)]
        kernel(*refs[:count], *weights, *refs[count + len(stacked) :])

    return pl.pallas_call(
        body,
        in_specs=[here] * (count + len(stacked)) + [there] * len(distant),
        out_specs=[there if far_outs else here] * len(outs),
        out_shape=[jax.ShapeDtypeStruct(s, d) for s, d in outs],
        scratch_shapes=[pltpu.VMEM(*one) if isinstance(one, tuple) else one for one in scratch],
        compiler_params=pltpu.CompilerParams(vmem_limit_bytes=limit),
        cost_estimate=pl.CostEstimate(flops=int(micros * 1.1e9), bytes_accessed=0, transcendentals=0),
    )(*args, *(arg for arg, _ in stacked), *distant)


def local(block_input, cotangent, qkv_weight, proj_weight, expand_weight, reduce_weight, bias_table):
    frames, rows, cols, width = block_input.shape
    n_row, n_col = lax.axis_size("row"), lax.axis_size("col")
    inner = expand_weight.shape[2]
    heads = bias_table.shape[1]
    tokens = frames * rows * cols
    wide = jnp.swapaxes(reduce_weight, 1, 2)
    weights = (qkv_weight, proj_weight, expand_weight, wide)
    table = jnp.swapaxes(bias_table, 0, 1)
    axes = ("row", "col")

    def send(block, down, right):
        route = [
            (r * n_col + c, (r + down) % n_row * n_col + (c + right) % n_col)
            for r in range(n_row)
            for c in range(n_col)
        ]
        return lax.ppermute(block, axes, route)

    def swap(block, row_bits, col_bits):
        route = [
            (r * n_col + c, (r ^ row_bits) * n_col + (c ^ col_bits)) for r in range(n_row) for c in range(n_col)
        ]
        return lax.ppermute(block, axes, route)

    far = n_col // 2
    unit = 8 * far * 16
    used = (4 * width + 2 * inner) * width // 128 + 16
    size = -(-used // unit) * unit
    chunk = size // (8 * far)
    halves = [((size // 2, 128), BF)] * 2
    buffer = ((size, 128), BF)
    tile = (frames, rows, cols, width)
    strip = (frames, SHIFT, cols, width)
    patches = frames * SHIFT * SHIFT
    tight = ((4 * patches, width), F32)
    lines = ((heads * 64, 128), F32)
    first, top, left, corner = call(
        plain_forward,
        [(strip, F32), ((2, *strip), BF), ((2 * patches, width), BF), ((2 * patches, width), BF)],
        [tight, (tile, BF), *((w.shape[1:], BF) for w in weights), (tile, BF), (tile, F32), (table.shape, F32), pltpu.SemaphoreType.DMA((7,))],
        [],
        distant=(block_input, cotangent, table, *weights),
        micros=2.3,
        limit=FULL,
    )
    halo = [send(top, -1, 0), send(left, 0, -1), send(corner, -1, -1)]
    bias, *kept = call(
        functools.partial(keep_plain, n_row, n_col),
        [
            lines,
            ((inner, tokens), F32),
            ((width, tokens), F32),
            ((1, tokens), F32),
            ((width, tokens), BF),
            ((width, tokens), BF),
            ((tokens, width), BF),
            ((heads * 64, tokens), F32),
            ((width, tokens), BF),
            ((width, tokens), F32),
            ((1, tokens), F32),
            ((inner, tokens), BF),
        ],
        [],
        [block_input, table],
        [(w, 0) for w in weights[:3]],
        micros=2.3,
    )
    own, bottom, right, corner, keep, away = call(
        shifted_block,
        [(strip, F32), (strip, BF), ((patches, width), BF), ((patches, width), BF), *halves],
        [((frames, rows, cols + 8, width), F32)] * 2 + [tight, buffer],
        [first, cotangent, *halo, bias],
        [(w, 1) for w in weights],
        micros=4.8,
    )
    back = [own, send(bottom, 1, 0), send(right, 0, 1), send(corner, 1, 1)]

    eighth, quarter, piece = (size // 8, 128), (size // 4, 128), (2 * chunk, 128)

    def near(own, *sends):
        return [own] + [swap(one, d & 2, d & 1) for d, one in enumerate(sends, 1)]

    quarters = [(eighth, F32)] + [(eighth, BF)] * 3
    summed = [((size // 2, 128), F32)]
    shifted = call(add_core, quarters, summed, [keep, swap(away, 1, 0)])
    kept[0], *shifted = lax.optimization_barrier((kept[0], *shifted))
    shifted = near(*shifted)
    operands = [((n, tokens), BF) for n in (width, 3 * width, width, inner, width)]
    input_grad, *given = call(
        plain_backward,
        [(tile, F32), lines, *operands],
        [(tile, F32), tight],
        [*back, *kept],
        [(w, 0) for w in weights],
        micros=3.2,
    )
    given = [given[1], given[2], kept[7], given[3], kept[8], given[4], kept[10], given[5], given[0]]
    keep, away, other = call(plain_grads, [*halves, (eighth, F32)], [buffer], [*given, *shifted])
    plain = call(add_core, quarters, summed, [keep, swap(away, 1, 0)])
    own, *sends = call(
        functools.partial(add_near, far),
        [(piece, F32)] + [(piece, BF)] * (far - 1),
        [(eighth, F32)],
        [*near(*plain), other],
    )
    distant = [own] + [swap(one, 0, 2 * d) for d, one in enumerate(sends, 1)]
    (done,) = call(add_far, [(piece, BF)], [], distant)
    distant = [done] + [swap(done, 0, 2 * d) for d in range(1, far)]
    (joined,) = call(join_far, [(quarter, BF)], [], distant)
    near = [joined] + [swap(joined, d & 2, d & 1) for d in range(1, 4)]
    near = near + [swap(one, 1, 0) for one in near]
    factor = 1.0 / math.sqrt(frames * rows * n_row * cols * n_col)
    shapes = [(w.shape, F32) for w in (*weights, table)]
    qkv, proj, expand, reduce, table = call(
        functools.partial(finish, factor), shapes, [buffer, pltpu.SemaphoreType.DMA((9,)), *shapes], near, far_outs=True
    )
    return input_grad, qkv, proj, expand, jnp.swapaxes(reduce, 1, 2), jnp.swapaxes(table, 0, 1)


def solution(mesh):
    in_specs = (P(None, "row", "col", None), P(None, "row", "col", None), P(), P(), P(), P(), P())
    out_specs = (P(None, "row", "col", None), P(), P(), P(), P(), P())
    return jax.shard_map(local, mesh=mesh, in_specs=in_specs, out_specs=out_specs, check_vma=False)
```

time: 104 us -> 76.7 us (0.74)
  starting transfers between devices: 46.1 us -> 29.6 us
  waiting for transfers between devices: 36.7 us -> 27.7 us
  local copies, waits for them, and re-layouts: 5.04 us -> 0.03 us
  Pallas kernels: 15.1 us -> 18.2 us
    ppermute x34 -> x21, starting transfers between devices: 31.6 us -> 19.3 us  [swap(): return lax.ppermute(block, axes, route)]
    ppermute x9 -> x6, waiting for transfers between devices: 10.1 us -> 4.23 us  [send(): return lax.ppermute(block, axes, route)]
    unnamed x16, local copies, waits for them, and re-layouts: 5.04 us -> 0.03 us
    ppermute x9 -> x6, starting transfers between devices: 14.5 us -> 10.3 us  [send(): return lax.ppermute(block, axes, route)]
    ppermute x34 -> x21, waiting for transfers between devices: 26.6 us -> 23.5 us  [swap(): return lax.ppermute(block, axes, route)]
    pallas_call x13 -> x11, Pallas kernels: 15.1 us -> 18.2 us  [call(): pl.pallas_call(body, in_specs=[here] * (count + len(stacked)) + [there] *...]
  transfers between devices with their start and end apart: 43 -> 27, of which waited for: 17 -> 16; matrix products, arithmetic and copies ran while one was open for 2% -> 0% of each run, Pallas kernels for 8% -> 7%
where the time goes in v2:
time: 76.7 us; the launch traced here: 76.5 us
  starting transfers between devices  29.6 us (39%)
  waiting for transfers between devices  27.7 us (36%)
  Pallas kernels  18.2 us (24%)
  between operations  0.95 us (1%)
    ppermute x21, waiting for transfers between devices, swap(): return lax.ppermute(block, axes, route)  23.5 us
    ppermute x21, starting transfers between devices, swap(): return lax.ppermute(block, axes, route)  19.3 us
    pallas_call x11, Pallas kernels, call(): pl.pallas_call(body, in_specs=[here] * (count + len(stacked)) + [there] *...  18.2 us
    ppermute x6, starting transfers between devices, send(): return lax.ppermute(block, axes, route)  10.3 us
    ppermute x6, waiting for transfers between devices, send(): return lax.ppermute(block, axes, route)  4.23 us
  transfers between devices with their start and end apart: 27, of which 16 were waited for; matrix products, arithmetic and copies ran while one was open for 0% of the time, Pallas kernels for 7%

profile of v2, /device:TPU:0, one launch (start us, length us, event | category | flops | bytes accessed | tf_op | source)
XLA Modules:
  0.0 76.5 jit_solution(11797676274785415379)
XLA Ops:
  0.7 4.8 %shard_map.118 = (f32[2,4,16,192]{3,2,1,0:T(8,128)}, bf16[2,2,4,16,192]{4,3,2,1,0:T(8,128)(2,1)}, bf16[64,192]{1,0:T(8,128)(2,1)}, bf16[64,192]{1,0:T(8,128)(2,1)}) custom-call(bf16[2,8,16,192]{3,2,1,0:T(8,128)(2,1)} %refs_0_.3, bf16[2,8,16,192]{3,2,1,0:T(8,128)(2,1)} %refs_1_.3, f32[6,2,225]{2,1,0:T(2,128)} %bitcast.7, bf16[2,192,576]{2,1,0:T(8,128)(2,1)} %refs_15_.1, ...), custom_call_target="tpu_custom_call" | custom-call | flops 2529999872 | tf_op jit(solution)/shard_map/pallas_call | solution.py:528
  5.5 6.1 %collective-permute-start.1 = (bf16[64,192]{1,0:T(8,128)(2,1)}, bf16[64,192]{1,0:T(8,128)(2,1)S(1)}, u32[]{:S(2)}, u32[]{:S(2)}) collective-permute-start(bf16[64,192]{1,0:T(8,128)(2,1)} %get-tuple-element.62), channel_id=1, source_target_pairs={{0,7},{1,0},{2,1},{3,2},{4,3},{5,4},{6,5},{7,6},{8,15},{9,8},{10,9... | collective-permute-start | bytes 73736 | tf_op jit(solution)/shard_map/ppermute | solution.py:556
  12.1 1.1 %collective-permute-start = (bf16[2,2,4,16,192]{4,3,2,1,0:T(8,128)(2,1)}, bf16[2,2,4,16,192]{4,3,2,1,0:T(8,128)(2,1)S(1)}, u32[]{:S(2)}, u32[]{:S(2)}) collective-permute-start(bf16[2,2,4,16,192]{4,3,2,1,0:T(8,128)(2,1)} %get-tuple-element.61), channel_id=1, source_target_pairs={{0,24},{1,25},{2,26},{3,27},{4,28},{5,29},{6,30},{7,31},{8,0},{9,1... | collective-permute-start | bytes 294920 | tf_op jit(solution)/shard_map/ppermute | solution.py:556
  13.3 2.3 %shard_map.119 = (f32[384,128]{1,0:T(8,128)S(1)}, f32[768,256]{1,0:T(8,128)S(1)}, f32[192,256]{1,0:T(8,128)S(1)}, f32[1,256]{1,0:T(1,128)S(1)}, bf16[192,256]{1,...) custom-call(bf16[2,8,16,192]{3,2,1,0:T(8,128)(2,1)S(1)} %copy-done.4, ...), custom_call_target="tpu_custom_call" | custom-call | flops 2529999872 | tf_op jit(solution)/shard_map/pallas_call | solution.py:528
  16.1 4.5 %shard_map.120 = (f32[2,4,16,192]{3,2,1,0:T(8,128)S(1)}, bf16[2,4,16,192]{3,2,1,0:T(8,128)(2,1)S(1)}, bf16[32,192]{1,0:T(8,128)(2,1)S(1)}, bf16[32,192]{1,0:T(8,...) custom-call(f32[2,4,16,192]{3,2,1,0:T(8,128)S(1)} %copy-done.7, ...), custom_call_target="tpu_custom_call" | custom-call | flops 5280000000 | tf_op jit(solution)/shard_map/pallas_call | solution.py:528
  20.6 0.7 collective-permute-start.6
  21.4 1.5 %collective-permute-start.4 = (bf16[32,192]{1,0:T(8,128)(2,1)S(1)}, bf16[32,192]{1,0:T(8,128)(2,1)S(1)}, u32[]{:S(2)}, u32[]{:S(2)}) collective-permute-start(bf16[32,192]{1,0:T(8,128)(2,1)S(1)} %get-tuple-element.67), channel_id=1, source_target_pairs={{0,1},{1,2},{2,3},{3,4},{4,5},{5,6},{6,7},{7,0},{8,9},{9,10},{10,1... | collective-permute-start | bytes 36872 | tf_op jit(solution)/shard_map/ppermute | solution.py:556
  22.9 1.0 %collective-permute-start.3 = (bf16[2,4,16,192]{3,2,1,0:T(8,128)(2,1)S(1)}, bf16[2,4,16,192]{3,2,1,0:T(8,128)(2,1)S(1)}, u32[]{:S(2)}, u32[]{:S(2)}) collective-permute-start(bf16[2,4,16,192]{3,2,1,0:T(8,128)(2,1)S(1)} %get-tuple-element.66), channel_id=1, source_target_pairs={{0,8},{1,9},{2,10},{3,11},{4,12},{5,13},{6,14},{7,15},{8,16},{9,17... | collective-permute-start | bytes 147464 | tf_op jit(solution)/shard_map/ppermute | solution.py:556
  24.6 1.5 %collective-permute-start.8 = (bf16[448,128]{1,0:T(8,128)(2,1)S(1)}, bf16[448,128]{1,0:T(8,128)(2,1)S(1)}, u32[]{:S(2)}, u32[]{:S(2)}) collective-permute-start(bf16[448,128]{1,0:T(8,128)(2,1)S(1)} %get-tuple-element.96), channel_id=1, source_target_pairs={{0,16},{1,17},{2,18},{3,19},{4,20},{5,21},{6,22},{7,23},{8,24},{9,... | collective-permute-start | bytes 344072 | tf_op jit(solution)/shard_map/ppermute | solution.py:562
  26.1 1.8 %collective-permute-done.4.refs_2_ = bf16[32,192]{1,0:T(8,128)(2,1)S(1)} collective-permute-done((bf16[32,192]{1,0:T(8,128)(2,1)S(1)}, bf16[32,192]{1,0:T(8,128)(2,1)S(1)}, u32[]{:S(2)}, u32[]{:S(2)}) %collective-permute-start.4) | collective-permute-done | bytes 12320 | tf_op jit(solution)/shard_map/ppermute | solution.py:556
  27.9 1.9 %collective-permute-done.5.refs_3_ = bf16[32,192]{1,0:T(8,128)(2,1)S(1)} collective-permute-done((bf16[32,192]{1,0:T(8,128)(2,1)S(1)}, bf16[32,192]{1,0:T(8,128)(2,1)S(1)}, u32[]{:S(2)}, u32[]{:S(2)}) %collective-permute-start.5) | collective-permute-done | bytes 12320 | tf_op jit(solution)/shard_map/ppermute | solution.py:556
  29.8 3.1 %shard_map.122 = (f32[2,8,16,192]{3,2,1,0:T(8,128)}, f32[384,128]{1,0:T(8,128)S(1)}, bf16[192,256]{1,0:T(8,128)(2,1)S(1)}, bf16[576,256]{1,0:T(8,128)(2,1)S(1)},...) custom-call(f32[2,4,16,192]{3,2,1,0:T(8,128)S(1)} %get-tuple-element.65.refs_0_, ...), custom_call_target="tpu_custom_call" | custom-call | flops 3520000000 | tf_op jit(solution)/shard_map/pallas_call | solution.py:528
  33.6 0.7 shard_map.123
  34.5 1.8 %collective-permute-done.10.refs_1_ = bf16[1792,128]{1,0:T(8,128)(2,1)S(1)} collective-permute-done((bf16[1792,128]{1,0:T(8,128)(2,1)S(1)}, bf16[1792,128]{1,0:T(8,128)(2,1)S(1)}, u32[]{:S(2)}, u32[]{:S(2)}) %collective-permute-start.10) | collective-permute-done | bytes 458784 | tf_op jit(solution)/shard_map/ppermute | solution.py:562
  36.9 1.2 %collective-permute-start.12 = (bf16[448,128]{1,0:T(8,128)(2,1)S(1)}, bf16[448,128]{1,0:T(8,128)(2,1)S(1)}, u32[]{:S(2)}, u32[]{:S(2)}) collective-permute-start(bf16[448,128]{1,0:T(8,128)(2,1)S(1)} %get-tuple-element.102), channel_id=1, source_target_pairs={{0,16},{1,17},{2,18},{3,19},{4,20},{5,21},{6,22},{7,23},{8,24},{9,... | collective-permute-start | bytes 344072 | tf_op jit(solution)/shard_map/ppermute | solution.py:562
  38.1 1.9 %collective-permute-start.13 = (bf16[448,128]{1,0:T(8,128)(2,1)S(1)}, bf16[448,128]{1,0:T(8,128)(2,1)S(1)}, u32[]{:S(2)}, u32[]{:S(2)}) collective-permute-start(bf16[448,128]{1,0:T(8,128)(2,1)S(1)} %get-tuple-element.103), channel_id=1, source_target_pairs={{0,17},{1,16},{2,19},{3,18},{4,21},{5,20},{6,23},{7,22},{8,25},{9,... | collective-permute-start | bytes 344072 | tf_op jit(solution)/shard_map/ppermute | solution.py:562
  40.0 1.7 %collective-permute-done.11.refs_1_ = bf16[448,128]{1,0:T(8,128)(2,1)S(1)} collective-permute-done((bf16[448,128]{1,0:T(8,128)(2,1)S(1)}, bf16[448,128]{1,0:T(8,128)(2,1)S(1)}, u32[]{:S(2)}, u32[]{:S(2)}) %collective-permute-start.11) | collective-permute-done | bytes 114720 | tf_op jit(solution)/shard_map/ppermute | solution.py:562
  42.0 3.3 %collective-permute-done.13.refs_3_ = bf16[448,128]{1,0:T(8,128)(2,1)S(1)} collective-permute-done((bf16[448,128]{1,0:T(8,128)(2,1)S(1)}, bf16[448,128]{1,0:T(8,128)(2,1)S(1)}, u32[]{:S(2)}, u32[]{:S(2)}) %collective-permute-start.13) | collective-permute-done | bytes 114720 | tf_op jit(solution)/shard_map/ppermute | solution.py:562
  45.5 3.6 %collective-permute-start.15 = (bf16[224,128]{1,0:T(8,128)(2,1)S(1)}, bf16[224,128]{1,0:T(8,128)(2,1)S(1)}, u32[]{:S(2)}, u32[]{:S(2)}) collective-permute-start(bf16[224,128]{1,0:T(8,128)(2,1)S(1)} %get-tuple-element.107), channel_id=1, source_target_pairs={{0,4},{1,5},{2,6},{3,7},{4,0},{5,1},{6,2},{7,3},{8,12},{9,13},{10,... | collective-permute-start | bytes 172040 | tf_op jit(solution)/shard_map/ppermute | solution.py:562
  49.1 0.8 %collective-permute-start.16 = (bf16[224,128]{1,0:T(8,128)(2,1)S(1)}, bf16[224,128]{1,0:T(8,128)(2,1)S(1)}, u32[]{:S(2)}, u32[]{:S(2)}) collective-permute-start(bf16[224,128]{1,0:T(8,128)(2,1)S(1)} %get-tuple-element.108), channel_id=1, source_target_pairs={{0,6},{1,7},{2,4},{3,5},{4,2},{5,3},{6,0},{7,1},{8,14},{9,15},{10,... | collective-permute-start | bytes 172040 | tf_op jit(solution)/shard_map/ppermute | solution.py:562
  49.9 1.4 %collective-permute-done.15.refs_2_ = bf16[224,128]{1,0:T(8,128)(2,1)S(1)} collective-permute-done((bf16[224,128]{1,0:T(8,128)(2,1)S(1)}, bf16[224,128]{1,0:T(8,128)(2,1)S(1)}, u32[]{:S(2)}, u32[]{:S(2)}) %collective-permute-start.15) | collective-permute-done | bytes 57376 | tf_op jit(solution)/shard_map/ppermute | solution.py:562
  51.3 3.8 %collective-permute-done.16.refs_3_ = bf16[224,128]{1,0:T(8,128)(2,1)S(1)} collective-permute-done((bf16[224,128]{1,0:T(8,128)(2,1)S(1)}, bf16[224,128]{1,0:T(8,128)(2,1)S(1)}, u32[]{:S(2)}, u32[]{:S(2)}) %collective-permute-start.16) | collective-permute-done | bytes 57376 | tf_op jit(solution)/shard_map/ppermute | solution.py:562
  55.1 0.9 %collective-permute-start.19 = (bf16[224,128]{1,0:T(8,128)(2,1)S(1)}, bf16[224,128]{1,0:T(8,128)(2,1)S(1)}, u32[]{:S(2)}, u32[]{:S(2)}) collective-permute-start(bf16[224,128]{1,0:T(8,128)(2,1)S(1)} %shard_map.126.refs_0_), channel_id=1, source_target_pairs={{0,6},{1,7},{2,4},{3,5},{4,2},{5,3},{6,0},{7,1},{8,14},{9,15},{10,... | collective-permute-start | bytes 172040 | tf_op jit(solution)/shard_map/ppermute | solution.py:562
  56.0 3.5 %collective-permute-start.17 = (bf16[224,128]{1,0:T(8,128)(2,1)S(1)}, bf16[224,128]{1,0:T(8,128)(2,1)S(1)}, u32[]{:S(2)}, u32[]{:S(2)}) collective-permute-start(bf16[224,128]{1,0:T(8,128)(2,1)S(1)} %shard_map.126.refs_0_), channel_id=1, source_target_pairs={{0,2},{1,3},{2,0},{3,1},{4,6},{5,7},{6,4},{7,5},{8,10},{9,11},{10,... | collective-permute-start | bytes 172040 | tf_op jit(solution)/shard_map/ppermute | solution.py:562
  59.6 1.7 %collective-permute-done.19.refs_3_ = bf16[224,128]{1,0:T(8,128)(2,1)S(1)} collective-permute-done((bf16[224,128]{1,0:T(8,128)(2,1)S(1)}, bf16[224,128]{1,0:T(8,128)(2,1)S(1)}, u32[]{:S(2)}, u32[]{:S(2)}) %collective-permute-start.19) | collective-permute-done | bytes 57376 | tf_op jit(solution)/shard_map/ppermute | solution.py:562
  61.3 1.1 %collective-permute-done.18.refs_2_ = bf16[224,128]{1,0:T(8,128)(2,1)S(1)} collective-permute-done((bf16[224,128]{1,0:T(8,128)(2,1)S(1)}, bf16[224,128]{1,0:T(8,128)(2,1)S(1)}, u32[]{:S(2)}, u32[]{:S(2)}) %collective-permute-start.18) | collective-permute-done | bytes 57376 | tf_op jit(solution)/shard_map/ppermute | solution.py:562
  62.4 1.4 %collective-permute-start.22 = (bf16[896,128]{1,0:T(8,128)(2,1)S(1)}, bf16[896,128]{1,0:T(8,128)(2,1)S(1)}, u32[]{:S(2)}, u32[]{:S(2)}) collective-permute-start(bf16[896,128]{1,0:T(8,128)(2,1)S(1)} %shard_map.127.refs_0_), channel_id=1, source_target_pairs={{0,17},{1,16},{2,19},{3,18},{4,21},{5,20},{6,23},{7,22},{8,25},{9,... | collective-permute-start | bytes 688136 | tf_op jit(solution)/shard_map/ppermute | solution.py:562
  63.8 1.5 %collective-permute-start.21 = (bf16[896,128]{1,0:T(8,128)(2,1)S(1)}, bf16[896,128]{1,0:T(8,128)(2,1)S(1)}, u32[]{:S(2)}, u32[]{:S(2)}) collective-permute-start(bf16[896,128]{1,0:T(8,128)(2,1)S(1)} %shard_map.127.refs_0_), channel_id=1, source_target_pairs={{0,16},{1,17},{2,18},{3,19},{4,20},{5,21},{6,22},{7,23},{8,24},{9,... | collective-permute-start | bytes 688136 | tf_op jit(solution)/shard_map/ppermute | solution.py:562
  65.9 3.8 %collective-permute-done.22.refs_3_ = bf16[896,128]{1,0:T(8,128)(2,1)S(1)} collective-permute-done((bf16[896,128]{1,0:T(8,128)(2,1)S(1)}, bf16[896,128]{1,0:T(8,128)(2,1)S(1)}, u32[]{:S(2)}, u32[]{:S(2)}) %collective-permute-start.22) | collective-permute-done | bytes 229408 | tf_op jit(solution)/shard_map/ppermute | solution.py:562
  69.7 2.6 %collective-permute-done.21.refs_2_ = bf16[896,128]{1,0:T(8,128)(2,1)S(1)} collective-permute-done((bf16[896,128]{1,0:T(8,128)(2,1)S(1)}, bf16[896,128]{1,0:T(8,128)(2,1)S(1)}, u32[]{:S(2)}, u32[]{:S(2)}) %collective-permute-start.21) | collective-permute-done | bytes 229408 | tf_op jit(solution)/shard_map/ppermute | solution.py:562
  72.9 1.0 %collective-permute-done.25.refs_6_ = bf16[896,128]{1,0:T(8,128)(2,1)S(1)} collective-permute-done((bf16[896,128]{1,0:T(8,128)(2,1)S(1)}, bf16[896,128]{1,0:T(8,128)(2,1)S(1)}, u32[]{:S(2)}, u32[]{:S(2)}) %collective-permute-start.25) | collective-permute-done | bytes 229408 | tf_op jit(solution)/shard_map/ppermute | solution.py:562
  74.2 2.2 %shard_map.128 = (f32[2,192,576]{2,1,0:T(8,128)}, f32[2,192,192]{2,1,0:T(8,128)}, f32[2,192,768]{2,1,0:T(8,128)}, f32[2,192,768]{2,1,0:T(8,128)}, f32[6,2,225]{2,1,0:T(2,128)}) custom-call(bf16[896,128]{1,0:T(8,128)(2,1)S(1)} %shard_map.127.refs_0_, bf16[896,128]{1,0:T(8,128)(2,1)S(1)} %collective-permute-done.20.refs_1_, ...), custom_call_target="tpu_custom_call" | custom-call | flops 550000000 | tf_op jit(solution)/shard_map/pallas_call | solution.py:528
  (49 shorter events, 5.2 us)
Async XLA Ops:
  0.6 12.6 %copy-start = (bf16[2,192,768]{2,1,0:T(8,128)(2,1)S(1)}, bf16[2,192,768]{2,1,0:T(8,128)(2,1)}, u32[]{:S(2)}) copy-start(bf16[2,192,768]{2,1,0:T(8,128)(2,1)} %refs_17_.1) | copy-start | bytes 1769476
  0.6 12.6 %copy-start.2 = (bf16[2,192,576]{2,1,0:T(8,128)(2,1)S(1)}, bf16[2,192,576]{2,1,0:T(8,128)(2,1)}, u32[]{:S(2)}) copy-start(bf16[2,192,576]{2,1,0:T(8,128)(2,1)} %refs_15_.1) | copy-start | bytes 1327108
  0.7 12.6 %copy-start.3 = (bf16[2,192,192]{2,1,0:T(8,128)(2,1)S(1)}, bf16[2,192,192]{2,1,0:T(8,128)(2,1)}, u32[]{:S(2)}) copy-start(bf16[2,192,192]{2,1,0:T(8,128)(2,1)} %refs_16_.1) | copy-start | bytes 442372
  0.7 12.6 %copy-start.4 = (bf16[2,8,16,192]{3,2,1,0:T(8,128)(2,1)S(1)}, bf16[2,8,16,192]{3,2,1,0:T(8,128)(2,1)}, u32[]{:S(2)}) copy-start(bf16[2,8,16,192]{3,2,1,0:T(8,128)(2,1)} %refs_0_.3) | copy-start | bytes 294916
  0.7 12.6 %copy-start.6 = (f32[2,6,225]{2,0,1:T(2,128)S(1)}, f32[2,6,225]{2,0,1:T(2,128)}, u32[]{:S(2)}) copy-start(f32[2,6,225]{2,0,1:T(2,128)} %param.13) | copy-start | bytes 32404
  5.5 10.1 %collective-permute-start.1 = (bf16[64,192]{1,0:T(8,128)(2,1)}, bf16[64,192]{1,0:T(8,128)(2,1)S(1)}, u32[]{:S(2)}, u32[]{:S(2)}) collective-permute-start(bf16[64,192]{1,0:T(8,128)(2,1)} %get-tuple-element.62), channel_id=1, source_target_pairs={{0,7},{1,0},{2,1},{3,2},{4,3},{5,4},{6,5},{7,6},{8,15},{9,8},{10,9... | collective-permute-start | bytes 73736 | tf_op jit(solution)/shard_map/ppermute | solution.py:556
  11.5 4.1 %collective-permute-start.2 = (bf16[64,192]{1,0:T(8,128)(2,1)}, bf16[64,192]{1,0:T(8,128)(2,1)S(1)}, u32[]{:S(2)}, u32[]{:S(2)}) collective-permute-start(bf16[64,192]{1,0:T(8,128)(2,1)} %get-tuple-element.63), channel_id=1, source_target_pairs={{0,31},{1,24},{2,25},{3,26},{4,27},{5,28},{6,29},{7,30},{8,7},{9,0... | collective-permute-start | bytes 73736 | tf_op jit(solution)/shard_map/ppermute | solution.py:556
  12.1 4.0 %collective-permute-start = (bf16[2,2,4,16,192]{4,3,2,1,0:T(8,128)(2,1)}, bf16[2,2,4,16,192]{4,3,2,1,0:T(8,128)(2,1)S(1)}, u32[]{:S(2)}, u32[]{:S(2)}) collective-permute-start(bf16[2,2,4,16,192]{4,3,2,1,0:T(8,128)(2,1)} %get-tuple-element.61), channel_id=1, source_target_pairs={{0,24},{1,25},{2,26},{3,27},{4,28},{5,29},{6,30},{7,31},{8,0},{9,1... | collective-permute-start | bytes 294920 | tf_op jit(solution)/shard_map/ppermute | solution.py:556
  20.6 3.3 %collective-permute-start.6 = (bf16[1792,128]{1,0:T(8,128)(2,1)S(1)}, bf16[1792,128]{1,0:T(8,128)(2,1)S(1)}, u32[]{:S(2)}, u32[]{:S(2)}) collective-permute-start(bf16[1792,128]{1,0:T(8,128)(2,1)S(1)} %get-tuple-element.71), channel_id=1, source_target_pairs={{0,8},{1,9},{2,10},{3,11},{4,12},{5,13},{6,14},{7,15},{8,0},{9,1},... | collective-permute-start | bytes 1376264 | tf_op jit(solution)/shard_map/ppermute | solution.py:562
  21.4 6.5 %collective-permute-start.4 = (bf16[32,192]{1,0:T(8,128)(2,1)S(1)}, bf16[32,192]{1,0:T(8,128)(2,1)S(1)}, u32[]{:S(2)}, u32[]{:S(2)}) collective-permute-start(bf16[32,192]{1,0:T(8,128)(2,1)S(1)} %get-tuple-element.67), channel_id=1, source_target_pairs={{0,1},{1,2},{2,3},{3,4},{4,5},{5,6},{6,7},{7,0},{8,9},{9,10},{10,1... | collective-permute-start | bytes 36872 | tf_op jit(solution)/shard_map/ppermute | solution.py:556
  22.9 6.9 %collective-permute-start.5 = (bf16[32,192]{1,0:T(8,128)(2,1)S(1)}, bf16[32,192]{1,0:T(8,128)(2,1)S(1)}, u32[]{:S(2)}, u32[]{:S(2)}) collective-permute-start(bf16[32,192]{1,0:T(8,128)(2,1)S(1)} %get-tuple-element.68), channel_id=1, source_target_pairs={{0,9},{1,10},{2,11},{3,12},{4,13},{5,14},{6,15},{7,8},{8,17},{9,18... | collective-permute-start | bytes 36872 | tf_op jit(solution)/shard_map/ppermute | solution.py:556
  22.9 6.9 %collective-permute-start.3 = (bf16[2,4,16,192]{3,2,1,0:T(8,128)(2,1)S(1)}, bf16[2,4,16,192]{3,2,1,0:T(8,128)(2,1)S(1)}, u32[]{:S(2)}, u32[]{:S(2)}) collective-permute-start(bf16[2,4,16,192]{3,2,1,0:T(8,128)(2,1)S(1)} %get-tuple-element.66), channel_id=1, source_target_pairs={{0,8},{1,9},{2,10},{3,11},{4,12},{5,13},{6,14},{7,15},{8,16},{9,17... | collective-permute-start | bytes 147464 | tf_op jit(solution)/shard_map/ppermute | solution.py:556
  24.1 8.8 %collective-permute-start.7 = (bf16[448,128]{1,0:T(8,128)(2,1)S(1)}, bf16[448,128]{1,0:T(8,128)(2,1)S(1)}, u32[]{:S(2)}, u32[]{:S(2)}) collective-permute-start(bf16[448,128]{1,0:T(8,128)(2,1)S(1)} %get-tuple-element.95), channel_id=1, source_target_pairs={{0,1},{1,0},{2,3},{3,2},{4,5},{5,4},{6,7},{7,6},{8,9},{9,8},{10,11... | collective-permute-start | bytes 344072 | tf_op jit(solution)/shard_map/ppermute | solution.py:562
  24.6 8.4 %collective-permute-start.8 = (bf16[448,128]{1,0:T(8,128)(2,1)S(1)}, bf16[448,128]{1,0:T(8,128)(2,1)S(1)}, u32[]{:S(2)}, u32[]{:S(2)}) collective-permute-start(bf16[448,128]{1,0:T(8,128)(2,1)S(1)} %get-tuple-element.96), channel_id=1, source_target_pairs={{0,16},{1,17},{2,18},{3,19},{4,20},{5,21},{6,22},{7,23},{8,24},{9,... | collective-permute-start | bytes 344072 | tf_op jit(solution)/shard_map/ppermute | solution.py:562
  27.9 5.7 %collective-permute-start.9 = (bf16[448,128]{1,0:T(8,128)(2,1)S(1)}, bf16[448,128]{1,0:T(8,128)(2,1)S(1)}, u32[]{:S(2)}, u32[]{:S(2)}) collective-permute-start(bf16[448,128]{1,0:T(8,128)(2,1)S(1)} %get-tuple-element.97), channel_id=1, source_target_pairs={{0,17},{1,16},{2,19},{3,18},{4,21},{5,20},{6,23},{7,22},{8,25},{9,... | collective-permute-start | bytes 344072 | tf_op jit(solution)/shard_map/ppermute | solution.py:562
  34.4 1.9 %collective-permute-start.10 = (bf16[1792,128]{1,0:T(8,128)(2,1)S(1)}, bf16[1792,128]{1,0:T(8,128)(2,1)S(1)}, u32[]{:S(2)}, u32[]{:S(2)}) collective-permute-start(bf16[1792,128]{1,0:T(8,128)(2,1)S(1)} %get-tuple-element.99), channel_id=1, source_target_pairs={{0,8},{1,9},{2,10},{3,11},{4,12},{5,13},{6,14},{7,15},{8,0},{9,1},... | collective-permute-start | bytes 1376264 | tf_op jit(solution)/shard_map/ppermute | solution.py:562
  36.5 5.3 %collective-permute-start.11 = (bf16[448,128]{1,0:T(8,128)(2,1)S(1)}, bf16[448,128]{1,0:T(8,128)(2,1)S(1)}, u32[]{:S(2)}, u32[]{:S(2)}) collective-permute-start(bf16[448,128]{1,0:T(8,128)(2,1)S(1)} %get-tuple-element.101), channel_id=1, source_target_pairs={{0,1},{1,0},{2,3},{3,2},{4,5},{5,4},{6,7},{7,6},{8,9},{9,8},{10,11... | collective-permute-start | bytes 344072 | tf_op jit(solution)/shard_map/ppermute | solution.py:562
  36.9 5.1 %collective-permute-start.12 = (bf16[448,128]{1,0:T(8,128)(2,1)S(1)}, bf16[448,128]{1,0:T(8,128)(2,1)S(1)}, u32[]{:S(2)}, u32[]{:S(2)}) collective-permute-start(bf16[448,128]{1,0:T(8,128)(2,1)S(1)} %get-tuple-element.102), channel_id=1, source_target_pairs={{0,16},{1,17},{2,18},{3,19},{4,20},{5,21},{6,22},{7,23},{8,24},{9,... | collective-permute-start | bytes 344072 | tf_op jit(solution)/shard_map/ppermute | solution.py:562
  38.1 7.3 %collective-permute-start.13 = (bf16[448,128]{1,0:T(8,128)(2,1)S(1)}, bf16[448,128]{1,0:T(8,128)(2,1)S(1)}, u32[]{:S(2)}, u32[]{:S(2)}) collective-permute-start(bf16[448,128]{1,0:T(8,128)(2,1)S(1)} %get-tuple-element.103), channel_id=1, source_target_pairs={{0,17},{1,16},{2,19},{3,18},{4,21},{5,20},{6,23},{7,22},{8,25},{9,... | collective-permute-start | bytes 344072 | tf_op jit(solution)/shard_map/ppermute | solution.py:562
  45.4 4.5 %collective-permute-start.14 = (bf16[224,128]{1,0:T(8,128)(2,1)S(1)}, bf16[224,128]{1,0:T(8,128)(2,1)S(1)}, u32[]{:S(2)}, u32[]{:S(2)}) collective-permute-start(bf16[224,128]{1,0:T(8,128)(2,1)S(1)} %get-tuple-element.106), channel_id=1, source_target_pairs={{0,2},{1,3},{2,0},{3,1},{4,6},{5,7},{6,4},{7,5},{8,10},{9,11},{10,... | collective-permute-start | bytes 172040 | tf_op jit(solution)/shard_map/ppermute | solution.py:562
  45.5 5.7 %collective-permute-start.15 = (bf16[224,128]{1,0:T(8,128)(2,1)S(1)}, bf16[224,128]{1,0:T(8,128)(2,1)S(1)}, u32[]{:S(2)}, u32[]{:S(2)}) collective-permute-start(bf16[224,128]{1,0:T(8,128)(2,1)S(1)} %get-tuple-element.107), channel_id=1, source_target_pairs={{0,4},{1,5},{2,6},{3,7},{4,0},{5,1},{6,2},{7,3},{8,12},{9,13},{10,... | collective-permute-start | bytes 172040 | tf_op jit(solution)/shard_map/ppermute | solution.py:562
  49.1 6.0 %collective-permute-start.16 = (bf16[224,128]{1,0:T(8,128)(2,1)S(1)}, bf16[224,128]{1,0:T(8,128)(2,1)S(1)}, u32[]{:S(2)}, u32[]{:S(2)}) collective-permute-start(bf16[224,128]{1,0:T(8,128)(2,1)S(1)} %get-tuple-element.108), channel_id=1, source_target_pairs={{0,6},{1,7},{2,4},{3,5},{4,2},{5,3},{6,0},{7,1},{8,14},{9,15},{10,... | collective-permute-start | bytes 172040 | tf_op jit(solution)/shard_map/ppermute | solution.py:562
  55.1 6.2 %collective-permute-start.19 = (bf16[224,128]{1,0:T(8,128)(2,1)S(1)}, bf16[224,128]{1,0:T(8,128)(2,1)S(1)}, u32[]{:S(2)}, u32[]{:S(2)}) collective-permute-start(bf16[224,128]{1,0:T(8,128)(2,1)S(1)} %shard_map.126.refs_0_), channel_id=1, source_target_pairs={{0,6},{1,7},{2,4},{3,5},{4,2},{5,3},{6,0},{7,1},{8,14},{9,15},{10,... | collective-permute-start | bytes 172040 | tf_op jit(solution)/shard_map/ppermute | solution.py:562
  56.0 6.3 %collective-permute-start.18 = (bf16[224,128]{1,0:T(8,128)(2,1)S(1)}, bf16[224,128]{1,0:T(8,128)(2,1)S(1)}, u32[]{:S(2)}, u32[]{:S(2)}) collective-permute-start(bf16[224,128]{1,0:T(8,128)(2,1)S(1)} %shard_map.126.refs_0_), channel_id=1, source_target_pairs={{0,4},{1,5},{2,6},{3,7},{4,0},{5,1},{6,2},{7,3},{8,12},{9,13},{10,... | collective-permute-start | bytes 172040 | tf_op jit(solution)/shard_map/ppermute | solution.py:562
  56.0 6.3 %collective-permute-start.17 = (bf16[224,128]{1,0:T(8,128)(2,1)S(1)}, bf16[224,128]{1,0:T(8,128)(2,1)S(1)}, u32[]{:S(2)}, u32[]{:S(2)}) collective-permute-start(bf16[224,128]{1,0:T(8,128)(2,1)S(1)} %shard_map.126.refs_0_), channel_id=1, source_target_pairs={{0,2},{1,3},{2,0},{3,1},{4,6},{5,7},{6,4},{7,5},{8,10},{9,11},{10,... | collective-permute-start | bytes 172040 | tf_op jit(solution)/shard_map/ppermute | solution.py:562
  62.4 7.3 %collective-permute-start.22 = (bf16[896,128]{1,0:T(8,128)(2,1)S(1)}, bf16[896,128]{1,0:T(8,128)(2,1)S(1)}, u32[]{:S(2)}, u32[]{:S(2)}) collective-permute-start(bf16[896,128]{1,0:T(8,128)(2,1)S(1)} %shard_map.127.refs_0_), channel_id=1, source_target_pairs={{0,17},{1,16},{2,19},{3,18},{4,21},{5,20},{6,23},{7,22},{8,25},{9,... | collective-permute-start | bytes 688136 | tf_op jit(solution)/shard_map/ppermute | solution.py:562
  63.8 8.6 %collective-permute-start.21 = (bf16[896,128]{1,0:T(8,128)(2,1)S(1)}, bf16[896,128]{1,0:T(8,128)(2,1)S(1)}, u32[]{:S(2)}, u32[]{:S(2)}) collective-permute-start(bf16[896,128]{1,0:T(8,128)(2,1)S(1)} %shard_map.127.refs_0_), channel_id=1, source_target_pairs={{0,16},{1,17},{2,18},{3,19},{4,20},{5,21},{6,22},{7,23},{8,24},{9,... | collective-permute-start | bytes 688136 | tf_op jit(solution)/shard_map/ppermute | solution.py:562
  65.3 7.1 %collective-permute-start.20 = (bf16[896,128]{1,0:T(8,128)(2,1)S(1)}, bf16[896,128]{1,0:T(8,128)(2,1)S(1)}, u32[]{:S(2)}, u32[]{:S(2)}) collective-permute-start(bf16[896,128]{1,0:T(8,128)(2,1)S(1)} %shard_map.127.refs_0_), channel_id=1, source_target_pairs={{0,1},{1,0},{2,3},{3,2},{4,5},{5,4},{6,7},{7,6},{8,9},{9,8},{10,11... | collective-permute-start | bytes 688136 | tf_op jit(solution)/shard_map/ppermute | solution.py:562
  65.9 6.9 %collective-permute-start.23 = (bf16[896,128]{1,0:T(8,128)(2,1)S(1)}, bf16[896,128]{1,0:T(8,128)(2,1)S(1)}, u32[]{:S(2)}, u32[]{:S(2)}) collective-permute-start(bf16[896,128]{1,0:T(8,128)(2,1)S(1)} %shard_map.127.refs_0_), channel_id=1, source_target_pairs={{0,8},{1,9},{2,10},{3,11},{4,12},{5,13},{6,14},{7,15},{8,0},{9,1},... | collective-permute-start | bytes 688136 | tf_op jit(solution)/shard_map/ppermute | solution.py:562
  69.7 3.2 %collective-permute-start.26 = (bf16[896,128]{1,0:T(8,128)(2,1)S(1)}, bf16[896,128]{1,0:T(8,128)(2,1)S(1)}, u32[]{:S(2)}, u32[]{:S(2)}) collective-permute-start(bf16[896,128]{1,0:T(8,128)(2,1)S(1)} %collective-permute-done.22.refs_3_), channel_id=1, source_target_pairs={{0,8},{1,9},{2,10},{3,11},{4,12},{5,13},{6,14},{7,15},{8,0},{9,1},... | collective-permute-start | bytes 688136 | tf_op jit(solution)/shard_map/ppermute | solution.py:562
  72.4 1.5 %collective-permute-start.25 = (bf16[896,128]{1,0:T(8,128)(2,1)S(1)}, bf16[896,128]{1,0:T(8,128)(2,1)S(1)}, u32[]{:S(2)}, u32[]{:S(2)}) collective-permute-start(bf16[896,128]{1,0:T(8,128)(2,1)S(1)} %collective-permute-done.21.refs_2_), channel_id=1, source_target_pairs={{0,8},{1,9},{2,10},{3,11},{4,12},{5,13},{6,14},{7,15},{8,0},{9,1},... | collective-permute-start | bytes 688136 | tf_op jit(solution)/shard_map/ppermute | solution.py:562
  72.4 1.8 %collective-permute-start.24 = (bf16[896,128]{1,0:T(8,128)(2,1)S(1)}, bf16[896,128]{1,0:T(8,128)(2,1)S(1)}, u32[]{:S(2)}, u32[]{:S(2)}) collective-permute-start(bf16[896,128]{1,0:T(8,128)(2,1)S(1)} %collective-permute-done.20.refs_1_), channel_id=1, source_target_pairs={{0,8},{1,9},{2,10},{3,11},{4,12},{5,13},{6,14},{7,15},{8,0},{9,1},... | collective-permute-start | bytes 688136 | tf_op jit(solution)/shard_map/ppermute | solution.py:562
  (3 other events, 11.9 us)

commit v3 on v2

--- a/solution.py
+++ b/solution.py
@@ -61,16 +61,11 @@
     return iota(shape, 1) < 64
 
 
-def head_masks(heads, head):
-    tall = (heads * 64, heads * head)
-    wide = (heads * head, heads * 64)
-    over = (iota(tall, 0) // 64 == iota(tall, 1) // head).astype(F32).astype(BF)
-    across = (iota(wide, 0) // head == iota(wide, 1) // 64).astype(F32).astype(BF)
-    return over, across
-
-
-def spread_bias(table, heads):
-    entries = table.shape[1]
+def pair_mask(rows, head):
+    return (iota((rows, 128), 0) // head) % 2 == iota((rows, 128), 1) // 64
+
+
+def spread_bias(read, entries, heads):
     side = 2 * WIN - 1
     lanes = iota((entries, 256), 1)
     rows = iota((entries, 256), 0)
@@ -81,7 +76,7 @@
     fits = (down >= 1 - WIN) & (right >= 1 - WIN)
     pick = (fits & (wanted == rows)).astype(F32)
     vectors = lax.dot_general(
-        table, pick, (((1,), (0,)), ((), ())), precision=lax.Precision.HIGHEST, preferred_element_type=F32
+        read(), pick, (((1,), (0,)), ((), ())), precision=lax.Precision.HIGHEST, preferred_element_type=F32
     )
     ahead = jnp.broadcast_to(vectors[:, None, :128], (heads, 8, 128)).reshape(heads * 8, 128)
     behind = jnp.broadcast_to(vectors[:, None, 128:], (heads, 8, 128)).reshape(heads * 8, 128)
@@ -133,45 +128,52 @@
     return jnp.where(differ, -10000.0, 0.0)
 
 
-def wide_of(field, heads, across):
+def wide_of(field, mask):
     field = field.astype(F32)
     half = first_half(field.shape)
     swapped = pltpu.roll(field, 64, 1)
     return [
-        jnp.concatenate([one.astype(BF)] * (heads // 2), axis=1) * across
-        for one in (jnp.where(half, field, swapped), jnp.where(half, swapped, field))
+        jnp.where(mask, one, 0.0).astype(BF) for one in (jnp.where(half, field, swapped), jnp.where(half, swapped, field))
     ]
 
 
-def tall_of(natural, heads, over):
-    return [jnp.concatenate([natural[64 * w : 64 * w + 64]] * heads, axis=0) * over for w in range(2)]
+def by_pairs(product, lhs, rhs, heads, left, right):
+    return jnp.concatenate(
+        [
+            product(lhs[left * n : left * n + left], rhs[right * n : right * n + right])
+            for n in range(heads // 2)
+        ],
+        axis=0,
+    )
 
 
 def forward(weights, field, bias, heads):
     width, tokens = field.shape
     head = width // heads
-    over, across = head_masks(heads, head)
+    two = 2 * head
+    mask = pair_mask(width, head)
     center, scale = norm(field)
     normed = center.astype(BF)
     mixed = dot_tn(weights[0][...], normed)
     query = (mixed[:width] * head ** (-0.5)).astype(BF)
     keys = mixed[width : 2 * width].astype(BF)
-    natural = mixed[width:].T.astype(BF)
-    values = natural[:, width:]
+    values = mixed[2 * width :].astype(BF)
     probs, attended = [], []
     half = first_half((width, 128))
     tall_half = first_half((heads * 64, 128))
     for p in range(tokens // 128):
         lanes = slice(128 * p, 128 * p + 128)
-        wide = wide_of(mixed[2 * width :, lanes], heads, across)
-        tall = tall_of(natural[lanes, :width], heads, over)
+        k = wide_of(mixed[width : 2 * width, lanes], mask)
+        v = wide_of(mixed[2 * width :, lanes], mask)
         q = query[:, lanes]
-        scores = jnp.where(tall_half, dot(tall[0], q), dot(tall[1], q)) + bias
+        first, second = (by_pairs(dot_tn, one, q, heads, two, two) for one in k)
+        scores = jnp.where(tall_half, first, second) + bias
         scores = scores.reshape(heads, 64, 128)
         expos = jnp.exp(scores - jnp.max(scores, axis=1, keepdims=True))
         prob = (expos / jnp.sum(expos, axis=1, keepdims=True)).reshape(heads * 64, 128)
         prob_b = prob.astype(BF)
-        attended.append(jnp.where(half, dot(wide[0], prob_b), dot(wide[1], prob_b)))
+        first, second = (by_pairs(dot, one, prob_b, heads, two, 128) for one in v)
+        attended.append(jnp.where(half, first, second))
         probs.append(prob)
     attended = jnp.concatenate(attended, axis=1).astype(BF)
     prob = jnp.concatenate(probs, axis=1)
@@ -194,7 +196,8 @@
     center, scale, query, keys, values, prob, attended, center_two, scale_two, hidden = saved
     width, tokens = grad.shape
     head = width // heads
-    over, across = head_masks(heads, head)
+    two = 2 * head
+    mask = pair_mask(width, head)
     grad_b = grad.astype(BF)
     grad_hidden = dot_tn(reduce_w, grad_b).astype(BF).astype(F32)
     grad_pre = (grad_hidden * slope).astype(BF)
@@ -204,13 +207,12 @@
     grad_att = dot(proj_w, grad_resid_b)
     half = first_half((width, 128))
     tall_half = first_half((heads * 64, 128))
-    across_f = across.astype(F32)
     grad_q, grad_k, grad_v = [], [], []
     grad_bias = jnp.zeros((heads * 64, 128), F32)
     for p in range(tokens // 128):
         lanes = slice(128 * p, 128 * p + 128)
-        tall = tall_of(values[lanes], heads, over)
-        wide = wide_of(keys[:, lanes], heads, across)
+        k = wide_of(keys[:, lanes], mask)
+        v = wide_of(values[:, lanes], mask)
         p_f = prob[:, lanes]
         p_b = p_f.astype(BF)
         att = grad_att[:, lanes]
@@ -219,18 +221,19 @@
         att_w = (jnp.where(half, att, zero).astype(BF), jnp.where(half, zero, att).astype(BF))
         query_f = query[:, lanes].astype(F32)
         query_w = (jnp.where(half, query_f, zero).astype(BF), jnp.where(half, zero, query_f).astype(BF))
-        grad_prob = jnp.where(tall_half, dot(tall[0], att_b), dot(tall[1], att_b))
+        first, second = (by_pairs(dot_tn, one, att_b, heads, two, two) for one in v)
+        grad_prob = jnp.where(tall_half, first, second)
         grad_prob = grad_prob.astype(BF).astype(F32)
         along = jnp.sum((p_f * grad_prob).reshape(heads, 64, 128), axis=1, keepdims=True)
         grad_score = p_f * (grad_prob.reshape(heads, 64, 128) - along).reshape(heads * 64, 128)
         grad_bias = grad_bias + grad_score
         score_b = grad_score.astype(BF)
-        grad_q.append(jnp.where(half, dot(wide[0], score_b), dot(wide[1], score_b)))
+        first, second = (by_pairs(dot, one, score_b, heads, two, 128) for one in k)
+        grad_q.append(jnp.where(half, first, second))
         for store, lhs, rhs in ((grad_k, query_w, score_b), (grad_v, att_w, p_b)):
             both = []
             for w in range(2):
-                full = dot_nt(lhs[w], rhs) * across_f
-                folded = sum(full[:, 128 * n : 128 * n + 128] for n in range(heads // 2))
+                folded = jnp.where(mask, by_pairs(dot_nt, lhs[w], rhs, heads, two, 128), 0.0)
                 both.append(folded + pltpu.roll(folded, 64, 1))
             store.append(jnp.where(half, both[0], both[1]))
     grad_q = jnp.concatenate(grad_q, axis=1).astype(BF).astype(F32) * head ** (-0.5)
@@ -263,39 +266,58 @@
         put(qkv[:, 128 * n : 128 * n + 128])
     put(jnp.concatenate([qkv[:, 128 * full :], proj[:, 128:]], axis=1))
     put(proj[:, :128])
-    for one in (expand, reduce):
-        for n in range(inner // 128):
-            put(one[:, 128 * n : 128 * n + 128])
+    columns = inner // 128
+    for n in range(columns // 2):
+        put(expand[:, 128 * n : 128 * n + 128])
+    half = buffer.shape[0] // 2
+    if half > at:
+        put(jnp.zeros((half - at, 128), F32))
+    for n in range(columns // 2, columns):
+        put(expand[:, 128 * n : 128 * n + 128])
+    for n in range(columns):
+        put(reduce[:, 128 * n : 128 * n + 128])
     heads = ahead.shape[0]
     put(jnp.concatenate([ahead, behind, jnp.zeros((16 - 2 * heads, 128), F32)], axis=0))
-    rest = buffer.shape[0] - at
-    if rest:
-        put(jnp.zeros((rest, 128), F32))
-
-
-def unpack_grads(buffer, outs, block, factor):
-    qkv, proj, expand, reduce, table = outs
-    width, inner = expand.shape[1:]
-    heads, _, entries = table.shape
-    at = 0
-
-    def take(rows):
-        nonlocal at
-        piece = buffer[at : at + rows, :].astype(F32) * factor
-        at += rows
-        return piece
-
+    if buffer.shape[0] > at:
+        put(jnp.zeros((buffer.shape[0] - at, 128), F32))
+
+
+class Taker:
+    def __init__(self, buffer, factor):
+        self.buffer, self.factor, self.at = buffer, factor, 0
+
+    def __call__(self, rows):
+        piece = self.buffer[self.at : self.at + rows, :]
+        self.at += rows
+        return piece.astype(F32) * self.factor
+
+
+def unpack_first(buffer, qkv, proj, expand, sent, factor):
+    take = Taker(buffer, factor)
+    width = proj.shape[0]
     full = 3 * width // 128
     for n in range(full):
-        qkv[block, :, 128 * n : 128 * n + 128] = take(width)
+        qkv[:, 128 * n : 128 * n + 128] = take(width)
     shared = take(width)
-    qkv[block, :, 128 * full :] = shared[:, :64]
-    proj[block, :, 128:] = shared[:, 64:]
-    proj[block, :, :128] = take(width)
-    for one in (expand, reduce):
-        for n in range(inner // 128):
-            one[block, :, 128 * n : 128 * n + 128] = take(width)
-    vectors = buffer[at : at + 16, :]
+    qkv[:, 128 * full :] = shared[:, :64]
+    sent(0)
+    proj[:, 128:] = shared[:, 64:]
+    proj[:, :128] = take(width)
+    sent(1)
+    for n in range(expand.shape[1] // 128):
+        expand[:, 128 * n : 128 * n + 128] = take(width)
+    sent(2)
+
+
+def unpack_second(buffer, expand, reduce, sent, table, block, factor):
+    take = Taker(buffer, factor)
+    width = reduce.shape[0]
+    for which, one in enumerate((expand, reduce)):
+        for n in range(one.shape[1] // 128):
+            one[:, 128 * n : 128 * n + 128] = take(width)
+        sent(which)
+    vectors = buffer[take.at : take.at + 16, :]
+    heads, _, entries = table.shape
     side = 2 * WIN - 1
     shape = (128, entries)
     rows, lanes = iota(shape, 0), iota(shape, 1)
@@ -324,7 +346,7 @@
 
 
 def plain_forward(x_far, cot_far, table_far, *refs):
-    far, (first, top, left, corner, tight), near, done = refs[:4], refs[4:9], refs[9:17], refs[17]
+    far, outs, (first, top, left, corner), (tight, *near), done = refs[:4], refs[4:8], refs[8:12], refs[12:21], refs[21]
     heads = table_far.shape[0]
     qkv_far, *rest = (there.at[0] for there in far)
     pairs = [(x_far, near[0]), (qkv_far, near[1]), *zip(rest, near[2:5], strict=True)]
@@ -341,7 +363,7 @@
     def write(f, c, piece):
         whole[f, :, 8 * c : 8 * c + 8, :] = piece
 
-    bias = spread_bias(table[:, 0, :], heads)
+    bias = spread_bias(lambda: table[:, 0, :], table_far.shape[2], heads)
     field = tokens_of(lambda f, c: x_ref[f, :, 8 * c : 8 * c + 8, :].astype(F32))
     resid, hidden, _, _, _ = forward((qkv, proj, expand), field, bias, heads)
     tile_of(resid + dot(reduce[...], hidden), write)
@@ -355,18 +377,23 @@
         tight[96 + n : 100 + n, :] = cot[f, 4 + r, :8, :].astype(F32)[:4]
     corner[...] = tight[:64].astype(BF)
     left[...] = tight[64:].astype(BF)
+    copies = [pltpu.make_async_copy(here, there, done.at[n]) for n, (here, there) in enumerate(zip((first, top, left, corner), outs, strict=True))]
+    for copy in copies:
+        copy.start()
+    for copy in copies:
+        copy.wait()
 
 
 def keep_plain(n_row, n_col, x_ref, table, qkv, proj, expand, bias_out, slope_out, *outs):
     heads = table.shape[0]
     field = tokens_of(lambda f, c: x_ref[f, :, 8 * c : 8 * c + 8, :].astype(F32))
-    _, _, pre, bell, saved = forward((qkv, proj, expand), field, spread_bias(table[:, 0, :], heads), heads)
+    _, _, pre, bell, saved = forward((qkv, proj, expand), field, spread_bias(lambda: table[:, 0, :], table.shape[2], heads), heads)
     slope_out[...] = slope_of(pre, bell)
     for ref, value in zip(outs, saved, strict=True):
         ref[...] = value
     last_row = lax.axis_index("row") == n_row - 1
     last_col = lax.axis_index("col") == n_col - 1
-    bias_out[...] = spread_bias(table[:, 1, :], heads) + shift_mask(bias_out.shape, last_row, last_col)
+    bias_out[...] = spread_bias(lambda: table[:, 1, :], table.shape[2], heads) + shift_mask(bias_out.shape, last_row, last_col)
 
 
 def shifted_block(
@@ -451,17 +478,17 @@
     return lax.axis_index("row") // 2 * 2 + lax.axis_index("col") % 2
 
 
-def cut(total, me, own, sends, here=slice(None)):
+def cut(total, me, own, sends, partners, here=slice(None)):
     rows = total.shape[0] // (len(sends) + 1)
     own[here, :] = total[pl.ds(pl.multiple_of(me * rows, 16), rows), :]
-    for d, send in enumerate(sends, 1):
+    for d, send in zip(partners, sends, strict=True):
         send[here, :] = total[pl.ds(pl.multiple_of((me ^ d) * rows, 16), rows), :].astype(BF)
 
 
 def add_core(keep, came, own, *rest):
     sends, total = rest[:-1], rest[-1]
     total[...] = keep[...].astype(F32) + came[...].astype(F32)
-    cut(total, near_place(), own, sends)
+    cut(total, near_place(), own, sends, (1, 2, 3))
 
 
 def add_near(count, mine, one, two, three, other, own, *rest):
@@ -469,8 +496,9 @@
     rows = own.shape[0] // 2
     place = lax.axis_index("col") // 2
     total[...] = mine[...] + one[...].astype(F32) + two[...].astype(F32) + three[...].astype(F32)
-    cut(total, place, own, sends, slice(0, rows))
-    cut(other, place, own, sends, slice(rows, 2 * rows))
+    partners = range(count - 1, 0, -1)
+    cut(total, place, own, sends, partners, slice(0, rows))
+    cut(other, place, own, sends, partners, slice(rows, 2 * rows))
 
 
 def add_far(*refs):
@@ -488,25 +516,50 @@
             out[pl.ds(there, rows), :] = piece[block * rows : block * rows + rows, :]
 
 
-def finish(factor, *refs):
-    ins, outs, buffer, done, stage = refs[:8], refs[8:13], refs[13], refs[14], refs[15:20]
+def finish(other, factor, *refs):
+    ins, refs = refs[:4], refs[4 + 5 * other :]
+    outs, buffer, done, (qkv, proj, expand, reduce, table) = refs[:5], refs[5], refs[6], refs[7:12]
     rows = ins[0].shape[0] // 2
     me = near_place()
-    core = lax.axis_index("row") % 2
+    for block in range(2):
+        for d, piece in enumerate(ins):
+            there = pl.multiple_of((me ^ d) * rows, 16)
+            buffer[block, pl.ds(there, rows), :] = piece[block * rows : block * rows + rows, :]
+    half = (lax.axis_index("row") + other) % 2
+    columns = expand.shape[2]
     copies = []
-    for block in range(2):
-        for n in range(8):
-            where = (core ^ (n // 4)) * 4 + (me ^ (n % 4))
-            piece = ins[n][block * rows : block * rows + rows, :]
-            buffer[pl.ds(pl.multiple_of(where * rows, 16), rows), :] = piece
-        unpack_grads(buffer, stage, block, factor)
-        for n in range(4):
-            copies.append(pltpu.make_async_copy(stage[n].at[block], outs[n].at[block], done.at[4 * block + n]))
-            copies[-1].start()
-    copies.append(pltpu.make_async_copy(stage[4], outs[4], done.at[8]))
-    copies[-1].start()
-    for copy in copies:
-        copy.wait()
+
+    def copy(here, there):
+        copies.append(pltpu.make_async_copy(here, there, done.at[len(copies)]))
+        copies[-1].start()
+
+    @pl.when(half == 0)
+    def _():
+        copies.clear()
+        for block in range(2):
+            pairs = [
+                (qkv.at[block], outs[0].at[block]),
+                (proj.at[block], outs[1].at[block]),
+                (expand.at[block], outs[2].at[block, :, pl.ds(0, columns)]),
+            ]
+            sent = lambda n, pairs=pairs: copy(*pairs[n])
+            unpack_first(buffer.at[block], qkv.at[block], proj.at[block], expand.at[block], sent, factor)
+        for one in copies:
+            one.wait()
+
+    @pl.when(half == 1)
+    def _():
+        copies.clear()
+        for block in range(2):
+            pairs = [
+                (expand.at[block], outs[2].at[block, :, pl.ds(columns, columns)]),
+                (reduce.at[block], outs[3].at[block]),
+            ]
+            sent = lambda n, pairs=pairs: copy(*pairs[n])
+            unpack_second(buffer.at[block], expand.at[block], reduce.at[block], sent, table, block, factor)
+        copy(table, outs[4])
+        for one in copies:
+            one.wait()
 
 
 class Whole:
@@ -517,7 +570,7 @@
         return self.ref[self.block]
 
 
-def call(kernel, outs, scratch, args, stacked=(), distant=(), micros=0.5, limit=LIMIT, far_outs=False):
+def call(kernel, outs, scratch, args, stacked=(), distant=(), micros=0.5, limit=LIMIT, far_outs=0, aliases=None):
     here, there = pl.BlockSpec(memory_space=pltpu.VMEM), pl.BlockSpec(memory_space=pltpu.HBM)
     count = len(args)
 
@@ -528,9 +581,10 @@
     return pl.pallas_call(
         body,
         in_specs=[here] * (count + len(stacked)) + [there] * len(distant),
-        out_specs=[there if far_outs else here] * len(outs),
+        out_specs=[there] * far_outs + [here] * (len(outs) - far_outs),
         out_shape=[jax.ShapeDtypeStruct(s, d) for s, d in outs],
         scratch_shapes=[pltpu.VMEM(*one) if isinstance(one, tuple) else one for one in scratch],
+        input_output_aliases=aliases or {},
         compiler_params=pltpu.CompilerParams(vmem_limit_bytes=limit),
         cost_estimate=pl.CostEstimate(flops=int(micros * 1.1e9), bytes_accessed=0, transcendentals=0),
     )(*args, *(arg for arg, _ in stacked), *distant)
@@ -563,7 +617,7 @@
 
     far = n_col // 2
     unit = 8 * far * 16
-    used = (4 * width + 2 * inner) * width // 128 + 16
+    used = (4 * width + 2 * inner) * width // 128 + 2 * 16
     size = -(-used // unit) * unit
     chunk = size // (8 * far)
     halves = [((size // 2, 128), BF)] * 2
@@ -573,14 +627,16 @@
     patches = frames * SHIFT * SHIFT
     tight = ((4 * patches, width), F32)
     lines = ((heads * 64, 128), F32)
+    sent = [(strip, F32), ((2, *strip), BF), ((2 * patches, width), BF), ((2 * patches, width), BF)]
     first, top, left, corner = call(
         plain_forward,
-        [(strip, F32), ((2, *strip), BF), ((2 * patches, width), BF), ((2 * patches, width), BF)],
-        [tight, (tile, BF), *((w.shape[1:], BF) for w in weights), (tile, BF), (tile, F32), (table.shape, F32), pltpu.SemaphoreType.DMA((7,))],
+        sent,
+        [*sent, tight, (tile, BF), *((w.shape[1:], BF) for w in weights), (tile, BF), (tile, F32), (table.shape, F32), pltpu.SemaphoreType.DMA((7,))],
         [],
         distant=(block_input, cotangent, table, *weights),
         micros=2.3,
         limit=FULL,
+        far_outs=4,
     )
     halo = [send(top, -1, 0), send(left, 0, -1), send(corner, -1, -1)]
     bias, *kept = call(
@@ -592,7 +648,7 @@
             ((1, tokens), F32),
             ((width, tokens), BF),
             ((width, tokens), BF),
-            ((tokens, width), BF),
+            ((width, tokens), BF),
             ((heads * 64, tokens), F32),
             ((width, tokens), BF),
             ((width, tokens), F32),
@@ -617,7 +673,8 @@
     eighth, quarter, piece = (size // 8, 128), (size // 4, 128), (2 * chunk, 128)
 
     def near(own, *sends):
-        return [own] + [swap(one, d & 2, d & 1) for d, one in enumerate(sends, 1)]
+        came = [swap(one, d & 2, d & 1) for d, one in reversed(list(enumerate(sends, 1)))]
+        return [own] + came[::-1]
 
     quarters = [(eighth, F32)] + [(eighth, BF)] * 3
     summed = [((size // 2, 128), F32)]
@@ -642,16 +699,25 @@
         [(eighth, F32)],
         [*near(*plain), other],
     )
-    distant = [own] + [swap(one, 0, 2 * d) for d, one in enumerate(sends, 1)]
+    distant = [own] + [swap(one, 0, 2 * d) for d, one in zip(range(far - 1, 0, -1), sends, strict=True)]
     (done,) = call(add_far, [(piece, BF)], [], distant)
     distant = [done] + [swap(done, 0, 2 * d) for d in range(1, far)]
     (joined,) = call(join_far, [(quarter, BF)], [], distant)
     near = [joined] + [swap(joined, d & 2, d & 1) for d in range(1, 4)]
-    near = near + [swap(one, 1, 0) for one in near]
     factor = 1.0 / math.sqrt(frames * rows * n_row * cols * n_col)
     shapes = [(w.shape, F32) for w in (*weights, table)]
+    stage = [((2, size // 2, 128), BF), pltpu.SemaphoreType.DMA((6,)), *shapes]
+    stage[4] = ((2, width, inner // 2), F32)
+    grads = call(functools.partial(finish, 0, factor), shapes, stage, near, far_outs=5, micros=1.2)
     qkv, proj, expand, reduce, table = call(
-        functools.partial(finish, factor), shapes, [buffer, pltpu.SemaphoreType.DMA((9,)), *shapes], near, far_outs=True
+        functools.partial(finish, 1, factor),
+        shapes,
+        stage,
+        [swap(one, 1, 0) for one in near],
+        distant=grads,
+        far_outs=5,
+        aliases={4 + n: n for n in range(5)},
+        micros=1.2,
     )
     return input_grad, qkv, proj, expand, jnp.swapaxes(reduce, 1, 2), jnp.swapaxes(table, 0, 1)
 

time: 76.7 us -> 75.6 us (0.986)
  waiting for transfers between devices: 27.7 us -> 26.1 us
    ppermute x21, waiting for transfers between devices: 23.5 us -> 21.9 us  [swap(): return lax.ppermute(block, axes, route)]
    pallas_call x11 -> x12, Pallas kernels: 18.2 us -> 18.7 us  [call(): pl.pallas_call(body, in_specs=[here] * (count + len(stacked)) + [there] *...]
  transfers between devices with their start and end apart: 27 -> 27, of which waited for: 16 -> 14; matrix products, arithmetic and copies ran while one was open for 0% -> 0% of each run, Pallas kernels for 7% -> 9%
where the time goes in v3:
time: 75.6 us; the launch traced here: 75.4 us
  starting transfers between devices  29.7 us (39%)
  waiting for transfers between devices  26.1 us (35%)
  Pallas kernels  18.7 us (25%)
  between operations  0.98 us (1%)
    ppermute x21, waiting for transfers between devices, swap(): return lax.ppermute(block, axes, route)  21.9 us
    ppermute x21, starting transfers between devices, swap(): return lax.ppermute(block, axes, route)  19.3 us
    pallas_call x12, Pallas kernels, call(): pl.pallas_call(body, in_specs=[here] * (count + len(stacked)) + [there] *...  18.7 us
    ppermute x6, starting transfers between devices, send(): return lax.ppermute(block, axes, route)  10.3 us
    ppermute x6, waiting for transfers between devices, send(): return lax.ppermute(block, axes, route)  4.16 us
  transfers between devices with their start and end apart: 27, of which 14 were waited for; matrix products, arithmetic and copies ran while one was open for 0% of the time, Pallas kernels for 9%

profile of v3, /device:TPU:0, one launch (start us, length us, event | category | flops | bytes accessed | tf_op | source)
XLA Modules:
  0.0 75.4 jit_solution(12315093795577708867)
XLA Ops:
  0.7 4.6 %shard_map.118 = (f32[2,4,16,192]{3,2,1,0:T(8,128)}, bf16[2,2,4,16,192]{4,3,2,1,0:T(8,128)(2,1)}, bf16[64,192]{1,0:T(8,128)(2,1)}, bf16[64,192]{1,0:T(8,128)(2,1)}) custom-call(bf16[2,8,16,192]{3,2,1,0:T(8,128)(2,1)} %refs_0_.3, bf16[2,8,16,192]{3,2,1,0:T(8,128)(2,1)} %refs_1_.3, f32[6,2,225]{2,1,0:T(2,128)} %bitcast.7, bf16[2,192,576]{2,1,0:T(8,128)(2,1)} %refs_15_.1, ...), custom_call_target="tpu_custom_call" | custom-call | flops 2529999872 | tf_op jit(solution)/shard_map/pallas_call | solution.py:581
  5.3 6.1 %collective-permute-start.1 = (bf16[64,192]{1,0:T(8,128)(2,1)}, bf16[64,192]{1,0:T(8,128)(2,1)S(1)}, u32[]{:S(2)}, u32[]{:S(2)}) collective-permute-start(bf16[64,192]{1,0:T(8,128)(2,1)} %get-tuple-element.67), channel_id=1, source_target_pairs={{0,7},{1,0},{2,1},{3,2},{4,3},{5,4},{6,5},{7,6},{8,15},{9,8},{10,9... | collective-permute-start | bytes 73736 | tf_op jit(solution)/shard_map/ppermute | solution.py:610
  12.0 1.1 %collective-permute-start = (bf16[2,2,4,16,192]{4,3,2,1,0:T(8,128)(2,1)}, bf16[2,2,4,16,192]{4,3,2,1,0:T(8,128)(2,1)S(1)}, u32[]{:S(2)}, u32[]{:S(2)}) collective-permute-start(bf16[2,2,4,16,192]{4,3,2,1,0:T(8,128)(2,1)} %get-tuple-element.66), channel_id=1, source_target_pairs={{0,24},{1,25},{2,26},{3,27},{4,28},{5,29},{6,30},{7,31},{8,0},{9,1... | collective-permute-start | bytes 294920 | tf_op jit(solution)/shard_map/ppermute | solution.py:610
  13.1 2.3 %shard_map.119 = (f32[384,128]{1,0:T(8,128)S(1)}, f32[768,256]{1,0:T(8,128)S(1)}, f32[192,256]{1,0:T(8,128)S(1)}, f32[1,256]{1,0:T(1,128)S(1)}, bf16[192,256]{1,...) custom-call(bf16[2,8,16,192]{3,2,1,0:T(8,128)(2,1)S(1)} %copy-done.4, ...), custom_call_target="tpu_custom_call" | custom-call | flops 2529999872 | tf_op jit(solution)/shard_map/pallas_call | solution.py:581
  15.9 4.4 %shard_map.120 = (f32[2,4,16,192]{3,2,1,0:T(8,128)S(1)}, bf16[2,4,16,192]{3,2,1,0:T(8,128)(2,1)S(1)}, bf16[32,192]{1,0:T(8,128)(2,1)S(1)}, bf16[32,192]{1,0:T(8,...) custom-call(f32[2,4,16,192]{3,2,1,0:T(8,128)S(1)} %copy-done.7, ...), custom_call_target="tpu_custom_call" | custom-call | flops 5280000000 | tf_op jit(solution)/shard_map/pallas_call | solution.py:581
  20.3 0.7 collective-permute-start.6
  21.1 1.5 %collective-permute-start.4 = (bf16[32,192]{1,0:T(8,128)(2,1)S(1)}, bf16[32,192]{1,0:T(8,128)(2,1)S(1)}, u32[]{:S(2)}, u32[]{:S(2)}) collective-permute-start(bf16[32,192]{1,0:T(8,128)(2,1)S(1)} %get-tuple-element.72), channel_id=1, source_target_pairs={{0,1},{1,2},{2,3},{3,4},{4,5},{5,6},{6,7},{7,0},{8,9},{9,10},{10,1... | collective-permute-start | bytes 36872 | tf_op jit(solution)/shard_map/ppermute | solution.py:610
  22.6 1.0 %collective-permute-start.3 = (bf16[2,4,16,192]{3,2,1,0:T(8,128)(2,1)S(1)}, bf16[2,4,16,192]{3,2,1,0:T(8,128)(2,1)S(1)}, u32[]{:S(2)}, u32[]{:S(2)}) collective-permute-start(bf16[2,4,16,192]{3,2,1,0:T(8,128)(2,1)S(1)} %get-tuple-element.71), channel_id=1, source_target_pairs={{0,8},{1,9},{2,10},{3,11},{4,12},{5,13},{6,14},{7,15},{8,16},{9,17... | collective-permute-start | bytes 147464 | tf_op jit(solution)/shard_map/ppermute | solution.py:610
  24.3 1.5 %collective-permute-start.8 = (bf16[448,128]{1,0:T(8,128)(2,1)S(1)}, bf16[448,128]{1,0:T(8,128)(2,1)S(1)}, u32[]{:S(2)}, u32[]{:S(2)}) collective-permute-start(bf16[448,128]{1,0:T(8,128)(2,1)S(1)} %get-tuple-element.101), channel_id=1, source_target_pairs={{0,16},{1,17},{2,18},{3,19},{4,20},{5,21},{6,22},{7,23},{8,24},{9,... | collective-permute-start | bytes 344072 | tf_op jit(solution)/shard_map/ppermute | solution.py:616
  25.8 1.8 %collective-permute-done.4.refs_2_ = bf16[32,192]{1,0:T(8,128)(2,1)S(1)} collective-permute-done((bf16[32,192]{1,0:T(8,128)(2,1)S(1)}, bf16[32,192]{1,0:T(8,128)(2,1)S(1)}, u32[]{:S(2)}, u32[]{:S(2)}) %collective-permute-start.4) | collective-permute-done | bytes 12320 | tf_op jit(solution)/shard_map/ppermute | solution.py:610
  27.6 1.9 %collective-permute-done.5.refs_3_ = bf16[32,192]{1,0:T(8,128)(2,1)S(1)} collective-permute-done((bf16[32,192]{1,0:T(8,128)(2,1)S(1)}, bf16[32,192]{1,0:T(8,128)(2,1)S(1)}, u32[]{:S(2)}, u32[]{:S(2)}) %collective-permute-start.5) | collective-permute-done | bytes 12320 | tf_op jit(solution)/shard_map/ppermute | solution.py:610
  29.5 3.1 %shard_map.122 = (f32[2,8,16,192]{3,2,1,0:T(8,128)}, f32[384,128]{1,0:T(8,128)S(1)}, bf16[192,256]{1,0:T(8,128)(2,1)S(1)}, bf16[576,256]{1,0:T(8,128)(2,1)S(1)},...) custom-call(f32[2,4,16,192]{3,2,1,0:T(8,128)S(1)} %get-tuple-element.70.refs_0_, ...), custom_call_target="tpu_custom_call" | custom-call | flops 3520000000 | tf_op jit(solution)/shard_map/pallas_call | solution.py:581
  34.2 1.8 %collective-permute-done.10.refs_1_ = bf16[1792,128]{1,0:T(8,128)(2,1)S(1)} collective-permute-done((bf16[1792,128]{1,0:T(8,128)(2,1)S(1)}, bf16[1792,128]{1,0:T(8,128)(2,1)S(1)}, u32[]{:S(2)}, u32[]{:S(2)}) %collective-permute-start.10) | collective-permute-done | bytes 458784 | tf_op jit(solution)/shard_map/ppermute | solution.py:616
  36.6 1.2 %collective-permute-start.12 = (bf16[448,128]{1,0:T(8,128)(2,1)S(1)}, bf16[448,128]{1,0:T(8,128)(2,1)S(1)}, u32[]{:S(2)}, u32[]{:S(2)}) collective-permute-start(bf16[448,128]{1,0:T(8,128)(2,1)S(1)} %get-tuple-element.107), channel_id=1, source_target_pairs={{0,16},{1,17},{2,18},{3,19},{4,20},{5,21},{6,22},{7,23},{8,24},{9,... | collective-permute-start | bytes 344072 | tf_op jit(solution)/shard_map/ppermute | solution.py:616
  37.8 1.9 %collective-permute-start.13 = (bf16[448,128]{1,0:T(8,128)(2,1)S(1)}, bf16[448,128]{1,0:T(8,128)(2,1)S(1)}, u32[]{:S(2)}, u32[]{:S(2)}) collective-permute-start(bf16[448,128]{1,0:T(8,128)(2,1)S(1)} %get-tuple-element.108), channel_id=1, source_target_pairs={{0,17},{1,16},{2,19},{3,18},{4,21},{5,20},{6,23},{7,22},{8,25},{9,... | collective-permute-start | bytes 344072 | tf_op jit(solution)/shard_map/ppermute | solution.py:616
  39.7 1.7 %collective-permute-done.11.refs_1_ = bf16[448,128]{1,0:T(8,128)(2,1)S(1)} collective-permute-done((bf16[448,128]{1,0:T(8,128)(2,1)S(1)}, bf16[448,128]{1,0:T(8,128)(2,1)S(1)}, u32[]{:S(2)}, u32[]{:S(2)}) %collective-permute-start.11) | collective-permute-done | bytes 114720 | tf_op jit(solution)/shard_map/ppermute | solution.py:616
  41.7 3.4 %collective-permute-done.13.refs_3_ = bf16[448,128]{1,0:T(8,128)(2,1)S(1)} collective-permute-done((bf16[448,128]{1,0:T(8,128)(2,1)S(1)}, bf16[448,128]{1,0:T(8,128)(2,1)S(1)}, u32[]{:S(2)}, u32[]{:S(2)}) %collective-permute-start.13) | collective-permute-done | bytes 114720 | tf_op jit(solution)/shard_map/ppermute | solution.py:616
  45.2 3.1 %collective-permute-start.14 = (bf16[224,128]{1,0:T(8,128)(2,1)S(1)}, bf16[224,128]{1,0:T(8,128)(2,1)S(1)}, u32[]{:S(2)}, u32[]{:S(2)}) collective-permute-start(bf16[224,128]{1,0:T(8,128)(2,1)S(1)} %get-tuple-element.111), channel_id=1, source_target_pairs={{0,6},{1,7},{2,4},{3,5},{4,2},{5,3},{6,0},{7,1},{8,14},{9,15},{10,... | collective-permute-start | bytes 172040 | tf_op jit(solution)/shard_map/ppermute | solution.py:616
  48.2 1.4 %collective-permute-start.16 = (bf16[224,128]{1,0:T(8,128)(2,1)S(1)}, bf16[224,128]{1,0:T(8,128)(2,1)S(1)}, u32[]{:S(2)}, u32[]{:S(2)}) collective-permute-start(bf16[224,128]{1,0:T(8,128)(2,1)S(1)} %get-tuple-element.113), channel_id=1, source_target_pairs={{0,2},{1,3},{2,0},{3,1},{4,6},{5,7},{6,4},{7,5},{8,10},{9,11},{10,... | collective-permute-start | bytes 172040 | tf_op jit(solution)/shard_map/ppermute | solution.py:616
  49.6 1.7 %collective-permute-done.14.refs_1_ = bf16[224,128]{1,0:T(8,128)(2,1)S(1)} collective-permute-done((bf16[224,128]{1,0:T(8,128)(2,1)S(1)}, bf16[224,128]{1,0:T(8,128)(2,1)S(1)}, u32[]{:S(2)}, u32[]{:S(2)}) %collective-permute-start.14) | collective-permute-done | bytes 57376 | tf_op jit(solution)/shard_map/ppermute | solution.py:616
  51.3 2.1 %collective-permute-done.15.refs_2_ = bf16[224,128]{1,0:T(8,128)(2,1)S(1)} collective-permute-done((bf16[224,128]{1,0:T(8,128)(2,1)S(1)}, bf16[224,128]{1,0:T(8,128)(2,1)S(1)}, u32[]{:S(2)}, u32[]{:S(2)}) %collective-permute-start.15) | collective-permute-done | bytes 57376 | tf_op jit(solution)/shard_map/ppermute | solution.py:616
  53.4 2.0 %collective-permute-start.19 = (bf16[224,128]{1,0:T(8,128)(2,1)S(1)}, bf16[224,128]{1,0:T(8,128)(2,1)S(1)}, u32[]{:S(2)}, u32[]{:S(2)}) collective-permute-start(bf16[224,128]{1,0:T(8,128)(2,1)S(1)} %shard_map.126.refs_0_), channel_id=1, source_target_pairs={{0,6},{1,7},{2,4},{3,5},{4,2},{5,3},{6,0},{7,1},{8,14},{9,15},{10,... | collective-permute-start | bytes 172040 | tf_op jit(solution)/shard_map/ppermute | solution.py:616
  55.5 2.3 %collective-permute-start.17 = (bf16[224,128]{1,0:T(8,128)(2,1)S(1)}, bf16[224,128]{1,0:T(8,128)(2,1)S(1)}, u32[]{:S(2)}, u32[]{:S(2)}) collective-permute-start(bf16[224,128]{1,0:T(8,128)(2,1)S(1)} %shard_map.126.refs_0_), channel_id=1, source_target_pairs={{0,2},{1,3},{2,0},{3,1},{4,6},{5,7},{6,4},{7,5},{8,10},{9,11},{10,... | collective-permute-start | bytes 172040 | tf_op jit(solution)/shard_map/ppermute | solution.py:616
  57.9 1.6 %collective-permute-done.19.refs_3_ = bf16[224,128]{1,0:T(8,128)(2,1)S(1)} collective-permute-done((bf16[224,128]{1,0:T(8,128)(2,1)S(1)}, bf16[224,128]{1,0:T(8,128)(2,1)S(1)}, u32[]{:S(2)}, u32[]{:S(2)}) %collective-permute-start.19) | collective-permute-done | bytes 57376 | tf_op jit(solution)/shard_map/ppermute | solution.py:616
  59.5 1.7 %collective-permute-done.18.refs_2_ = bf16[224,128]{1,0:T(8,128)(2,1)S(1)} collective-permute-done((bf16[224,128]{1,0:T(8,128)(2,1)S(1)}, bf16[224,128]{1,0:T(8,128)(2,1)S(1)}, u32[]{:S(2)}, u32[]{:S(2)}) %collective-permute-start.18) | collective-permute-done | bytes 57376 | tf_op jit(solution)/shard_map/ppermute | solution.py:616
  61.2 1.6 %collective-permute-start.25 = (bf16[896,128]{1,0:T(8,128)(2,1)S(1)}, bf16[896,128]{1,0:T(8,128)(2,1)S(1)}, u32[]{:S(2)}, u32[]{:S(2)}) collective-permute-start(bf16[896,128]{1,0:T(8,128)(2,1)S(1)} %shard_map.127.refs_0_), channel_id=1, source_target_pairs={{0,17},{1,16},{2,19},{3,18},{4,21},{5,20},{6,23},{7,22},{8,25},{9,... | collective-permute-start | bytes 688136 | tf_op jit(solution)/shard_map/ppermute | solution.py:616
  62.7 1.3 %collective-permute-start.23 = (bf16[896,128]{1,0:T(8,128)(2,1)S(1)}, bf16[896,128]{1,0:T(8,128)(2,1)S(1)}, u32[]{:S(2)}, u32[]{:S(2)}) collective-permute-start(bf16[896,128]{1,0:T(8,128)(2,1)S(1)} %shard_map.127.refs_0_), channel_id=1, source_target_pairs={{0,16},{1,17},{2,18},{3,19},{4,20},{5,21},{6,22},{7,23},{8,24},{9,... | collective-permute-start | bytes 688136 | tf_op jit(solution)/shard_map/ppermute | solution.py:616
  64.0 0.7 collective-permute-start.21
  64.7 4.4 %collective-permute-done.25.refs_3_ = bf16[896,128]{1,0:T(8,128)(2,1)S(1)} collective-permute-done((bf16[896,128]{1,0:T(8,128)(2,1)S(1)}, bf16[896,128]{1,0:T(8,128)(2,1)S(1)}, u32[]{:S(2)}, u32[]{:S(2)}) %collective-permute-start.25) | collective-permute-done | bytes 229408 | tf_op jit(solution)/shard_map/ppermute | solution.py:616
  69.1 2.7 %collective-permute-done.23.refs_2_ = bf16[896,128]{1,0:T(8,128)(2,1)S(1)} collective-permute-done((bf16[896,128]{1,0:T(8,128)(2,1)S(1)}, bf16[896,128]{1,0:T(8,128)(2,1)S(1)}, u32[]{:S(2)}, u32[]{:S(2)}) %collective-permute-start.23) | collective-permute-done | bytes 229408 | tf_op jit(solution)/shard_map/ppermute | solution.py:616
  72.3 1.5 %shard_map.128 = (f32[2,192,576]{2,1,0:T(8,128)}, f32[2,192,192]{2,1,0:T(8,128)}, f32[2,192,768]{2,1,0:T(8,128)}, f32[2,192,768]{2,1,0:T(8,128)}, f32[6,2,225]{2,1,0:T(2,128)}) custom-call(bf16[896,128]{1,0:T(8,128)(2,1)S(1)} %shard_map.127.refs_0_, bf16[896,128]{1,0:T(8,128)(2,1)S(1)} %collective-permute-done.21.refs_1_, ...), custom_call_target="tpu_custom_call" | custom-call | flops 1320000000 | tf_op jit(solution)/shard_map/pallas_call | solution.py:581
  73.8 1.5 %shard_map.129 = (f32[2,192,576]{2,1,0:T(8,128)}, f32[2,192,192]{2,1,0:T(8,128)}, f32[2,192,768]{2,1,0:T(8,128)}, f32[2,192,768]{2,1,0:T(8,128)}, f32[6,2,225]{2,1,0:T(2,128)}) custom-call(bf16[896,128]{1,0:T(8,128)(2,1)S(1)} %collective-permute-done.20.refs_0_, ...), custom_call_target="tpu_custom_call", output_to_operand_aliasing={{0}: (4, {}), {1}: (5, {}), {2}: (6, {}), {3}: (7, {}), {4}... | custom-call | flops 1320000000 | tf_op jit(solution)/shard_map/pallas_call | solution.py:581
  (50 shorter events, 4.9 us)
Async XLA Ops:
  0.6 12.5 %copy-start = (bf16[2,192,768]{2,1,0:T(8,128)(2,1)S(1)}, bf16[2,192,768]{2,1,0:T(8,128)(2,1)}, u32[]{:S(2)}) copy-start(bf16[2,192,768]{2,1,0:T(8,128)(2,1)} %refs_17_.1) | copy-start | bytes 1769476
  0.6 12.4 %copy-start.2 = (bf16[2,192,576]{2,1,0:T(8,128)(2,1)S(1)}, bf16[2,192,576]{2,1,0:T(8,128)(2,1)}, u32[]{:S(2)}) copy-start(bf16[2,192,576]{2,1,0:T(8,128)(2,1)} %refs_15_.1) | copy-start | bytes 1327108
  0.7 12.4 %copy-start.3 = (bf16[2,192,192]{2,1,0:T(8,128)(2,1)S(1)}, bf16[2,192,192]{2,1,0:T(8,128)(2,1)}, u32[]{:S(2)}) copy-start(bf16[2,192,192]{2,1,0:T(8,128)(2,1)} %refs_16_.1) | copy-start | bytes 442372
  0.7 12.4 %copy-start.4 = (bf16[2,8,16,192]{3,2,1,0:T(8,128)(2,1)S(1)}, bf16[2,8,16,192]{3,2,1,0:T(8,128)(2,1)}, u32[]{:S(2)}) copy-start(bf16[2,8,16,192]{3,2,1,0:T(8,128)(2,1)} %refs_0_.3) | copy-start | bytes 294916
  0.7 12.4 %copy-start.6 = (f32[2,6,225]{2,0,1:T(2,128)S(1)}, f32[2,6,225]{2,0,1:T(2,128)}, u32[]{:S(2)}) copy-start(f32[2,6,225]{2,0,1:T(2,128)} %param.13) | copy-start | bytes 32404
  5.3 10.2 %collective-permute-start.1 = (bf16[64,192]{1,0:T(8,128)(2,1)}, bf16[64,192]{1,0:T(8,128)(2,1)S(1)}, u32[]{:S(2)}, u32[]{:S(2)}) collective-permute-start(bf16[64,192]{1,0:T(8,128)(2,1)} %get-tuple-element.67), channel_id=1, source_target_pairs={{0,7},{1,0},{2,1},{3,2},{4,3},{5,4},{6,5},{7,6},{8,15},{9,8},{10,9... | collective-permute-start | bytes 73736 | tf_op jit(solution)/shard_map/ppermute | solution.py:610
  11.4 4.1 %collective-permute-start.2 = (bf16[64,192]{1,0:T(8,128)(2,1)}, bf16[64,192]{1,0:T(8,128)(2,1)S(1)}, u32[]{:S(2)}, u32[]{:S(2)}) collective-permute-start(bf16[64,192]{1,0:T(8,128)(2,1)} %get-tuple-element.68), channel_id=1, source_target_pairs={{0,31},{1,24},{2,25},{3,26},{4,27},{5,28},{6,29},{7,30},{8,7},{9,0... | collective-permute-start | bytes 73736 | tf_op jit(solution)/shard_map/ppermute | solution.py:610
  12.0 4.0 %collective-permute-start = (bf16[2,2,4,16,192]{4,3,2,1,0:T(8,128)(2,1)}, bf16[2,2,4,16,192]{4,3,2,1,0:T(8,128)(2,1)S(1)}, u32[]{:S(2)}, u32[]{:S(2)}) collective-permute-start(bf16[2,2,4,16,192]{4,3,2,1,0:T(8,128)(2,1)} %get-tuple-element.66), channel_id=1, source_target_pairs={{0,24},{1,25},{2,26},{3,27},{4,28},{5,29},{6,30},{7,31},{8,0},{9,1... | collective-permute-start | bytes 294920 | tf_op jit(solution)/shard_map/ppermute | solution.py:610
  20.3 3.3 %collective-permute-start.6 = (bf16[1792,128]{1,0:T(8,128)(2,1)S(1)}, bf16[1792,128]{1,0:T(8,128)(2,1)S(1)}, u32[]{:S(2)}, u32[]{:S(2)}) collective-permute-start(bf16[1792,128]{1,0:T(8,128)(2,1)S(1)} %get-tuple-element.76), channel_id=1, source_target_pairs={{0,8},{1,9},{2,10},{3,11},{4,12},{5,13},{6,14},{7,15},{8,0},{9,1},... | collective-permute-start | bytes 1376264 | tf_op jit(solution)/shard_map/ppermute | solution.py:616
  21.1 6.5 %collective-permute-start.4 = (bf16[32,192]{1,0:T(8,128)(2,1)S(1)}, bf16[32,192]{1,0:T(8,128)(2,1)S(1)}, u32[]{:S(2)}, u32[]{:S(2)}) collective-permute-start(bf16[32,192]{1,0:T(8,128)(2,1)S(1)} %get-tuple-element.72), channel_id=1, source_target_pairs={{0,1},{1,2},{2,3},{3,4},{4,5},{5,6},{6,7},{7,0},{8,9},{9,10},{10,1... | collective-permute-start | bytes 36872 | tf_op jit(solution)/shard_map/ppermute | solution.py:610
  22.6 6.9 %collective-permute-start.5 = (bf16[32,192]{1,0:T(8,128)(2,1)S(1)}, bf16[32,192]{1,0:T(8,128)(2,1)S(1)}, u32[]{:S(2)}, u32[]{:S(2)}) collective-permute-start(bf16[32,192]{1,0:T(8,128)(2,1)S(1)} %get-tuple-element.73), channel_id=1, source_target_pairs={{0,9},{1,10},{2,11},{3,12},{4,13},{5,14},{6,15},{7,8},{8,17},{9,18... | collective-permute-start | bytes 36872 | tf_op jit(solution)/shard_map/ppermute | solution.py:610
  22.6 6.9 %collective-permute-start.3 = (bf16[2,4,16,192]{3,2,1,0:T(8,128)(2,1)S(1)}, bf16[2,4,16,192]{3,2,1,0:T(8,128)(2,1)S(1)}, u32[]{:S(2)}, u32[]{:S(2)}) collective-permute-start(bf16[2,4,16,192]{3,2,1,0:T(8,128)(2,1)S(1)} %get-tuple-element.71), channel_id=1, source_target_pairs={{0,8},{1,9},{2,10},{3,11},{4,12},{5,13},{6,14},{7,15},{8,16},{9,17... | collective-permute-start | bytes 147464 | tf_op jit(solution)/shard_map/ppermute | solution.py:610
  23.9 8.8 %collective-permute-start.7 = (bf16[448,128]{1,0:T(8,128)(2,1)S(1)}, bf16[448,128]{1,0:T(8,128)(2,1)S(1)}, u32[]{:S(2)}, u32[]{:S(2)}) collective-permute-start(bf16[448,128]{1,0:T(8,128)(2,1)S(1)} %get-tuple-element.100), channel_id=1, source_target_pairs={{0,1},{1,0},{2,3},{3,2},{4,5},{5,4},{6,7},{7,6},{8,9},{9,8},{10,11... | collective-permute-start | bytes 344072 | tf_op jit(solution)/shard_map/ppermute | solution.py:616
  24.3 8.3 %collective-permute-start.8 = (bf16[448,128]{1,0:T(8,128)(2,1)S(1)}, bf16[448,128]{1,0:T(8,128)(2,1)S(1)}, u32[]{:S(2)}, u32[]{:S(2)}) collective-permute-start(bf16[448,128]{1,0:T(8,128)(2,1)S(1)} %get-tuple-element.101), channel_id=1, source_target_pairs={{0,16},{1,17},{2,18},{3,19},{4,20},{5,21},{6,22},{7,23},{8,24},{9,... | collective-permute-start | bytes 344072 | tf_op jit(solution)/shard_map/ppermute | solution.py:616
  27.6 5.7 %collective-permute-start.9 = (bf16[448,128]{1,0:T(8,128)(2,1)S(1)}, bf16[448,128]{1,0:T(8,128)(2,1)S(1)}, u32[]{:S(2)}, u32[]{:S(2)}) collective-permute-start(bf16[448,128]{1,0:T(8,128)(2,1)S(1)} %get-tuple-element.102), channel_id=1, source_target_pairs={{0,17},{1,16},{2,19},{3,18},{4,21},{5,20},{6,23},{7,22},{8,25},{9,... | collective-permute-start | bytes 344072 | tf_op jit(solution)/shard_map/ppermute | solution.py:616
  34.1 1.9 %collective-permute-start.10 = (bf16[1792,128]{1,0:T(8,128)(2,1)S(1)}, bf16[1792,128]{1,0:T(8,128)(2,1)S(1)}, u32[]{:S(2)}, u32[]{:S(2)}) collective-permute-start(bf16[1792,128]{1,0:T(8,128)(2,1)S(1)} %get-tuple-element.104), channel_id=1, source_target_pairs={{0,8},{1,9},{2,10},{3,11},{4,12},{5,13},{6,14},{7,15},{8,0},{9,1},... | collective-permute-start | bytes 1376264 | tf_op jit(solution)/shard_map/ppermute | solution.py:616
  36.2 5.3 %collective-permute-start.11 = (bf16[448,128]{1,0:T(8,128)(2,1)S(1)}, bf16[448,128]{1,0:T(8,128)(2,1)S(1)}, u32[]{:S(2)}, u32[]{:S(2)}) collective-permute-start(bf16[448,128]{1,0:T(8,128)(2,1)S(1)} %get-tuple-element.106), channel_id=1, source_target_pairs={{0,1},{1,0},{2,3},{3,2},{4,5},{5,4},{6,7},{7,6},{8,9},{9,8},{10,11... | collective-permute-start | bytes 344072 | tf_op jit(solution)/shard_map/ppermute | solution.py:616
  36.6 5.1 %collective-permute-start.12 = (bf16[448,128]{1,0:T(8,128)(2,1)S(1)}, bf16[448,128]{1,0:T(8,128)(2,1)S(1)}, u32[]{:S(2)}, u32[]{:S(2)}) collective-permute-start(bf16[448,128]{1,0:T(8,128)(2,1)S(1)} %get-tuple-element.107), channel_id=1, source_target_pairs={{0,16},{1,17},{2,18},{3,19},{4,20},{5,21},{6,22},{7,23},{8,24},{9,... | collective-permute-start | bytes 344072 | tf_op jit(solution)/shard_map/ppermute | solution.py:616
  37.8 7.3 %collective-permute-start.13 = (bf16[448,128]{1,0:T(8,128)(2,1)S(1)}, bf16[448,128]{1,0:T(8,128)(2,1)S(1)}, u32[]{:S(2)}, u32[]{:S(2)}) collective-permute-start(bf16[448,128]{1,0:T(8,128)(2,1)S(1)} %get-tuple-element.108), channel_id=1, source_target_pairs={{0,17},{1,16},{2,19},{3,18},{4,21},{5,20},{6,23},{7,22},{8,25},{9,... | collective-permute-start | bytes 344072 | tf_op jit(solution)/shard_map/ppermute | solution.py:616
  45.2 6.1 %collective-permute-start.14 = (bf16[224,128]{1,0:T(8,128)(2,1)S(1)}, bf16[224,128]{1,0:T(8,128)(2,1)S(1)}, u32[]{:S(2)}, u32[]{:S(2)}) collective-permute-start(bf16[224,128]{1,0:T(8,128)(2,1)S(1)} %get-tuple-element.111), channel_id=1, source_target_pairs={{0,6},{1,7},{2,4},{3,5},{4,2},{5,3},{6,0},{7,1},{8,14},{9,15},{10,... | collective-permute-start | bytes 172040 | tf_op jit(solution)/shard_map/ppermute | solution.py:616
  48.2 5.1 %collective-permute-start.15 = (bf16[224,128]{1,0:T(8,128)(2,1)S(1)}, bf16[224,128]{1,0:T(8,128)(2,1)S(1)}, u32[]{:S(2)}, u32[]{:S(2)}) collective-permute-start(bf16[224,128]{1,0:T(8,128)(2,1)S(1)} %get-tuple-element.112), channel_id=1, source_target_pairs={{0,4},{1,5},{2,6},{3,7},{4,0},{5,1},{6,2},{7,3},{8,12},{9,13},{10,... | collective-permute-start | bytes 172040 | tf_op jit(solution)/shard_map/ppermute | solution.py:616
  48.2 5.1 %collective-permute-start.16 = (bf16[224,128]{1,0:T(8,128)(2,1)S(1)}, bf16[224,128]{1,0:T(8,128)(2,1)S(1)}, u32[]{:S(2)}, u32[]{:S(2)}) collective-permute-start(bf16[224,128]{1,0:T(8,128)(2,1)S(1)} %get-tuple-element.113), channel_id=1, source_target_pairs={{0,2},{1,3},{2,0},{3,1},{4,6},{5,7},{6,4},{7,5},{8,10},{9,11},{10,... | collective-permute-start | bytes 172040 | tf_op jit(solution)/shard_map/ppermute | solution.py:616
  53.4 6.0 %collective-permute-start.19 = (bf16[224,128]{1,0:T(8,128)(2,1)S(1)}, bf16[224,128]{1,0:T(8,128)(2,1)S(1)}, u32[]{:S(2)}, u32[]{:S(2)}) collective-permute-start(bf16[224,128]{1,0:T(8,128)(2,1)S(1)} %shard_map.126.refs_0_), channel_id=1, source_target_pairs={{0,6},{1,7},{2,4},{3,5},{4,2},{5,3},{6,0},{7,1},{8,14},{9,15},{10,... | collective-permute-start | bytes 172040 | tf_op jit(solution)/shard_map/ppermute | solution.py:616
  55.5 5.7 %collective-permute-start.18 = (bf16[224,128]{1,0:T(8,128)(2,1)S(1)}, bf16[224,128]{1,0:T(8,128)(2,1)S(1)}, u32[]{:S(2)}, u32[]{:S(2)}) collective-permute-start(bf16[224,128]{1,0:T(8,128)(2,1)S(1)} %shard_map.126.refs_0_), channel_id=1, source_target_pairs={{0,4},{1,5},{2,6},{3,7},{4,0},{5,1},{6,2},{7,3},{8,12},{9,13},{10,... | collective-permute-start | bytes 172040 | tf_op jit(solution)/shard_map/ppermute | solution.py:616
  55.5 5.6 %collective-permute-start.17 = (bf16[224,128]{1,0:T(8,128)(2,1)S(1)}, bf16[224,128]{1,0:T(8,128)(2,1)S(1)}, u32[]{:S(2)}, u32[]{:S(2)}) collective-permute-start(bf16[224,128]{1,0:T(8,128)(2,1)S(1)} %shard_map.126.refs_0_), channel_id=1, source_target_pairs={{0,2},{1,3},{2,0},{3,1},{4,6},{5,7},{6,4},{7,5},{8,10},{9,11},{10,... | collective-permute-start | bytes 172040 | tf_op jit(solution)/shard_map/ppermute | solution.py:616
  61.2 7.9 %collective-permute-start.25 = (bf16[896,128]{1,0:T(8,128)(2,1)S(1)}, bf16[896,128]{1,0:T(8,128)(2,1)S(1)}, u32[]{:S(2)}, u32[]{:S(2)}) collective-permute-start(bf16[896,128]{1,0:T(8,128)(2,1)S(1)} %shard_map.127.refs_0_), channel_id=1, source_target_pairs={{0,17},{1,16},{2,19},{3,18},{4,21},{5,20},{6,23},{7,22},{8,25},{9,... | collective-permute-start | bytes 688136 | tf_op jit(solution)/shard_map/ppermute | solution.py:616
  62.7 9.1 %collective-permute-start.23 = (bf16[896,128]{1,0:T(8,128)(2,1)S(1)}, bf16[896,128]{1,0:T(8,128)(2,1)S(1)}, u32[]{:S(2)}, u32[]{:S(2)}) collective-permute-start(bf16[896,128]{1,0:T(8,128)(2,1)S(1)} %shard_map.127.refs_0_), channel_id=1, source_target_pairs={{0,16},{1,17},{2,18},{3,19},{4,20},{5,21},{6,22},{7,23},{8,24},{9,... | collective-permute-start | bytes 688136 | tf_op jit(solution)/shard_map/ppermute | solution.py:616
  64.0 7.8 %collective-permute-start.21 = (bf16[896,128]{1,0:T(8,128)(2,1)S(1)}, bf16[896,128]{1,0:T(8,128)(2,1)S(1)}, u32[]{:S(2)}, u32[]{:S(2)}) collective-permute-start(bf16[896,128]{1,0:T(8,128)(2,1)S(1)} %shard_map.127.refs_0_), channel_id=1, source_target_pairs={{0,1},{1,0},{2,3},{3,2},{4,5},{5,4},{6,7},{7,6},{8,9},{9,8},{10,11... | collective-permute-start | bytes 688136 | tf_op jit(solution)/shard_map/ppermute | solution.py:616
  64.7 9.0 %collective-permute-start.20 = (bf16[896,128]{1,0:T(8,128)(2,1)S(1)}, bf16[896,128]{1,0:T(8,128)(2,1)S(1)}, u32[]{:S(2)}, u32[]{:S(2)}) collective-permute-start(bf16[896,128]{1,0:T(8,128)(2,1)S(1)} %shard_map.127.refs_0_), channel_id=1, source_target_pairs={{0,8},{1,9},{2,10},{3,11},{4,12},{5,13},{6,14},{7,15},{8,0},{9,1},... | collective-permute-start | bytes 688136 | tf_op jit(solution)/shard_map/ppermute | solution.py:616
  69.1 4.7 %collective-permute-start.26 = (bf16[896,128]{1,0:T(8,128)(2,1)S(1)}, bf16[896,128]{1,0:T(8,128)(2,1)S(1)}, u32[]{:S(2)}, u32[]{:S(2)}) collective-permute-start(bf16[896,128]{1,0:T(8,128)(2,1)S(1)} %collective-permute-done.25.refs_3_), channel_id=1, source_target_pairs={{0,8},{1,9},{2,10},{3,11},{4,12},{5,13},{6,14},{7,15},{8,0},{9,1},... | collective-permute-start | bytes 688136 | tf_op jit(solution)/shard_map/ppermute | solution.py:616
  71.8 2.0 %collective-permute-start.24 = (bf16[896,128]{1,0:T(8,128)(2,1)S(1)}, bf16[896,128]{1,0:T(8,128)(2,1)S(1)}, u32[]{:S(2)}, u32[]{:S(2)}) collective-permute-start(bf16[896,128]{1,0:T(8,128)(2,1)S(1)} %collective-permute-done.23.refs_2_), channel_id=1, source_target_pairs={{0,8},{1,9},{2,10},{3,11},{4,12},{5,13},{6,14},{7,15},{8,0},{9,1},... | collective-permute-start | bytes 688136 | tf_op jit(solution)/shard_map/ppermute | solution.py:616
  71.8 2.0 %collective-permute-start.22 = (bf16[896,128]{1,0:T(8,128)(2,1)S(1)}, bf16[896,128]{1,0:T(8,128)(2,1)S(1)}, u32[]{:S(2)}, u32[]{:S(2)}) collective-permute-start(bf16[896,128]{1,0:T(8,128)(2,1)S(1)} %collective-permute-done.21.refs_1_), channel_id=1, source_target_pairs={{0,8},{1,9},{2,10},{3,11},{4,12},{5,13},{6,14},{7,15},{8,0},{9,1},... | collective-permute-start | bytes 688136 | tf_op jit(solution)/shard_map/ppermute | solution.py:616
  (3 other events, 11.9 us)

commit v4 on v3

--- a/solution.py
+++ b/solution.py
@@ -443,7 +443,7 @@
 
 def plain_backward(own, above, beside, across, slope, *refs):
     saved, weights = refs[:10], refs[10:14]
-    out, lines, outs, middle, tight = refs[14], refs[15], refs[16:21], refs[21], refs[22]
+    out, keep, send, middle, tight, buffer = refs[14:]
     heads = saved[5].shape[0] // 64
     middle[:, 4:] = own[...]
     middle[:, :4] = above[...].astype(F32)
@@ -460,18 +460,9 @@
         out[f, :, 8 * c : 8 * c + 8, :] = piece
 
     tile_of(grad_field, write)
-    lines[...] = grad_bias
-    for ref, n in zip(outs, (0, 1, 3, 5, 7), strict=True):
-        ref[...] = operands[n]
-
-
-def plain_grads(normed, mixed, attended, resid, two, pre, hidden, grad, lines, mine, one, *refs):
-    two_came, three_came, keep, send, done, buffer = refs
-    kept = (normed, mixed, attended, resid, two, pre, hidden, grad)
-    ahead, behind = fold_bias(lines[...], lines.shape[0] // 64)
-    pack_grads(tuple(ref[...].astype(BF) for ref in kept), ahead, behind, buffer)
+    ahead, behind = fold_bias(grad_bias, heads)
+    pack_grads(operands, ahead, behind, buffer)
     split_core(buffer, keep, send)
-    done[...] = mine[...] + one[...].astype(F32) + two_came[...].astype(F32) + three_came[...].astype(F32)
 
 
 def near_place():
@@ -491,12 +482,20 @@
     cut(total, near_place(), own, sends, (1, 2, 3))
 
 
+def sum_near(mine, one, two, three, out):
+    out[...] = mine[...] + one[...].astype(F32) + two[...].astype(F32) + three[...].astype(F32)
+
+
+def add_core_later(keep, came, other, *rest):
+    add_core(keep, came, *rest)
+
+
 def add_near(count, mine, one, two, three, other, own, *rest):
     sends, total = rest[: count - 1], rest[-1]
     rows = own.shape[0] // 2
     place = lax.axis_index("col") // 2
-    total[...] = mine[...] + one[...].astype(F32) + two[...].astype(F32) + three[...].astype(F32)
     partners = range(count - 1, 0, -1)
+    sum_near(mine, one, two, three, total)
     cut(total, place, own, sends, partners, slice(0, rows))
     cut(other, place, own, sends, partners, slice(rows, 2 * rows))
 
@@ -680,24 +679,21 @@
     summed = [((size // 2, 128), F32)]
     shifted = call(add_core, quarters, summed, [keep, swap(away, 1, 0)])
     kept[0], *shifted = lax.optimization_barrier((kept[0], *shifted))
-    shifted = near(*shifted)
-    operands = [((n, tokens), BF) for n in (width, 3 * width, width, inner, width)]
-    input_grad, *given = call(
+    (other,) = call(sum_near, [(eighth, F32)], [], near(*shifted), micros=4.0)
+    input_grad, keep, away = call(
         plain_backward,
-        [(tile, F32), lines, *operands],
-        [(tile, F32), tight],
+        [(tile, F32), *halves],
+        [(tile, F32), tight, buffer],
         [*back, *kept],
         [(w, 0) for w in weights],
-        micros=3.2,
-    )
-    given = [given[1], given[2], kept[7], given[3], kept[8], given[4], kept[10], given[5], given[0]]
-    keep, away, other = call(plain_grads, [*halves, (eighth, F32)], [buffer], [*given, *shifted])
-    plain = call(add_core, quarters, summed, [keep, swap(away, 1, 0)])
+        micros=3.5,
+    )
+    plain = near(*call(add_core_later, quarters, summed, [keep, swap(away, 1, 0), other]))
     own, *sends = call(
         functools.partial(add_near, far),
         [(piece, F32)] + [(piece, BF)] * (far - 1),
         [(eighth, F32)],
-        [*near(*plain), other],
+        [*plain, other],
     )
     distant = [own] + [swap(one, 0, 2 * d) for d, one in zip(range(far - 1, 0, -1), sends, strict=True)]
     (done,) = call(add_far, [(piece, BF)], [], distant)

time: 75.6 us -> 72.8 us (0.963)
  waiting for transfers between devices: 26.1 us -> 23.8 us
    ppermute x21, waiting for transfers between devices: 21.9 us -> 19.7 us  [swap(): return lax.ppermute(block, axes, route)]
  transfers between devices with their start and end apart: 27 -> 27, of which waited for: 14 -> 15; matrix products, arithmetic and copies ran while one was open for 0% -> 0% of each run, Pallas kernels for 9% -> 10%
where the time goes in v4:
time: 72.8 us; the launch traced here: 72.7 us
  starting transfers between devices  29.6 us (41%)
  waiting for transfers between devices  23.8 us (33%)
  Pallas kernels  18.2 us (25%)
  between operations  0.98 us (1%)
    ppermute x21, waiting for transfers between devices, swap(): return lax.ppermute(block, axes, route)  19.7 us
    ppermute x21, starting transfers between devices, swap(): return lax.ppermute(block, axes, route)  19.2 us
    pallas_call x12, Pallas kernels, call(): pl.pallas_call(body, in_specs=[here] * (count + len(stacked)) + [there] *...  18.2 us
    ppermute x6, starting transfers between devices, send(): return lax.ppermute(block, axes, route)  10.3 us
    ppermute x6, waiting for transfers between devices, send(): return lax.ppermute(block, axes, route)  4.16 us
  transfers between devices with their start and end apart: 27, of which 15 were waited for; matrix products, arithmetic and copies ran while one was open for 0% of the time, Pallas kernels for 10%

profile of v4, /device:TPU:0, one launch (start us, length us, event | category | flops | bytes accessed | tf_op | source)
XLA Modules:
  0.0 72.7 jit_solution(17491053580586509020)
XLA Ops:
  0.7 4.6 %shard_map.118 = (f32[2,4,16,192]{3,2,1,0:T(8,128)}, bf16[2,2,4,16,192]{4,3,2,1,0:T(8,128)(2,1)}, bf16[64,192]{1,0:T(8,128)(2,1)}, bf16[64,192]{1,0:T(8,128)(2,1)}) custom-call(bf16[2,8,16,192]{3,2,1,0:T(8,128)(2,1)} %refs_0_.3, bf16[2,8,16,192]{3,2,1,0:T(8,128)(2,1)} %refs_1_.3, f32[6,2,225]{2,1,0:T(2,128)} %bitcast.7, bf16[2,192,576]{2,1,0:T(8,128)(2,1)} %refs_15_.1, ...), custom_call_target="tpu_custom_call" | custom-call | flops 2529999872 | tf_op jit(solution)/shard_map/pallas_call | solution.py:580
  5.3 6.1 %collective-permute-start.1 = (bf16[64,192]{1,0:T(8,128)(2,1)}, bf16[64,192]{1,0:T(8,128)(2,1)S(1)}, u32[]{:S(2)}, u32[]{:S(2)}) collective-permute-start(bf16[64,192]{1,0:T(8,128)(2,1)} %get-tuple-element.60), channel_id=1, source_target_pairs={{0,7},{1,0},{2,1},{3,2},{4,3},{5,4},{6,5},{7,6},{8,15},{9,8},{10,9... | collective-permute-start | bytes 73736 | tf_op jit(solution)/shard_map/ppermute | solution.py:609
  12.0 1.1 %collective-permute-start = (bf16[2,2,4,16,192]{4,3,2,1,0:T(8,128)(2,1)}, bf16[2,2,4,16,192]{4,3,2,1,0:T(8,128)(2,1)S(1)}, u32[]{:S(2)}, u32[]{:S(2)}) collective-permute-start(bf16[2,2,4,16,192]{4,3,2,1,0:T(8,128)(2,1)} %get-tuple-element.59), channel_id=1, source_target_pairs={{0,24},{1,25},{2,26},{3,27},{4,28},{5,29},{6,30},{7,31},{8,0},{9,1... | collective-permute-start | bytes 294920 | tf_op jit(solution)/shard_map/ppermute | solution.py:609
  13.1 2.3 %shard_map.119 = (f32[384,128]{1,0:T(8,128)S(1)}, f32[768,256]{1,0:T(8,128)S(1)}, f32[192,256]{1,0:T(8,128)S(1)}, f32[1,256]{1,0:T(1,128)S(1)}, bf16[192,256]{1,...) custom-call(bf16[2,8,16,192]{3,2,1,0:T(8,128)(2,1)S(1)} %copy-done.4, ...), custom_call_target="tpu_custom_call" | custom-call | flops 2529999872 | tf_op jit(solution)/shard_map/pallas_call | solution.py:580
  15.9 4.4 %shard_map.120 = (f32[2,4,16,192]{3,2,1,0:T(8,128)S(1)}, bf16[2,4,16,192]{3,2,1,0:T(8,128)(2,1)S(1)}, bf16[32,192]{1,0:T(8,128)(2,1)S(1)}, bf16[32,192]{1,0:T(8,...) custom-call(f32[2,4,16,192]{3,2,1,0:T(8,128)S(1)} %copy-done.7, ...), custom_call_target="tpu_custom_call" | custom-call | flops 5280000000 | tf_op jit(solution)/shard_map/pallas_call | solution.py:580
  21.1 1.5 %collective-permute-start.4 = (bf16[32,192]{1,0:T(8,128)(2,1)S(1)}, bf16[32,192]{1,0:T(8,128)(2,1)S(1)}, u32[]{:S(2)}, u32[]{:S(2)}) collective-permute-start(bf16[32,192]{1,0:T(8,128)(2,1)S(1)} %get-tuple-element.65), channel_id=1, source_target_pairs={{0,1},{1,2},{2,3},{3,4},{4,5},{5,6},{6,7},{7,0},{8,9},{9,10},{10,1... | collective-permute-start | bytes 36872 | tf_op jit(solution)/shard_map/ppermute | solution.py:609
  22.6 1.0 %collective-permute-start.3 = (bf16[2,4,16,192]{3,2,1,0:T(8,128)(2,1)S(1)}, bf16[2,4,16,192]{3,2,1,0:T(8,128)(2,1)S(1)}, u32[]{:S(2)}, u32[]{:S(2)}) collective-permute-start(bf16[2,4,16,192]{3,2,1,0:T(8,128)(2,1)S(1)} %get-tuple-element.64), channel_id=1, source_target_pairs={{0,8},{1,9},{2,10},{3,11},{4,12},{5,13},{6,14},{7,15},{8,16},{9,17... | collective-permute-start | bytes 147464 | tf_op jit(solution)/shard_map/ppermute | solution.py:609
  24.3 1.5 %collective-permute-start.9 = (bf16[448,128]{1,0:T(8,128)(2,1)S(1)}, bf16[448,128]{1,0:T(8,128)(2,1)S(1)}, u32[]{:S(2)}, u32[]{:S(2)}) collective-permute-start(bf16[448,128]{1,0:T(8,128)(2,1)S(1)} %get-tuple-element.90), channel_id=1, source_target_pairs={{0,16},{1,17},{2,18},{3,19},{4,20},{5,21},{6,22},{7,23},{8,24},{9,... | collective-permute-start | bytes 344072 | tf_op jit(solution)/shard_map/ppermute | solution.py:615
  25.8 1.8 %collective-permute-done.4.refs_2_ = bf16[32,192]{1,0:T(8,128)(2,1)S(1)} collective-permute-done((bf16[32,192]{1,0:T(8,128)(2,1)S(1)}, bf16[32,192]{1,0:T(8,128)(2,1)S(1)}, u32[]{:S(2)}, u32[]{:S(2)}) %collective-permute-start.4) | collective-permute-done | bytes 12320 | tf_op jit(solution)/shard_map/ppermute | solution.py:609
  27.6 1.9 %collective-permute-done.5.refs_3_ = bf16[32,192]{1,0:T(8,128)(2,1)S(1)} collective-permute-done((bf16[32,192]{1,0:T(8,128)(2,1)S(1)}, bf16[32,192]{1,0:T(8,128)(2,1)S(1)}, u32[]{:S(2)}, u32[]{:S(2)}) %collective-permute-start.5) | collective-permute-done | bytes 12320 | tf_op jit(solution)/shard_map/ppermute | solution.py:609
  29.5 3.4 %shard_map.122 = (f32[2,8,16,192]{3,2,1,0:T(8,128)}, bf16[1792,128]{1,0:T(8,128)(2,1)S(1)}, bf16[1792,128]{1,0:T(8,128)(2,1)S(1)}) custom-call(f32[2,4,16,192]{3,2,1,0:T(8,128)S(1)} %get-tuple-element.63.refs_0_, bf16[2,4,16,192]{3,2,1,0:T(8,128)(2,1)S(1)} %collective-permute-done.3.refs_1_, bf16[32,192]{1,0:T(8,128)(2,1)S(1)} %collective-permute-done.4.refs_2_, ...), custom_call_target="tpu_custom_call" | custom-call | flops 3849999872 | tf_op jit(solution)/shard_map/pallas_call | solution.py:580
  33.4 1.4 %collective-permute-done.7.refs_1_ = bf16[1792,128]{1,0:T(8,128)(2,1)S(1)} collective-permute-done((bf16[1792,128]{1,0:T(8,128)(2,1)S(1)}, bf16[1792,128]{1,0:T(8,128)(2,1)S(1)}, u32[]{:S(2)}, u32[]{:S(2)}) %collective-permute-start.7) | collective-permute-done | bytes 458784 | tf_op jit(solution)/shard_map/ppermute | solution.py:615
  34.9 1.1 %collective-permute-start.11 = (bf16[448,128]{1,0:T(8,128)(2,1)S(1)}, bf16[448,128]{1,0:T(8,128)(2,1)S(1)}, u32[]{:S(2)}, u32[]{:S(2)}) collective-permute-start(bf16[448,128]{1,0:T(8,128)(2,1)S(1)} %get-tuple-element.93), channel_id=1, source_target_pairs={{0,1},{1,0},{2,3},{3,2},{4,5},{5,4},{6,7},{7,6},{8,9},{9,8},{10,11... | collective-permute-start | bytes 344072 | tf_op jit(solution)/shard_map/ppermute | solution.py:615
  36.6 1.9 %collective-permute-start.13 = (bf16[448,128]{1,0:T(8,128)(2,1)S(1)}, bf16[448,128]{1,0:T(8,128)(2,1)S(1)}, u32[]{:S(2)}, u32[]{:S(2)}) collective-permute-start(bf16[448,128]{1,0:T(8,128)(2,1)S(1)} %get-tuple-element.95), channel_id=1, source_target_pairs={{0,17},{1,16},{2,19},{3,18},{4,21},{5,20},{6,23},{7,22},{8,25},{9,... | collective-permute-start | bytes 344072 | tf_op jit(solution)/shard_map/ppermute | solution.py:615
  38.5 1.7 %collective-permute-done.11.refs_1_ = bf16[448,128]{1,0:T(8,128)(2,1)S(1)} collective-permute-done((bf16[448,128]{1,0:T(8,128)(2,1)S(1)}, bf16[448,128]{1,0:T(8,128)(2,1)S(1)}, u32[]{:S(2)}, u32[]{:S(2)}) %collective-permute-start.11) | collective-permute-done | bytes 114720 | tf_op jit(solution)/shard_map/ppermute | solution.py:615
  40.2 1.7 %collective-permute-done.12.refs_2_ = bf16[448,128]{1,0:T(8,128)(2,1)S(1)} collective-permute-done((bf16[448,128]{1,0:T(8,128)(2,1)S(1)}, bf16[448,128]{1,0:T(8,128)(2,1)S(1)}, u32[]{:S(2)}, u32[]{:S(2)}) %collective-permute-start.12) | collective-permute-done | bytes 114720 | tf_op jit(solution)/shard_map/ppermute | solution.py:615
  41.9 2.0 %collective-permute-done.13.refs_3_ = bf16[448,128]{1,0:T(8,128)(2,1)S(1)} collective-permute-done((bf16[448,128]{1,0:T(8,128)(2,1)S(1)}, bf16[448,128]{1,0:T(8,128)(2,1)S(1)}, u32[]{:S(2)}, u32[]{:S(2)}) %collective-permute-start.13) | collective-permute-done | bytes 114720 | tf_op jit(solution)/shard_map/ppermute | solution.py:615
  43.9 1.7 %collective-permute-start.14 = (bf16[224,128]{1,0:T(8,128)(2,1)S(1)}, bf16[224,128]{1,0:T(8,128)(2,1)S(1)}, u32[]{:S(2)}, u32[]{:S(2)}) collective-permute-start(bf16[224,128]{1,0:T(8,128)(2,1)S(1)} %get-tuple-element.97), channel_id=1, source_target_pairs={{0,6},{1,7},{2,4},{3,5},{4,2},{5,3},{6,0},{7,1},{8,14},{9,15},{10,... | collective-permute-start | bytes 172040 | tf_op jit(solution)/shard_map/ppermute | solution.py:615
  45.6 2.7 %collective-permute-start.16 = (bf16[224,128]{1,0:T(8,128)(2,1)S(1)}, bf16[224,128]{1,0:T(8,128)(2,1)S(1)}, u32[]{:S(2)}, u32[]{:S(2)}) collective-permute-start(bf16[224,128]{1,0:T(8,128)(2,1)S(1)} %get-tuple-element.99), channel_id=1, source_target_pairs={{0,2},{1,3},{2,0},{3,1},{4,6},{5,7},{6,4},{7,5},{8,10},{9,11},{10,... | collective-permute-start | bytes 172040 | tf_op jit(solution)/shard_map/ppermute | solution.py:615
  48.4 1.8 %collective-permute-done.14.refs_1_ = bf16[224,128]{1,0:T(8,128)(2,1)S(1)} collective-permute-done((bf16[224,128]{1,0:T(8,128)(2,1)S(1)}, bf16[224,128]{1,0:T(8,128)(2,1)S(1)}, u32[]{:S(2)}, u32[]{:S(2)}) %collective-permute-start.14) | collective-permute-done | bytes 57376 | tf_op jit(solution)/shard_map/ppermute | solution.py:615
  50.2 1.2 %collective-permute-done.15.refs_2_ = bf16[224,128]{1,0:T(8,128)(2,1)S(1)} collective-permute-done((bf16[224,128]{1,0:T(8,128)(2,1)S(1)}, bf16[224,128]{1,0:T(8,128)(2,1)S(1)}, u32[]{:S(2)}, u32[]{:S(2)}) %collective-permute-start.15) | collective-permute-done | bytes 57376 | tf_op jit(solution)/shard_map/ppermute | solution.py:615
  51.4 2.0 %collective-permute-start.19 = (bf16[224,128]{1,0:T(8,128)(2,1)S(1)}, bf16[224,128]{1,0:T(8,128)(2,1)S(1)}, u32[]{:S(2)}, u32[]{:S(2)}) collective-permute-start(bf16[224,128]{1,0:T(8,128)(2,1)S(1)} %shard_map.126.refs_0_), channel_id=1, source_target_pairs={{0,6},{1,7},{2,4},{3,5},{4,2},{5,3},{6,0},{7,1},{8,14},{9,15},{10,... | collective-permute-start | bytes 172040 | tf_op jit(solution)/shard_map/ppermute | solution.py:615
  54.1 1.8 %collective-permute-start.17 = (bf16[224,128]{1,0:T(8,128)(2,1)S(1)}, bf16[224,128]{1,0:T(8,128)(2,1)S(1)}, u32[]{:S(2)}, u32[]{:S(2)}) collective-permute-start(bf16[224,128]{1,0:T(8,128)(2,1)S(1)} %shard_map.126.refs_0_), channel_id=1, source_target_pairs={{0,2},{1,3},{2,0},{3,1},{4,6},{5,7},{6,4},{7,5},{8,10},{9,11},{10,... | collective-permute-start | bytes 172040 | tf_op jit(solution)/shard_map/ppermute | solution.py:615
  55.9 1.6 %collective-permute-done.19.refs_3_ = bf16[224,128]{1,0:T(8,128)(2,1)S(1)} collective-permute-done((bf16[224,128]{1,0:T(8,128)(2,1)S(1)}, bf16[224,128]{1,0:T(8,128)(2,1)S(1)}, u32[]{:S(2)}, u32[]{:S(2)}) %collective-permute-start.19) | collective-permute-done | bytes 57376 | tf_op jit(solution)/shard_map/ppermute | solution.py:615
  57.5 1.3 %collective-permute-done.18.refs_2_ = bf16[224,128]{1,0:T(8,128)(2,1)S(1)} collective-permute-done((bf16[224,128]{1,0:T(8,128)(2,1)S(1)}, bf16[224,128]{1,0:T(8,128)(2,1)S(1)}, u32[]{:S(2)}, u32[]{:S(2)}) %collective-permute-start.18) | collective-permute-done | bytes 57376 | tf_op jit(solution)/shard_map/ppermute | solution.py:615
  58.9 1.5 %collective-permute-start.25 = (bf16[896,128]{1,0:T(8,128)(2,1)S(1)}, bf16[896,128]{1,0:T(8,128)(2,1)S(1)}, u32[]{:S(2)}, u32[]{:S(2)}) collective-permute-start(bf16[896,128]{1,0:T(8,128)(2,1)S(1)} %shard_map.127.refs_0_), channel_id=1, source_target_pairs={{0,17},{1,16},{2,19},{3,18},{4,21},{5,20},{6,23},{7,22},{8,25},{9,... | collective-permute-start | bytes 688136 | tf_op jit(solution)/shard_map/ppermute | solution.py:615
  60.5 1.2 %collective-permute-start.23 = (bf16[896,128]{1,0:T(8,128)(2,1)S(1)}, bf16[896,128]{1,0:T(8,128)(2,1)S(1)}, u32[]{:S(2)}, u32[]{:S(2)}) collective-permute-start(bf16[896,128]{1,0:T(8,128)(2,1)S(1)} %shard_map.127.refs_0_), channel_id=1, source_target_pairs={{0,16},{1,17},{2,18},{3,19},{4,20},{5,21},{6,22},{7,23},{8,24},{9,... | collective-permute-start | bytes 688136 | tf_op jit(solution)/shard_map/ppermute | solution.py:615
  61.7 0.8 %collective-permute-start.21 = (bf16[896,128]{1,0:T(8,128)(2,1)S(1)}, bf16[896,128]{1,0:T(8,128)(2,1)S(1)}, u32[]{:S(2)}, u32[]{:S(2)}) collective-permute-start(bf16[896,128]{1,0:T(8,128)(2,1)S(1)} %shard_map.127.refs_0_), channel_id=1, source_target_pairs={{0,1},{1,0},{2,3},{3,2},{4,5},{5,4},{6,7},{7,6},{8,9},{9,8},{10,11... | collective-permute-start | bytes 688136 | tf_op jit(solution)/shard_map/ppermute | solution.py:615
  62.5 3.7 %collective-permute-done.25.refs_3_ = bf16[896,128]{1,0:T(8,128)(2,1)S(1)} collective-permute-done((bf16[896,128]{1,0:T(8,128)(2,1)S(1)}, bf16[896,128]{1,0:T(8,128)(2,1)S(1)}, u32[]{:S(2)}, u32[]{:S(2)}) %collective-permute-start.25) | collective-permute-done | bytes 229408 | tf_op jit(solution)/shard_map/ppermute | solution.py:615
  66.3 2.8 %collective-permute-done.23.refs_2_ = bf16[896,128]{1,0:T(8,128)(2,1)S(1)} collective-permute-done((bf16[896,128]{1,0:T(8,128)(2,1)S(1)}, bf16[896,128]{1,0:T(8,128)(2,1)S(1)}, u32[]{:S(2)}, u32[]{:S(2)}) %collective-permute-start.23) | collective-permute-done | bytes 229408 | tf_op jit(solution)/shard_map/ppermute | solution.py:615
  69.5 1.5 %shard_map.128 = (f32[2,192,576]{2,1,0:T(8,128)}, f32[2,192,192]{2,1,0:T(8,128)}, f32[2,192,768]{2,1,0:T(8,128)}, f32[2,192,768]{2,1,0:T(8,128)}, f32[6,2,225]{2,1,0:T(2,128)}) custom-call(bf16[896,128]{1,0:T(8,128)(2,1)S(1)} %shard_map.127.refs_0_, bf16[896,128]{1,0:T(8,128)(2,1)S(1)} %collective-permute-done.21.refs_1_, ...), custom_call_target="tpu_custom_call" | custom-call | flops 1320000000 | tf_op jit(solution)/shard_map/pallas_call | solution.py:580
  71.1 1.5 %shard_map.129 = (f32[2,192,576]{2,1,0:T(8,128)}, f32[2,192,192]{2,1,0:T(8,128)}, f32[2,192,768]{2,1,0:T(8,128)}, f32[2,192,768]{2,1,0:T(8,128)}, f32[6,2,225]{2,1,0:T(2,128)}) custom-call(bf16[896,128]{1,0:T(8,128)(2,1)S(1)} %collective-permute-done.20.refs_0_, ...), custom_call_target="tpu_custom_call", output_to_operand_aliasing={{0}: (4, {}), {1}: (5, {}), {2}: (6, {}), {3}: (7, {}), {4}... | custom-call | flops 1320000000 | tf_op jit(solution)/shard_map/pallas_call | solution.py:580
  (50 shorter events, 5.1 us)
Async XLA Ops:
  0.6 12.5 %copy-start = (bf16[2,192,768]{2,1,0:T(8,128)(2,1)S(1)}, bf16[2,192,768]{2,1,0:T(8,128)(2,1)}, u32[]{:S(2)}) copy-start(bf16[2,192,768]{2,1,0:T(8,128)(2,1)} %refs_17_.1) | copy-start | bytes 1769476
  0.6 12.4 %copy-start.2 = (bf16[2,192,576]{2,1,0:T(8,128)(2,1)S(1)}, bf16[2,192,576]{2,1,0:T(8,128)(2,1)}, u32[]{:S(2)}) copy-start(bf16[2,192,576]{2,1,0:T(8,128)(2,1)} %refs_15_.1) | copy-start | bytes 1327108
  0.7 12.4 %copy-start.3 = (bf16[2,192,192]{2,1,0:T(8,128)(2,1)S(1)}, bf16[2,192,192]{2,1,0:T(8,128)(2,1)}, u32[]{:S(2)}) copy-start(bf16[2,192,192]{2,1,0:T(8,128)(2,1)} %refs_16_.1) | copy-start | bytes 442372
  0.7 12.4 %copy-start.4 = (bf16[2,8,16,192]{3,2,1,0:T(8,128)(2,1)S(1)}, bf16[2,8,16,192]{3,2,1,0:T(8,128)(2,1)}, u32[]{:S(2)}) copy-start(bf16[2,8,16,192]{3,2,1,0:T(8,128)(2,1)} %refs_0_.3) | copy-start | bytes 294916
  0.7 12.4 %copy-start.6 = (f32[2,6,225]{2,0,1:T(2,128)S(1)}, f32[2,6,225]{2,0,1:T(2,128)}, u32[]{:S(2)}) copy-start(f32[2,6,225]{2,0,1:T(2,128)} %param.13) | copy-start | bytes 32404
  5.3 10.2 %collective-permute-start.1 = (bf16[64,192]{1,0:T(8,128)(2,1)}, bf16[64,192]{1,0:T(8,128)(2,1)S(1)}, u32[]{:S(2)}, u32[]{:S(2)}) collective-permute-start(bf16[64,192]{1,0:T(8,128)(2,1)} %get-tuple-element.60), channel_id=1, source_target_pairs={{0,7},{1,0},{2,1},{3,2},{4,3},{5,4},{6,5},{7,6},{8,15},{9,8},{10,9... | collective-permute-start | bytes 73736 | tf_op jit(solution)/shard_map/ppermute | solution.py:609
  11.4 4.1 %collective-permute-start.2 = (bf16[64,192]{1,0:T(8,128)(2,1)}, bf16[64,192]{1,0:T(8,128)(2,1)S(1)}, u32[]{:S(2)}, u32[]{:S(2)}) collective-permute-start(bf16[64,192]{1,0:T(8,128)(2,1)} %get-tuple-element.61), channel_id=1, source_target_pairs={{0,31},{1,24},{2,25},{3,26},{4,27},{5,28},{6,29},{7,30},{8,7},{9,0... | collective-permute-start | bytes 73736 | tf_op jit(solution)/shard_map/ppermute | solution.py:609
  12.0 4.0 %collective-permute-start = (bf16[2,2,4,16,192]{4,3,2,1,0:T(8,128)(2,1)}, bf16[2,2,4,16,192]{4,3,2,1,0:T(8,128)(2,1)S(1)}, u32[]{:S(2)}, u32[]{:S(2)}) collective-permute-start(bf16[2,2,4,16,192]{4,3,2,1,0:T(8,128)(2,1)} %get-tuple-element.59), channel_id=1, source_target_pairs={{0,24},{1,25},{2,26},{3,27},{4,28},{5,29},{6,30},{7,31},{8,0},{9,1... | collective-permute-start | bytes 294920 | tf_op jit(solution)/shard_map/ppermute | solution.py:609
  20.3 3.3 %collective-permute-start.6 = (bf16[1792,128]{1,0:T(8,128)(2,1)S(1)}, bf16[1792,128]{1,0:T(8,128)(2,1)S(1)}, u32[]{:S(2)}, u32[]{:S(2)}) collective-permute-start(bf16[1792,128]{1,0:T(8,128)(2,1)S(1)} %get-tuple-element.69), channel_id=1, source_target_pairs={{0,8},{1,9},{2,10},{3,11},{4,12},{5,13},{6,14},{7,15},{8,0},{9,1},... | collective-permute-start | bytes 1376264 | tf_op jit(solution)/shard_map/ppermute | solution.py:615
  21.1 6.5 %collective-permute-start.4 = (bf16[32,192]{1,0:T(8,128)(2,1)S(1)}, bf16[32,192]{1,0:T(8,128)(2,1)S(1)}, u32[]{:S(2)}, u32[]{:S(2)}) collective-permute-start(bf16[32,192]{1,0:T(8,128)(2,1)S(1)} %get-tuple-element.65), channel_id=1, source_target_pairs={{0,1},{1,2},{2,3},{3,4},{4,5},{5,6},{6,7},{7,0},{8,9},{9,10},{10,1... | collective-permute-start | bytes 36872 | tf_op jit(solution)/shard_map/ppermute | solution.py:609
  22.6 6.9 %collective-permute-start.5 = (bf16[32,192]{1,0:T(8,128)(2,1)S(1)}, bf16[32,192]{1,0:T(8,128)(2,1)S(1)}, u32[]{:S(2)}, u32[]{:S(2)}) collective-permute-start(bf16[32,192]{1,0:T(8,128)(2,1)S(1)} %get-tuple-element.66), channel_id=1, source_target_pairs={{0,9},{1,10},{2,11},{3,12},{4,13},{5,14},{6,15},{7,8},{8,17},{9,18... | collective-permute-start | bytes 36872 | tf_op jit(solution)/shard_map/ppermute | solution.py:609
  22.6 6.9 %collective-permute-start.3 = (bf16[2,4,16,192]{3,2,1,0:T(8,128)(2,1)S(1)}, bf16[2,4,16,192]{3,2,1,0:T(8,128)(2,1)S(1)}, u32[]{:S(2)}, u32[]{:S(2)}) collective-permute-start(bf16[2,4,16,192]{3,2,1,0:T(8,128)(2,1)S(1)} %get-tuple-element.64), channel_id=1, source_target_pairs={{0,8},{1,9},{2,10},{3,11},{4,12},{5,13},{6,14},{7,15},{8,16},{9,17... | collective-permute-start | bytes 147464 | tf_op jit(solution)/shard_map/ppermute | solution.py:609
  23.8 9.1 %collective-permute-start.8 = (bf16[448,128]{1,0:T(8,128)(2,1)S(1)}, bf16[448,128]{1,0:T(8,128)(2,1)S(1)}, u32[]{:S(2)}, u32[]{:S(2)}) collective-permute-start(bf16[448,128]{1,0:T(8,128)(2,1)S(1)} %get-tuple-element.89), channel_id=1, source_target_pairs={{0,1},{1,0},{2,3},{3,2},{4,5},{5,4},{6,7},{7,6},{8,9},{9,8},{10,11... | collective-permute-start | bytes 344072 | tf_op jit(solution)/shard_map/ppermute | solution.py:615
  24.3 8.6 %collective-permute-start.9 = (bf16[448,128]{1,0:T(8,128)(2,1)S(1)}, bf16[448,128]{1,0:T(8,128)(2,1)S(1)}, u32[]{:S(2)}, u32[]{:S(2)}) collective-permute-start(bf16[448,128]{1,0:T(8,128)(2,1)S(1)} %get-tuple-element.90), channel_id=1, source_target_pairs={{0,16},{1,17},{2,18},{3,19},{4,20},{5,21},{6,22},{7,23},{8,24},{9,... | collective-permute-start | bytes 344072 | tf_op jit(solution)/shard_map/ppermute | solution.py:615
  27.6 5.7 %collective-permute-start.10 = (bf16[448,128]{1,0:T(8,128)(2,1)S(1)}, bf16[448,128]{1,0:T(8,128)(2,1)S(1)}, u32[]{:S(2)}, u32[]{:S(2)}) collective-permute-start(bf16[448,128]{1,0:T(8,128)(2,1)S(1)} %get-tuple-element.91), channel_id=1, source_target_pairs={{0,17},{1,16},{2,19},{3,18},{4,21},{5,20},{6,23},{7,22},{8,25},{9,... | collective-permute-start | bytes 344072 | tf_op jit(solution)/shard_map/ppermute | solution.py:615
  32.9 1.8 %collective-permute-start.7 = (bf16[1792,128]{1,0:T(8,128)(2,1)S(1)}, bf16[1792,128]{1,0:T(8,128)(2,1)S(1)}, u32[]{:S(2)}, u32[]{:S(2)}) collective-permute-start(bf16[1792,128]{1,0:T(8,128)(2,1)S(1)} %get-tuple-element.87), channel_id=1, source_target_pairs={{0,8},{1,9},{2,10},{3,11},{4,12},{5,13},{6,14},{7,15},{8,0},{9,1},... | collective-permute-start | bytes 1376264 | tf_op jit(solution)/shard_map/ppermute | solution.py:615
  34.9 5.3 %collective-permute-start.11 = (bf16[448,128]{1,0:T(8,128)(2,1)S(1)}, bf16[448,128]{1,0:T(8,128)(2,1)S(1)}, u32[]{:S(2)}, u32[]{:S(2)}) collective-permute-start(bf16[448,128]{1,0:T(8,128)(2,1)S(1)} %get-tuple-element.93), channel_id=1, source_target_pairs={{0,1},{1,0},{2,3},{3,2},{4,5},{5,4},{6,7},{7,6},{8,9},{9,8},{10,11... | collective-permute-start | bytes 344072 | tf_op jit(solution)/shard_map/ppermute | solution.py:615
  36.1 5.8 %collective-permute-start.12 = (bf16[448,128]{1,0:T(8,128)(2,1)S(1)}, bf16[448,128]{1,0:T(8,128)(2,1)S(1)}, u32[]{:S(2)}, u32[]{:S(2)}) collective-permute-start(bf16[448,128]{1,0:T(8,128)(2,1)S(1)} %get-tuple-element.94), channel_id=1, source_target_pairs={{0,16},{1,17},{2,18},{3,19},{4,20},{5,21},{6,22},{7,23},{8,24},{9,... | collective-permute-start | bytes 344072 | tf_op jit(solution)/shard_map/ppermute | solution.py:615
  36.6 7.2 %collective-permute-start.13 = (bf16[448,128]{1,0:T(8,128)(2,1)S(1)}, bf16[448,128]{1,0:T(8,128)(2,1)S(1)}, u32[]{:S(2)}, u32[]{:S(2)}) collective-permute-start(bf16[448,128]{1,0:T(8,128)(2,1)S(1)} %get-tuple-element.95), channel_id=1, source_target_pairs={{0,17},{1,16},{2,19},{3,18},{4,21},{5,20},{6,23},{7,22},{8,25},{9,... | collective-permute-start | bytes 344072 | tf_op jit(solution)/shard_map/ppermute | solution.py:615
  43.9 6.3 %collective-permute-start.14 = (bf16[224,128]{1,0:T(8,128)(2,1)S(1)}, bf16[224,128]{1,0:T(8,128)(2,1)S(1)}, u32[]{:S(2)}, u32[]{:S(2)}) collective-permute-start(bf16[224,128]{1,0:T(8,128)(2,1)S(1)} %get-tuple-element.97), channel_id=1, source_target_pairs={{0,6},{1,7},{2,4},{3,5},{4,2},{5,3},{6,0},{7,1},{8,14},{9,15},{10,... | collective-permute-start | bytes 172040 | tf_op jit(solution)/shard_map/ppermute | solution.py:615
  45.6 5.8 %collective-permute-start.15 = (bf16[224,128]{1,0:T(8,128)(2,1)S(1)}, bf16[224,128]{1,0:T(8,128)(2,1)S(1)}, u32[]{:S(2)}, u32[]{:S(2)}) collective-permute-start(bf16[224,128]{1,0:T(8,128)(2,1)S(1)} %get-tuple-element.98), channel_id=1, source_target_pairs={{0,4},{1,5},{2,6},{3,7},{4,0},{5,1},{6,2},{7,3},{8,12},{9,13},{10,... | collective-permute-start | bytes 172040 | tf_op jit(solution)/shard_map/ppermute | solution.py:615
  45.6 5.8 %collective-permute-start.16 = (bf16[224,128]{1,0:T(8,128)(2,1)S(1)}, bf16[224,128]{1,0:T(8,128)(2,1)S(1)}, u32[]{:S(2)}, u32[]{:S(2)}) collective-permute-start(bf16[224,128]{1,0:T(8,128)(2,1)S(1)} %get-tuple-element.99), channel_id=1, source_target_pairs={{0,2},{1,3},{2,0},{3,1},{4,6},{5,7},{6,4},{7,5},{8,10},{9,11},{10,... | collective-permute-start | bytes 172040 | tf_op jit(solution)/shard_map/ppermute | solution.py:615
  51.4 6.0 %collective-permute-start.19 = (bf16[224,128]{1,0:T(8,128)(2,1)S(1)}, bf16[224,128]{1,0:T(8,128)(2,1)S(1)}, u32[]{:S(2)}, u32[]{:S(2)}) collective-permute-start(bf16[224,128]{1,0:T(8,128)(2,1)S(1)} %shard_map.126.refs_0_), channel_id=1, source_target_pairs={{0,6},{1,7},{2,4},{3,5},{4,2},{5,3},{6,0},{7,1},{8,14},{9,15},{10,... | collective-permute-start | bytes 172040 | tf_op jit(solution)/shard_map/ppermute | solution.py:615
  53.5 5.3 %collective-permute-start.18 = (bf16[224,128]{1,0:T(8,128)(2,1)S(1)}, bf16[224,128]{1,0:T(8,128)(2,1)S(1)}, u32[]{:S(2)}, u32[]{:S(2)}) collective-permute-start(bf16[224,128]{1,0:T(8,128)(2,1)S(1)} %shard_map.126.refs_0_), channel_id=1, source_target_pairs={{0,4},{1,5},{2,6},{3,7},{4,0},{5,1},{6,2},{7,3},{8,12},{9,13},{10,... | collective-permute-start | bytes 172040 | tf_op jit(solution)/shard_map/ppermute | solution.py:615
  54.1 4.8 %collective-permute-start.17 = (bf16[224,128]{1,0:T(8,128)(2,1)S(1)}, bf16[224,128]{1,0:T(8,128)(2,1)S(1)}, u32[]{:S(2)}, u32[]{:S(2)}) collective-permute-start(bf16[224,128]{1,0:T(8,128)(2,1)S(1)} %shard_map.126.refs_0_), channel_id=1, source_target_pairs={{0,2},{1,3},{2,0},{3,1},{4,6},{5,7},{6,4},{7,5},{8,10},{9,11},{10,... | collective-permute-start | bytes 172040 | tf_op jit(solution)/shard_map/ppermute | solution.py:615
  58.9 7.3 %collective-permute-start.25 = (bf16[896,128]{1,0:T(8,128)(2,1)S(1)}, bf16[896,128]{1,0:T(8,128)(2,1)S(1)}, u32[]{:S(2)}, u32[]{:S(2)}) collective-permute-start(bf16[896,128]{1,0:T(8,128)(2,1)S(1)} %shard_map.127.refs_0_), channel_id=1, source_target_pairs={{0,17},{1,16},{2,19},{3,18},{4,21},{5,20},{6,23},{7,22},{8,25},{9,... | collective-permute-start | bytes 688136 | tf_op jit(solution)/shard_map/ppermute | solution.py:615
  60.5 8.6 %collective-permute-start.23 = (bf16[896,128]{1,0:T(8,128)(2,1)S(1)}, bf16[896,128]{1,0:T(8,128)(2,1)S(1)}, u32[]{:S(2)}, u32[]{:S(2)}) collective-permute-start(bf16[896,128]{1,0:T(8,128)(2,1)S(1)} %shard_map.127.refs_0_), channel_id=1, source_target_pairs={{0,16},{1,17},{2,18},{3,19},{4,20},{5,21},{6,22},{7,23},{8,24},{9,... | collective-permute-start | bytes 688136 | tf_op jit(solution)/shard_map/ppermute | solution.py:615
  61.7 7.3 %collective-permute-start.21 = (bf16[896,128]{1,0:T(8,128)(2,1)S(1)}, bf16[896,128]{1,0:T(8,128)(2,1)S(1)}, u32[]{:S(2)}, u32[]{:S(2)}) collective-permute-start(bf16[896,128]{1,0:T(8,128)(2,1)S(1)} %shard_map.127.refs_0_), channel_id=1, source_target_pairs={{0,1},{1,0},{2,3},{3,2},{4,5},{5,4},{6,7},{7,6},{8,9},{9,8},{10,11... | collective-permute-start | bytes 688136 | tf_op jit(solution)/shard_map/ppermute | solution.py:615
  62.5 8.5 %collective-permute-start.20 = (bf16[896,128]{1,0:T(8,128)(2,1)S(1)}, bf16[896,128]{1,0:T(8,128)(2,1)S(1)}, u32[]{:S(2)}, u32[]{:S(2)}) collective-permute-start(bf16[896,128]{1,0:T(8,128)(2,1)S(1)} %shard_map.127.refs_0_), channel_id=1, source_target_pairs={{0,8},{1,9},{2,10},{3,11},{4,12},{5,13},{6,14},{7,15},{8,0},{9,1},... | collective-permute-start | bytes 688136 | tf_op jit(solution)/shard_map/ppermute | solution.py:615
  66.3 4.8 %collective-permute-start.26 = (bf16[896,128]{1,0:T(8,128)(2,1)S(1)}, bf16[896,128]{1,0:T(8,128)(2,1)S(1)}, u32[]{:S(2)}, u32[]{:S(2)}) collective-permute-start(bf16[896,128]{1,0:T(8,128)(2,1)S(1)} %collective-permute-done.25.refs_3_), channel_id=1, source_target_pairs={{0,8},{1,9},{2,10},{3,11},{4,12},{5,13},{6,14},{7,15},{8,0},{9,1},... | collective-permute-start | bytes 688136 | tf_op jit(solution)/shard_map/ppermute | solution.py:615
  69.0 2.0 %collective-permute-start.24 = (bf16[896,128]{1,0:T(8,128)(2,1)S(1)}, bf16[896,128]{1,0:T(8,128)(2,1)S(1)}, u32[]{:S(2)}, u32[]{:S(2)}) collective-permute-start(bf16[896,128]{1,0:T(8,128)(2,1)S(1)} %collective-permute-done.23.refs_2_), channel_id=1, source_target_pairs={{0,8},{1,9},{2,10},{3,11},{4,12},{5,13},{6,14},{7,15},{8,0},{9,1},... | collective-permute-start | bytes 688136 | tf_op jit(solution)/shard_map/ppermute | solution.py:615
  69.0 2.0 %collective-permute-start.22 = (bf16[896,128]{1,0:T(8,128)(2,1)S(1)}, bf16[896,128]{1,0:T(8,128)(2,1)S(1)}, u32[]{:S(2)}, u32[]{:S(2)}) collective-permute-start(bf16[896,128]{1,0:T(8,128)(2,1)S(1)} %collective-permute-done.21.refs_1_), channel_id=1, source_target_pairs={{0,8},{1,9},{2,10},{3,11},{4,12},{5,13},{6,14},{7,15},{8,0},{9,1},... | collective-permute-start | bytes 688136 | tf_op jit(solution)/shard_map/ppermute | solution.py:615
  (3 other events, 11.9 us)

commit v5 on v4

--- a/solution.py
+++ b/solution.py
@@ -50,10 +50,13 @@
     def __init__(self, copy, here):
         self.copy, self.here = copy, here
 
-    def __getitem__(self, index):
+    def ready(self):
         if self.copy is not None:
             self.copy.wait()
             self.copy = None
+
+    def __getitem__(self, index):
+        self.ready()
         return self.here[index]
 
 
@@ -192,7 +195,7 @@
 
 
 def backward(weights, saved, slope, grad, heads):
-    qkv_w, proj_w, expand_w, reduce_w = (w[...] for w in weights)
+    proj_w, expand_w, reduce_w = (w[...] for w in weights[1:])
     center, scale, query, keys, values, prob, attended, center_two, scale_two, hidden = saved
     width, tokens = grad.shape
     head = width // heads
@@ -240,10 +243,13 @@
     grad_k = jnp.concatenate(grad_k, axis=1)
     grad_v = jnp.concatenate(grad_v, axis=1)
     grad_mixed = jnp.concatenate([grad_q, grad_k, grad_v], axis=0).astype(BF)
+    operands = (center.astype(BF), grad_mixed, attended, grad_resid_b, center_two.astype(BF), grad_pre, hidden, grad_b)
+    return grad_resid, operands, grad_bias
+
+
+def field_grad(qkv_w, grad_mixed, grad_resid, center, scale):
     grad_normed = dot(qkv_w, grad_mixed).astype(BF).astype(F32)
-    grad_field = grad_resid + norm_back(grad_normed, center, scale)
-    operands = (center.astype(BF), grad_mixed, attended, grad_resid_b, center_two.astype(BF), grad_pre, hidden, grad_b)
-    return grad_field, operands, grad_bias
+    return grad_resid + norm_back(grad_normed, center, scale)
 
 
 def pack_grads(operands, ahead, behind, buffer):
@@ -363,7 +369,12 @@
     def write(f, c, piece):
         whole[f, :, 8 * c : 8 * c + 8, :] = piece
 
-    bias = spread_bias(lambda: table[:, 0, :], table_far.shape[2], heads)
+    def read():
+        for one in (x_ref, qkv):
+            one.ready()
+        return table[:, 0, :]
+
+    bias = spread_bias(read, table_far.shape[2], heads)
     field = tokens_of(lambda f, c: x_ref[f, :, 8 * c : 8 * c + 8, :].astype(F32))
     resid, hidden, _, _, _ = forward((qkv, proj, expand), field, bias, heads)
     tile_of(resid + dot(reduce[...], hidden), write)
@@ -397,7 +408,7 @@
 
 
 def shifted_block(
-    first, cot, below, beside, across, bias, qkv, proj, expand, reduce,
+    first, cot, below, across, beside, bias, qkv, proj, expand, reduce,
     own, bottom, right, corner, keep, send, moved, turned, tight, buffer,
 ):
     heads = bias.shape[0] // 64
@@ -416,7 +427,8 @@
     cotangent = tokens_of(lambda f, c: turned[f, :, 4 + 8 * c : 12 + 8 * c, :])
     weights = (qkv, proj, expand, reduce)
     _, _, pre, bell, saved = forward(weights, field, bias[...], heads)
-    grad_field, operands, grad_bias = backward(weights, saved, slope_of(pre, bell), cotangent, heads)
+    grad_resid, operands, grad_bias = backward(weights, saved, slope_of(pre, bell), cotangent, heads)
+    grad_field = field_grad(qkv[...], operands[1], grad_resid, *saved[:2])
 
     def write(f, c, piece):
         moved[f, :, 4 + 8 * c : 12 + 8 * c, :] = piece
@@ -441,9 +453,9 @@
     send[...] = buffer[pl.ds(pl.multiple_of((1 - core) * rows, 16), rows), :]
 
 
-def plain_backward(own, above, beside, across, slope, *refs):
+def plain_backward(own, above, across, beside, slope, *refs):
     saved, weights = refs[:10], refs[10:14]
-    out, keep, send, middle, tight, buffer = refs[14:]
+    keep, send, mixed_out, resid_out, middle, tight, buffer = refs[14:]
     heads = saved[5].shape[0] // 64
     middle[:, 4:] = own[...]
     middle[:, :4] = above[...].astype(F32)
@@ -454,15 +466,21 @@
         middle[f, 4 + r, :4, :] = tight[32 + n : 36 + n, :]
     cotangent = tokens_of(lambda f, c: middle[f, :, 8 * c : 8 * c + 8, :])
     saved = tuple(ref[...] for ref in saved)
-    grad_field, operands, grad_bias = backward(weights, saved, slope[...], cotangent, heads)
-
-    def write(f, c, piece):
-        out[f, :, 8 * c : 8 * c + 8, :] = piece
-
-    tile_of(grad_field, write)
+    grad_resid, operands, grad_bias = backward(weights, saved, slope[...], cotangent, heads)
+    mixed_out[...] = operands[1]
+    resid_out[...] = grad_resid
     ahead, behind = fold_bias(grad_bias, heads)
     pack_grads(operands, ahead, behind, buffer)
     split_core(buffer, keep, send)
+
+
+def plain_field(mixed, resid, center, scale, qkv, out):
+    grad_field = field_grad(qkv[...], mixed[...], resid[...], center[...], scale[...])
+
+    def write(f, c, piece):
+        out[f, :, 8 * c : 8 * c + 8, :] = piece
+
+    tile_of(grad_field, write)
 
 
 def near_place():
@@ -637,7 +655,7 @@
         limit=FULL,
         far_outs=4,
     )
-    halo = [send(top, -1, 0), send(left, 0, -1), send(corner, -1, -1)]
+    halo = [send(top, -1, 0), send(corner, -1, -1), send(left, 0, -1)]
     bias, *kept = call(
         functools.partial(keep_plain, n_row, n_col),
         [
@@ -667,7 +685,7 @@
         [(w, 1) for w in weights],
         micros=4.8,
     )
-    back = [own, send(bottom, 1, 0), send(right, 0, 1), send(corner, 1, 1)]
+    back = [own, send(bottom, 1, 0), send(corner, 1, 1), send(right, 0, 1)]
 
     eighth, quarter, piece = (size // 8, 128), (size // 4, 128), (2 * chunk, 128)
 
@@ -680,13 +698,16 @@
     shifted = call(add_core, quarters, summed, [keep, swap(away, 1, 0)])
     kept[0], *shifted = lax.optimization_barrier((kept[0], *shifted))
     (other,) = call(sum_near, [(eighth, F32)], [], near(*shifted), micros=4.0)
-    input_grad, keep, away = call(
+    keep, away, mixed, resid = call(
         plain_backward,
-        [(tile, F32), *halves],
+        [*halves, ((3 * width, tokens), BF), ((width, tokens), F32)],
         [(tile, F32), tight, buffer],
         [*back, *kept],
         [(w, 0) for w in weights],
-        micros=3.5,
+        micros=3.0,
+    )
+    (input_grad,) = call(
+        plain_field, [(tile, F32)], [], [mixed, resid, kept[1], kept[2]], [(qkv_weight, 0)], micros=1.0
     )
     plain = near(*call(add_core_later, quarters, summed, [keep, swap(away, 1, 0), other]))
     own, *sends = call(
@@ -696,6 +717,7 @@
         [*plain, other],
     )
     distant = [own] + [swap(one, 0, 2 * d) for d, one in zip(range(far - 1, 0, -1), sends, strict=True)]
+    distant[0], input_grad = lax.optimization_barrier((distant[0], input_grad))
     (done,) = call(add_far, [(piece, BF)], [], distant)
     distant = [done] + [swap(done, 0, 2 * d) for d in range(1, far)]
     (joined,) = call(join_far, [(quarter, BF)], [], distant)

time: 72.8 us -> 71.2 us (0.978)
  waiting for transfers between devices: 23.8 us -> 22.8 us
  starting transfers between devices: 29.6 us -> 28.8 us
    pallas_call x12 -> x13, Pallas kernels: 18.2 us -> 18.3 us  [call(): pl.pallas_call(body, in_specs=[here] * (count + len(stacked)) + [there] *...]
  transfers between devices with their start and end apart: 27 -> 27, of which waited for: 15 -> 14; matrix products, arithmetic and copies ran while one was open for 0% -> 0% of each run, Pallas kernels for 10% -> 11%
where the time goes in v5:
time: 71.2 us; the launch traced here: 71 us
  starting transfers between devices  28.8 us (40%)
  waiting for transfers between devices  22.8 us (32%)
  Pallas kernels  18.3 us (26%)
  between operations  0.99 us (1%)
    ppermute x21, waiting for transfers between devices, swap(): return lax.ppermute(block, axes, route)  19.2 us
    ppermute x21, starting transfers between devices, swap(): return lax.ppermute(block, axes, route)  18.8 us
    pallas_call x13, Pallas kernels, call(): pl.pallas_call(body, in_specs=[here] * (count + len(stacked)) + [there] *...  18.3 us
    ppermute x6, starting transfers between devices, send(): return lax.ppermute(block, axes, route)  10.1 us
    ppermute x6, waiting for transfers between devices, send(): return lax.ppermute(block, axes, route)  3.66 us
  transfers between devices with their start and end apart: 27, of which 14 were waited for; matrix products, arithmetic and copies ran while one was open for 0% of the time, Pallas kernels for 11%

profile of v5, /device:TPU:0, one launch (start us, length us, event | category | flops | bytes accessed | tf_op | source)
XLA Modules:
  0.0 71.0 jit_solution(1937101688510339028)
XLA Ops:
  0.7 4.3 %shard_map.118 = (f32[2,4,16,192]{3,2,1,0:T(8,128)}, bf16[2,2,4,16,192]{4,3,2,1,0:T(8,128)(2,1)}, bf16[64,192]{1,0:T(8,128)(2,1)}, bf16[64,192]{1,0:T(8,128)(2,1)}) custom-call(bf16[2,8,16,192]{3,2,1,0:T(8,128)(2,1)} %refs_0_.3, bf16[2,8,16,192]{3,2,1,0:T(8,128)(2,1)} %refs_1_.3, f32[6,2,225]{2,1,0:T(2,128)} %bitcast.7, bf16[2,192,576]{2,1,0:T(8,128)(2,1)} %refs_4_.5, ...), custom_call_target="tpu_custom_call" | custom-call | flops 2529999872 | tf_op jit(solution)/shard_map/pallas_call | solution.py:598
  4.9 6.4 %collective-permute-start.1 = (bf16[64,192]{1,0:T(8,128)(2,1)}, bf16[64,192]{1,0:T(8,128)(2,1)S(1)}, u32[]{:S(2)}, u32[]{:S(2)}) collective-permute-start(bf16[64,192]{1,0:T(8,128)(2,1)} %get-tuple-element.63), channel_id=1, source_target_pairs={{0,31},{1,24},{2,25},{3,26},{4,27},{5,28},{6,29},{7,30},{8,7},{9,0... | collective-permute-start | bytes 73736 | tf_op jit(solution)/shard_map/ppermute | solution.py:627
  12.5 2.3 %shard_map.119 = (f32[384,128]{1,0:T(8,128)S(1)}, f32[768,256]{1,0:T(8,128)S(1)}, f32[192,256]{1,0:T(8,128)S(1)}, f32[1,256]{1,0:T(1,128)S(1)}, bf16[192,256]{1,...) custom-call(bf16[2,8,16,192]{3,2,1,0:T(8,128)(2,1)S(1)} %copy-done.4, ...), custom_call_target="tpu_custom_call" | custom-call | flops 2529999872 | tf_op jit(solution)/shard_map/pallas_call | solution.py:598
  14.8 0.7 collective-permute-done.2.refs_4_
  15.5 4.4 %shard_map.120 = (f32[2,4,16,192]{3,2,1,0:T(8,128)S(1)}, bf16[2,4,16,192]{3,2,1,0:T(8,128)(2,1)S(1)}, bf16[32,192]{1,0:T(8,128)(2,1)S(1)}, bf16[32,192]{1,0:T(8,...) custom-call(f32[2,4,16,192]{3,2,1,0:T(8,128)S(1)} %copy-done.7, ...), custom_call_target="tpu_custom_call" | custom-call | flops 5280000000 | tf_op jit(solution)/shard_map/pallas_call | solution.py:598
  20.4 1.2 %collective-permute-start.4 = (bf16[32,192]{1,0:T(8,128)(2,1)S(1)}, bf16[32,192]{1,0:T(8,128)(2,1)S(1)}, u32[]{:S(2)}, u32[]{:S(2)}) collective-permute-start(bf16[32,192]{1,0:T(8,128)(2,1)S(1)} %get-tuple-element.68), channel_id=1, source_target_pairs={{0,9},{1,10},{2,11},{3,12},{4,13},{5,14},{6,15},{7,8},{8,17},{9,18... | collective-permute-start | bytes 36872 | tf_op jit(solution)/shard_map/ppermute | solution.py:627
  22.0 1.0 %collective-permute-start.3 = (bf16[2,4,16,192]{3,2,1,0:T(8,128)(2,1)S(1)}, bf16[2,4,16,192]{3,2,1,0:T(8,128)(2,1)S(1)}, u32[]{:S(2)}, u32[]{:S(2)}) collective-permute-start(bf16[2,4,16,192]{3,2,1,0:T(8,128)(2,1)S(1)} %get-tuple-element.67), channel_id=1, source_target_pairs={{0,8},{1,9},{2,10},{3,11},{4,12},{5,13},{6,14},{7,15},{8,16},{9,17... | collective-permute-start | bytes 147464 | tf_op jit(solution)/shard_map/ppermute | solution.py:627
  23.7 1.5 %collective-permute-start.9 = (bf16[448,128]{1,0:T(8,128)(2,1)S(1)}, bf16[448,128]{1,0:T(8,128)(2,1)S(1)}, u32[]{:S(2)}, u32[]{:S(2)}) collective-permute-start(bf16[448,128]{1,0:T(8,128)(2,1)S(1)} %get-tuple-element.92), channel_id=1, source_target_pairs={{0,16},{1,17},{2,18},{3,19},{4,20},{5,21},{6,22},{7,23},{8,24},{9,... | collective-permute-start | bytes 344072 | tf_op jit(solution)/shard_map/ppermute | solution.py:633
  25.2 2.1 %collective-permute-done.4.refs_2_ = bf16[32,192]{1,0:T(8,128)(2,1)S(1)} collective-permute-done((bf16[32,192]{1,0:T(8,128)(2,1)S(1)}, bf16[32,192]{1,0:T(8,128)(2,1)S(1)}, u32[]{:S(2)}, u32[]{:S(2)}) %collective-permute-start.4) | collective-permute-done | bytes 12320 | tf_op jit(solution)/shard_map/ppermute | solution.py:627
  27.3 0.9 %collective-permute-done.5.refs_3_ = bf16[32,192]{1,0:T(8,128)(2,1)S(1)} collective-permute-done((bf16[32,192]{1,0:T(8,128)(2,1)S(1)}, bf16[32,192]{1,0:T(8,128)(2,1)S(1)}, u32[]{:S(2)}, u32[]{:S(2)}) %collective-permute-start.5) | collective-permute-done | bytes 12320 | tf_op jit(solution)/shard_map/ppermute | solution.py:627
  28.2 2.7 %shard_map.122 = (bf16[1792,128]{1,0:T(8,128)(2,1)S(1)}, bf16[1792,128]{1,0:T(8,128)(2,1)S(1)}, bf16[576,256]{1,0:T(8,128)(2,1)S(1)}, f32[192,256]{1,0:T(8,128)S(1)}) custom-call(f32[2,4,16,192]{3,2,1,0:T(8,128)S(1)} %get-tuple-element.66.refs_0_, bf16[2,4,16,192]{3,2,1,0:T(8,128)(2,1)S(1)} %collective-permute-done.3.refs_1_, ...), custom_call_target="tpu_custom_call" | custom-call | flops 3300000000 | tf_op jit(solution)/shard_map/pallas_call | solution.py:598
  31.1 1.9 %collective-permute-done.10.refs_3_ = bf16[448,128]{1,0:T(8,128)(2,1)S(1)} collective-permute-done((bf16[448,128]{1,0:T(8,128)(2,1)S(1)}, bf16[448,128]{1,0:T(8,128)(2,1)S(1)}, u32[]{:S(2)}, u32[]{:S(2)}) %collective-permute-start.10) | collective-permute-done | bytes 114720 | tf_op jit(solution)/shard_map/ppermute | solution.py:633
  33.3 1.9 %collective-permute-start.11 = (bf16[448,128]{1,0:T(8,128)(2,1)S(1)}, bf16[448,128]{1,0:T(8,128)(2,1)S(1)}, u32[]{:S(2)}, u32[]{:S(2)}) collective-permute-start(bf16[448,128]{1,0:T(8,128)(2,1)S(1)} %get-tuple-element.95), channel_id=1, source_target_pairs={{0,1},{1,0},{2,3},{3,2},{4,5},{5,4},{6,7},{7,6},{8,9},{9,8},{10,11... | collective-permute-start | bytes 344072 | tf_op jit(solution)/shard_map/ppermute | solution.py:633
  35.7 1.1 %collective-permute-start.13 = (bf16[448,128]{1,0:T(8,128)(2,1)S(1)}, bf16[448,128]{1,0:T(8,128)(2,1)S(1)}, u32[]{:S(2)}, u32[]{:S(2)}) collective-permute-start(bf16[448,128]{1,0:T(8,128)(2,1)S(1)} %get-tuple-element.97), channel_id=1, source_target_pairs={{0,17},{1,16},{2,19},{3,18},{4,21},{5,20},{6,23},{7,22},{8,25},{9,... | collective-permute-start | bytes 344072 | tf_op jit(solution)/shard_map/ppermute | solution.py:633
  36.8 1.8 %collective-permute-done.11.refs_1_ = bf16[448,128]{1,0:T(8,128)(2,1)S(1)} collective-permute-done((bf16[448,128]{1,0:T(8,128)(2,1)S(1)}, bf16[448,128]{1,0:T(8,128)(2,1)S(1)}, u32[]{:S(2)}, u32[]{:S(2)}) %collective-permute-start.11) | collective-permute-done | bytes 114720 | tf_op jit(solution)/shard_map/ppermute | solution.py:633
  38.6 2.6 %collective-permute-done.12.refs_2_ = bf16[448,128]{1,0:T(8,128)(2,1)S(1)} collective-permute-done((bf16[448,128]{1,0:T(8,128)(2,1)S(1)}, bf16[448,128]{1,0:T(8,128)(2,1)S(1)}, u32[]{:S(2)}, u32[]{:S(2)}) %collective-permute-start.12) | collective-permute-done | bytes 114720 | tf_op jit(solution)/shard_map/ppermute | solution.py:633
  41.2 1.1 %collective-permute-done.13.refs_3_ = bf16[448,128]{1,0:T(8,128)(2,1)S(1)} collective-permute-done((bf16[448,128]{1,0:T(8,128)(2,1)S(1)}, bf16[448,128]{1,0:T(8,128)(2,1)S(1)}, u32[]{:S(2)}, u32[]{:S(2)}) %collective-permute-start.13) | collective-permute-done | bytes 114720 | tf_op jit(solution)/shard_map/ppermute | solution.py:633
  42.4 2.2 %collective-permute-start.14 = (bf16[224,128]{1,0:T(8,128)(2,1)S(1)}, bf16[224,128]{1,0:T(8,128)(2,1)S(1)}, u32[]{:S(2)}, u32[]{:S(2)}) collective-permute-start(bf16[224,128]{1,0:T(8,128)(2,1)S(1)} %get-tuple-element.103), channel_id=1, source_target_pairs={{0,6},{1,7},{2,4},{3,5},{4,2},{5,3},{6,0},{7,1},{8,14},{9,15},{10,... | collective-permute-start | bytes 172040 | tf_op jit(solution)/shard_map/ppermute | solution.py:633
  44.6 2.3 %collective-permute-start.16 = (bf16[224,128]{1,0:T(8,128)(2,1)S(1)}, bf16[224,128]{1,0:T(8,128)(2,1)S(1)}, u32[]{:S(2)}, u32[]{:S(2)}) collective-permute-start(bf16[224,128]{1,0:T(8,128)(2,1)S(1)} %get-tuple-element.105), channel_id=1, source_target_pairs={{0,2},{1,3},{2,0},{3,1},{4,6},{5,7},{6,4},{7,5},{8,10},{9,11},{10,... | collective-permute-start | bytes 172040 | tf_op jit(solution)/shard_map/ppermute | solution.py:633
  46.8 1.1 %shard_map.126 = f32[2,8,16,192]{3,2,1,0:T(8,128)} custom-call(bf16[576,256]{1,0:T(8,128)(2,1)S(1)} %get-tuple-element.99.refs_0_, f32[192,256]{1,0:T(8,128)S(1)} %get-tuple-element.100.refs_1_, f32[192,256]{1,0:T(8,128)S(1)} %get-tuple-element.78.refs_5_.refs_2_, f32[1,256]{1,0:T(1,128)S(1)} %get-tuple-element.79.refs_6_.refs_3_, ...), custom_call_target="tpu_custom_call" | custom-call | flops 1100000000 | tf_op jit(solution)/shard_map/pallas_call | solution.py:598
  47.9 0.6 collective-permute-done.14.refs_1_
  48.6 1.2 %collective-permute-done.15.refs_2_ = bf16[224,128]{1,0:T(8,128)(2,1)S(1)} collective-permute-done((bf16[224,128]{1,0:T(8,128)(2,1)S(1)}, bf16[224,128]{1,0:T(8,128)(2,1)S(1)}, u32[]{:S(2)}, u32[]{:S(2)}) %collective-permute-start.15) | collective-permute-done | bytes 57376 | tf_op jit(solution)/shard_map/ppermute | solution.py:633
  49.8 2.5 %collective-permute-start.19 = (bf16[224,128]{1,0:T(8,128)(2,1)S(1)}, bf16[224,128]{1,0:T(8,128)(2,1)S(1)}, u32[]{:S(2)}, u32[]{:S(2)}) collective-permute-start(bf16[224,128]{1,0:T(8,128)(2,1)S(1)} %shard_map.127.refs_0_), channel_id=1, source_target_pairs={{0,6},{1,7},{2,4},{3,5},{4,2},{5,3},{6,0},{7,1},{8,14},{9,15},{10,... | collective-permute-start | bytes 172040 | tf_op jit(solution)/shard_map/ppermute | solution.py:633
  52.6 1.7 %collective-permute-start.17 = (bf16[224,128]{1,0:T(8,128)(2,1)S(1)}, bf16[224,128]{1,0:T(8,128)(2,1)S(1)}, u32[]{:S(2)}, u32[]{:S(2)}) collective-permute-start(bf16[224,128]{1,0:T(8,128)(2,1)S(1)} %shard_map.127.refs_0_), channel_id=1, source_target_pairs={{0,2},{1,3},{2,0},{3,1},{4,6},{5,7},{6,4},{7,5},{8,10},{9,11},{10,... | collective-permute-start | bytes 172040 | tf_op jit(solution)/shard_map/ppermute | solution.py:633
  54.3 1.6 %collective-permute-done.19.refs_3_ = bf16[224,128]{1,0:T(8,128)(2,1)S(1)} collective-permute-done((bf16[224,128]{1,0:T(8,128)(2,1)S(1)}, bf16[224,128]{1,0:T(8,128)(2,1)S(1)}, u32[]{:S(2)}, u32[]{:S(2)}) %collective-permute-start.19) | collective-permute-done | bytes 57376 | tf_op jit(solution)/shard_map/ppermute | solution.py:633
  55.8 1.6 %collective-permute-done.18.refs_2_ = bf16[224,128]{1,0:T(8,128)(2,1)S(1)} collective-permute-done((bf16[224,128]{1,0:T(8,128)(2,1)S(1)}, bf16[224,128]{1,0:T(8,128)(2,1)S(1)}, u32[]{:S(2)}, u32[]{:S(2)}) %collective-permute-start.18) | collective-permute-done | bytes 57376 | tf_op jit(solution)/shard_map/ppermute | solution.py:633
  57.5 1.6 %collective-permute-start.25 = (bf16[896,128]{1,0:T(8,128)(2,1)S(1)}, bf16[896,128]{1,0:T(8,128)(2,1)S(1)}, u32[]{:S(2)}, u32[]{:S(2)}) collective-permute-start(bf16[896,128]{1,0:T(8,128)(2,1)S(1)} %shard_map.128.refs_0_), channel_id=1, source_target_pairs={{0,17},{1,16},{2,19},{3,18},{4,21},{5,20},{6,23},{7,22},{8,25},{9,... | collective-permute-start | bytes 688136 | tf_op jit(solution)/shard_map/ppermute | solution.py:633
  59.1 1.5 %collective-permute-start.23 = (bf16[896,128]{1,0:T(8,128)(2,1)S(1)}, bf16[896,128]{1,0:T(8,128)(2,1)S(1)}, u32[]{:S(2)}, u32[]{:S(2)}) collective-permute-start(bf16[896,128]{1,0:T(8,128)(2,1)S(1)} %shard_map.128.refs_0_), channel_id=1, source_target_pairs={{0,16},{1,17},{2,18},{3,19},{4,20},{5,21},{6,22},{7,23},{8,24},{9,... | collective-permute-start | bytes 688136 | tf_op jit(solution)/shard_map/ppermute | solution.py:633
  61.0 4.5 %collective-permute-done.25.refs_3_ = bf16[896,128]{1,0:T(8,128)(2,1)S(1)} collective-permute-done((bf16[896,128]{1,0:T(8,128)(2,1)S(1)}, bf16[896,128]{1,0:T(8,128)(2,1)S(1)}, u32[]{:S(2)}, u32[]{:S(2)}) %collective-permute-start.25) | collective-permute-done | bytes 229408 | tf_op jit(solution)/shard_map/ppermute | solution.py:633
  65.5 1.9 %collective-permute-done.23.refs_2_ = bf16[896,128]{1,0:T(8,128)(2,1)S(1)} collective-permute-done((bf16[896,128]{1,0:T(8,128)(2,1)S(1)}, bf16[896,128]{1,0:T(8,128)(2,1)S(1)}, u32[]{:S(2)}, u32[]{:S(2)}) %collective-permute-start.23) | collective-permute-done | bytes 229408 | tf_op jit(solution)/shard_map/ppermute | solution.py:633
  67.9 1.5 %shard_map.129 = (f32[2,192,576]{2,1,0:T(8,128)}, f32[2,192,192]{2,1,0:T(8,128)}, f32[2,192,768]{2,1,0:T(8,128)}, f32[2,192,768]{2,1,0:T(8,128)}, f32[6,2,225]{2,1,0:T(2,128)}) custom-call(bf16[896,128]{1,0:T(8,128)(2,1)S(1)} %shard_map.128.refs_0_, bf16[896,128]{1,0:T(8,128)(2,1)S(1)} %collective-permute-done.21.refs_1_, ...), custom_call_target="tpu_custom_call" | custom-call | flops 1320000000 | tf_op jit(solution)/shard_map/pallas_call | solution.py:598
  69.4 1.5 %shard_map.130 = (f32[2,192,576]{2,1,0:T(8,128)}, f32[2,192,192]{2,1,0:T(8,128)}, f32[2,192,768]{2,1,0:T(8,128)}, f32[2,192,768]{2,1,0:T(8,128)}, f32[6,2,225]{2,1,0:T(2,128)}) custom-call(bf16[896,128]{1,0:T(8,128)(2,1)S(1)} %collective-permute-done.20.refs_0_, ...), custom_call_target="tpu_custom_call", output_to_operand_aliasing={{0}: (4, {}), {1}: (5, {}), {2}: (6, {}), {3}: (7, {}), {4}... | custom-call | flops 1320000000 | tf_op jit(solution)/shard_map/pallas_call | solution.py:598
  (51 shorter events, 5.1 us)
Async XLA Ops:
  0.6 11.8 %copy-start = (bf16[2,192,768]{2,1,0:T(8,128)(2,1)S(1)}, bf16[2,192,768]{2,1,0:T(8,128)(2,1)}, u32[]{:S(2)}) copy-start(bf16[2,192,768]{2,1,0:T(8,128)(2,1)} %refs_17_.1) | copy-start | bytes 1769476
  0.6 11.8 %copy-start.2 = (bf16[2,192,576]{2,1,0:T(8,128)(2,1)S(1)}, bf16[2,192,576]{2,1,0:T(8,128)(2,1)}, u32[]{:S(2)}) copy-start(bf16[2,192,576]{2,1,0:T(8,128)(2,1)} %refs_4_.5) | copy-start | bytes 1327108
  0.7 11.8 %copy-start.3 = (bf16[2,192,192]{2,1,0:T(8,128)(2,1)S(1)}, bf16[2,192,192]{2,1,0:T(8,128)(2,1)}, u32[]{:S(2)}) copy-start(bf16[2,192,192]{2,1,0:T(8,128)(2,1)} %refs_16_.1) | copy-start | bytes 442372
  0.7 11.8 %copy-start.4 = (bf16[2,8,16,192]{3,2,1,0:T(8,128)(2,1)S(1)}, bf16[2,8,16,192]{3,2,1,0:T(8,128)(2,1)}, u32[]{:S(2)}) copy-start(bf16[2,8,16,192]{3,2,1,0:T(8,128)(2,1)} %refs_0_.3) | copy-start | bytes 294916
  0.7 11.8 %copy-start.6 = (f32[2,6,225]{2,0,1:T(2,128)S(1)}, f32[2,6,225]{2,0,1:T(2,128)}, u32[]{:S(2)}) copy-start(f32[2,6,225]{2,0,1:T(2,128)} %param.13) | copy-start | bytes 32404
  4.9 9.9 %collective-permute-start.1 = (bf16[64,192]{1,0:T(8,128)(2,1)}, bf16[64,192]{1,0:T(8,128)(2,1)S(1)}, u32[]{:S(2)}, u32[]{:S(2)}) collective-permute-start(bf16[64,192]{1,0:T(8,128)(2,1)} %get-tuple-element.63), channel_id=1, source_target_pairs={{0,31},{1,24},{2,25},{3,26},{4,27},{5,28},{6,29},{7,30},{8,7},{9,0... | collective-permute-start | bytes 73736 | tf_op jit(solution)/shard_map/ppermute | solution.py:627
  11.4 4.1 %collective-permute-start.2 = (bf16[64,192]{1,0:T(8,128)(2,1)}, bf16[64,192]{1,0:T(8,128)(2,1)S(1)}, u32[]{:S(2)}, u32[]{:S(2)}) collective-permute-start(bf16[64,192]{1,0:T(8,128)(2,1)} %get-tuple-element.64), channel_id=1, source_target_pairs={{0,7},{1,0},{2,1},{3,2},{4,3},{5,4},{6,5},{7,6},{8,15},{9,8},{10,9... | collective-permute-start | bytes 73736 | tf_op jit(solution)/shard_map/ppermute | solution.py:627
  11.9 3.6 %collective-permute-start = (bf16[2,2,4,16,192]{4,3,2,1,0:T(8,128)(2,1)}, bf16[2,2,4,16,192]{4,3,2,1,0:T(8,128)(2,1)S(1)}, u32[]{:S(2)}, u32[]{:S(2)}) collective-permute-start(bf16[2,2,4,16,192]{4,3,2,1,0:T(8,128)(2,1)} %get-tuple-element.62), channel_id=1, source_target_pairs={{0,24},{1,25},{2,26},{3,27},{4,28},{5,29},{6,30},{7,31},{8,0},{9,1... | collective-permute-start | bytes 294920 | tf_op jit(solution)/shard_map/ppermute | solution.py:627
  19.9 3.1 %collective-permute-start.6 = (bf16[1792,128]{1,0:T(8,128)(2,1)S(1)}, bf16[1792,128]{1,0:T(8,128)(2,1)S(1)}, u32[]{:S(2)}, u32[]{:S(2)}) collective-permute-start(bf16[1792,128]{1,0:T(8,128)(2,1)S(1)} %get-tuple-element.72), channel_id=1, source_target_pairs={{0,8},{1,9},{2,10},{3,11},{4,12},{5,13},{6,14},{7,15},{8,0},{9,1},... | collective-permute-start | bytes 1376264 | tf_op jit(solution)/shard_map/ppermute | solution.py:633
  20.4 6.9 %collective-permute-start.4 = (bf16[32,192]{1,0:T(8,128)(2,1)S(1)}, bf16[32,192]{1,0:T(8,128)(2,1)S(1)}, u32[]{:S(2)}, u32[]{:S(2)}) collective-permute-start(bf16[32,192]{1,0:T(8,128)(2,1)S(1)} %get-tuple-element.68), channel_id=1, source_target_pairs={{0,9},{1,10},{2,11},{3,12},{4,13},{5,14},{6,15},{7,8},{8,17},{9,18... | collective-permute-start | bytes 36872 | tf_op jit(solution)/shard_map/ppermute | solution.py:627
  21.6 6.5 %collective-permute-start.5 = (bf16[32,192]{1,0:T(8,128)(2,1)S(1)}, bf16[32,192]{1,0:T(8,128)(2,1)S(1)}, u32[]{:S(2)}, u32[]{:S(2)}) collective-permute-start(bf16[32,192]{1,0:T(8,128)(2,1)S(1)} %get-tuple-element.69), channel_id=1, source_target_pairs={{0,1},{1,2},{2,3},{3,4},{4,5},{5,6},{6,7},{7,0},{8,9},{9,10},{10,1... | collective-permute-start | bytes 36872 | tf_op jit(solution)/shard_map/ppermute | solution.py:627
  22.0 6.2 %collective-permute-start.3 = (bf16[2,4,16,192]{3,2,1,0:T(8,128)(2,1)S(1)}, bf16[2,4,16,192]{3,2,1,0:T(8,128)(2,1)S(1)}, u32[]{:S(2)}, u32[]{:S(2)}) collective-permute-start(bf16[2,4,16,192]{3,2,1,0:T(8,128)(2,1)S(1)} %get-tuple-element.67), channel_id=1, source_target_pairs={{0,8},{1,9},{2,10},{3,11},{4,12},{5,13},{6,14},{7,15},{8,16},{9,17... | collective-permute-start | bytes 147464 | tf_op jit(solution)/shard_map/ppermute | solution.py:627
  23.2 7.9 %collective-permute-start.8 = (bf16[448,128]{1,0:T(8,128)(2,1)S(1)}, bf16[448,128]{1,0:T(8,128)(2,1)S(1)}, u32[]{:S(2)}, u32[]{:S(2)}) collective-permute-start(bf16[448,128]{1,0:T(8,128)(2,1)S(1)} %get-tuple-element.91), channel_id=1, source_target_pairs={{0,1},{1,0},{2,3},{3,2},{4,5},{5,4},{6,7},{7,6},{8,9},{9,8},{10,11... | collective-permute-start | bytes 344072 | tf_op jit(solution)/shard_map/ppermute | solution.py:633
  23.7 7.5 %collective-permute-start.9 = (bf16[448,128]{1,0:T(8,128)(2,1)S(1)}, bf16[448,128]{1,0:T(8,128)(2,1)S(1)}, u32[]{:S(2)}, u32[]{:S(2)}) collective-permute-start(bf16[448,128]{1,0:T(8,128)(2,1)S(1)} %get-tuple-element.92), channel_id=1, source_target_pairs={{0,16},{1,17},{2,18},{3,19},{4,20},{5,21},{6,22},{7,23},{8,24},{9,... | collective-permute-start | bytes 344072 | tf_op jit(solution)/shard_map/ppermute | solution.py:633
  27.3 5.7 %collective-permute-start.10 = (bf16[448,128]{1,0:T(8,128)(2,1)S(1)}, bf16[448,128]{1,0:T(8,128)(2,1)S(1)}, u32[]{:S(2)}, u32[]{:S(2)}) collective-permute-start(bf16[448,128]{1,0:T(8,128)(2,1)S(1)} %get-tuple-element.93), channel_id=1, source_target_pairs={{0,17},{1,16},{2,19},{3,18},{4,21},{5,20},{6,23},{7,22},{8,25},{9,... | collective-permute-start | bytes 344072 | tf_op jit(solution)/shard_map/ppermute | solution.py:633
  30.9 2.2 %collective-permute-start.7 = (bf16[1792,128]{1,0:T(8,128)(2,1)S(1)}, bf16[1792,128]{1,0:T(8,128)(2,1)S(1)}, u32[]{:S(2)}, u32[]{:S(2)}) collective-permute-start(bf16[1792,128]{1,0:T(8,128)(2,1)S(1)} %get-tuple-element.89), channel_id=1, source_target_pairs={{0,8},{1,9},{2,10},{3,11},{4,12},{5,13},{6,14},{7,15},{8,0},{9,1},... | collective-permute-start | bytes 1376264 | tf_op jit(solution)/shard_map/ppermute | solution.py:633
  33.3 5.3 %collective-permute-start.11 = (bf16[448,128]{1,0:T(8,128)(2,1)S(1)}, bf16[448,128]{1,0:T(8,128)(2,1)S(1)}, u32[]{:S(2)}, u32[]{:S(2)}) collective-permute-start(bf16[448,128]{1,0:T(8,128)(2,1)S(1)} %get-tuple-element.95), channel_id=1, source_target_pairs={{0,1},{1,0},{2,3},{3,2},{4,5},{5,4},{6,7},{7,6},{8,9},{9,8},{10,11... | collective-permute-start | bytes 344072 | tf_op jit(solution)/shard_map/ppermute | solution.py:633
  35.1 6.0 %collective-permute-start.12 = (bf16[448,128]{1,0:T(8,128)(2,1)S(1)}, bf16[448,128]{1,0:T(8,128)(2,1)S(1)}, u32[]{:S(2)}, u32[]{:S(2)}) collective-permute-start(bf16[448,128]{1,0:T(8,128)(2,1)S(1)} %get-tuple-element.96), channel_id=1, source_target_pairs={{0,16},{1,17},{2,18},{3,19},{4,20},{5,21},{6,22},{7,23},{8,24},{9,... | collective-permute-start | bytes 344072 | tf_op jit(solution)/shard_map/ppermute | solution.py:633
  35.7 6.6 %collective-permute-start.13 = (bf16[448,128]{1,0:T(8,128)(2,1)S(1)}, bf16[448,128]{1,0:T(8,128)(2,1)S(1)}, u32[]{:S(2)}, u32[]{:S(2)}) collective-permute-start(bf16[448,128]{1,0:T(8,128)(2,1)S(1)} %get-tuple-element.97), channel_id=1, source_target_pairs={{0,17},{1,16},{2,19},{3,18},{4,21},{5,20},{6,23},{7,22},{8,25},{9,... | collective-permute-start | bytes 344072 | tf_op jit(solution)/shard_map/ppermute | solution.py:633
  42.4 6.2 %collective-permute-start.14 = (bf16[224,128]{1,0:T(8,128)(2,1)S(1)}, bf16[224,128]{1,0:T(8,128)(2,1)S(1)}, u32[]{:S(2)}, u32[]{:S(2)}) collective-permute-start(bf16[224,128]{1,0:T(8,128)(2,1)S(1)} %get-tuple-element.103), channel_id=1, source_target_pairs={{0,6},{1,7},{2,4},{3,5},{4,2},{5,3},{6,0},{7,1},{8,14},{9,15},{10,... | collective-permute-start | bytes 172040 | tf_op jit(solution)/shard_map/ppermute | solution.py:633
  44.6 5.2 %collective-permute-start.15 = (bf16[224,128]{1,0:T(8,128)(2,1)S(1)}, bf16[224,128]{1,0:T(8,128)(2,1)S(1)}, u32[]{:S(2)}, u32[]{:S(2)}) collective-permute-start(bf16[224,128]{1,0:T(8,128)(2,1)S(1)} %get-tuple-element.104), channel_id=1, source_target_pairs={{0,4},{1,5},{2,6},{3,7},{4,0},{5,1},{6,2},{7,3},{8,12},{9,13},{10,... | collective-permute-start | bytes 172040 | tf_op jit(solution)/shard_map/ppermute | solution.py:633
  44.6 5.2 %collective-permute-start.16 = (bf16[224,128]{1,0:T(8,128)(2,1)S(1)}, bf16[224,128]{1,0:T(8,128)(2,1)S(1)}, u32[]{:S(2)}, u32[]{:S(2)}) collective-permute-start(bf16[224,128]{1,0:T(8,128)(2,1)S(1)} %get-tuple-element.105), channel_id=1, source_target_pairs={{0,2},{1,3},{2,0},{3,1},{4,6},{5,7},{6,4},{7,5},{8,10},{9,11},{10,... | collective-permute-start | bytes 172040 | tf_op jit(solution)/shard_map/ppermute | solution.py:633
  49.8 6.0 %collective-permute-start.19 = (bf16[224,128]{1,0:T(8,128)(2,1)S(1)}, bf16[224,128]{1,0:T(8,128)(2,1)S(1)}, u32[]{:S(2)}, u32[]{:S(2)}) collective-permute-start(bf16[224,128]{1,0:T(8,128)(2,1)S(1)} %shard_map.127.refs_0_), channel_id=1, source_target_pairs={{0,6},{1,7},{2,4},{3,5},{4,2},{5,3},{6,0},{7,1},{8,14},{9,15},{10,... | collective-permute-start | bytes 172040 | tf_op jit(solution)/shard_map/ppermute | solution.py:633
  52.3 5.2 %collective-permute-start.18 = (bf16[224,128]{1,0:T(8,128)(2,1)S(1)}, bf16[224,128]{1,0:T(8,128)(2,1)S(1)}, u32[]{:S(2)}, u32[]{:S(2)}) collective-permute-start(bf16[224,128]{1,0:T(8,128)(2,1)S(1)} %shard_map.127.refs_0_), channel_id=1, source_target_pairs={{0,4},{1,5},{2,6},{3,7},{4,0},{5,1},{6,2},{7,3},{8,12},{9,13},{10,... | collective-permute-start | bytes 172040 | tf_op jit(solution)/shard_map/ppermute | solution.py:633
  52.6 4.9 %collective-permute-start.17 = (bf16[224,128]{1,0:T(8,128)(2,1)S(1)}, bf16[224,128]{1,0:T(8,128)(2,1)S(1)}, u32[]{:S(2)}, u32[]{:S(2)}) collective-permute-start(bf16[224,128]{1,0:T(8,128)(2,1)S(1)} %shard_map.127.refs_0_), channel_id=1, source_target_pairs={{0,2},{1,3},{2,0},{3,1},{4,6},{5,7},{6,4},{7,5},{8,10},{9,11},{10,... | collective-permute-start | bytes 172040 | tf_op jit(solution)/shard_map/ppermute | solution.py:633
  57.5 8.0 %collective-permute-start.25 = (bf16[896,128]{1,0:T(8,128)(2,1)S(1)}, bf16[896,128]{1,0:T(8,128)(2,1)S(1)}, u32[]{:S(2)}, u32[]{:S(2)}) collective-permute-start(bf16[896,128]{1,0:T(8,128)(2,1)S(1)} %shard_map.128.refs_0_), channel_id=1, source_target_pairs={{0,17},{1,16},{2,19},{3,18},{4,21},{5,20},{6,23},{7,22},{8,25},{9,... | collective-permute-start | bytes 688136 | tf_op jit(solution)/shard_map/ppermute | solution.py:633
  59.1 8.3 %collective-permute-start.23 = (bf16[896,128]{1,0:T(8,128)(2,1)S(1)}, bf16[896,128]{1,0:T(8,128)(2,1)S(1)}, u32[]{:S(2)}, u32[]{:S(2)}) collective-permute-start(bf16[896,128]{1,0:T(8,128)(2,1)S(1)} %shard_map.128.refs_0_), channel_id=1, source_target_pairs={{0,16},{1,17},{2,18},{3,19},{4,20},{5,21},{6,22},{7,23},{8,24},{9,... | collective-permute-start | bytes 688136 | tf_op jit(solution)/shard_map/ppermute | solution.py:633
  60.6 7.2 %collective-permute-start.21 = (bf16[896,128]{1,0:T(8,128)(2,1)S(1)}, bf16[896,128]{1,0:T(8,128)(2,1)S(1)}, u32[]{:S(2)}, u32[]{:S(2)}) collective-permute-start(bf16[896,128]{1,0:T(8,128)(2,1)S(1)} %shard_map.128.refs_0_), channel_id=1, source_target_pairs={{0,1},{1,0},{2,3},{3,2},{4,5},{5,4},{6,7},{7,6},{8,9},{9,8},{10,11... | collective-permute-start | bytes 688136 | tf_op jit(solution)/shard_map/ppermute | solution.py:633
  61.0 8.3 %collective-permute-start.20 = (bf16[896,128]{1,0:T(8,128)(2,1)S(1)}, bf16[896,128]{1,0:T(8,128)(2,1)S(1)}, u32[]{:S(2)}, u32[]{:S(2)}) collective-permute-start(bf16[896,128]{1,0:T(8,128)(2,1)S(1)} %shard_map.128.refs_0_), channel_id=1, source_target_pairs={{0,8},{1,9},{2,10},{3,11},{4,12},{5,13},{6,14},{7,15},{8,0},{9,1},... | collective-permute-start | bytes 688136 | tf_op jit(solution)/shard_map/ppermute | solution.py:633
  65.5 3.9 %collective-permute-start.26 = (bf16[896,128]{1,0:T(8,128)(2,1)S(1)}, bf16[896,128]{1,0:T(8,128)(2,1)S(1)}, u32[]{:S(2)}, u32[]{:S(2)}) collective-permute-start(bf16[896,128]{1,0:T(8,128)(2,1)S(1)} %collective-permute-done.25.refs_3_), channel_id=1, source_target_pairs={{0,8},{1,9},{2,10},{3,11},{4,12},{5,13},{6,14},{7,15},{8,0},{9,1},... | collective-permute-start | bytes 688136 | tf_op jit(solution)/shard_map/ppermute | solution.py:633
  67.4 2.0 %collective-permute-start.24 = (bf16[896,128]{1,0:T(8,128)(2,1)S(1)}, bf16[896,128]{1,0:T(8,128)(2,1)S(1)}, u32[]{:S(2)}, u32[]{:S(2)}) collective-permute-start(bf16[896,128]{1,0:T(8,128)(2,1)S(1)} %collective-permute-done.23.refs_2_), channel_id=1, source_target_pairs={{0,8},{1,9},{2,10},{3,11},{4,12},{5,13},{6,14},{7,15},{8,0},{9,1},... | collective-permute-start | bytes 688136 | tf_op jit(solution)/shard_map/ppermute | solution.py:633
  67.9 1.5 %collective-permute-start.22 = (bf16[896,128]{1,0:T(8,128)(2,1)S(1)}, bf16[896,128]{1,0:T(8,128)(2,1)S(1)}, u32[]{:S(2)}, u32[]{:S(2)}) collective-permute-start(bf16[896,128]{1,0:T(8,128)(2,1)S(1)} %collective-permute-done.21.refs_1_), channel_id=1, source_target_pairs={{0,8},{1,9},{2,10},{3,11},{4,12},{5,13},{6,14},{7,15},{8,0},{9,1},... | collective-permute-start | bytes 688136 | tf_op jit(solution)/shard_map/ppermute | solution.py:633
  (3 other events, 10.9 us)

commit v6 on v5

--- a/solution.py
+++ b/solution.py
@@ -710,6 +710,7 @@
         plain_field, [(tile, F32)], [], [mixed, resid, kept[1], kept[2]], [(qkv_weight, 0)], micros=1.0
     )
     plain = near(*call(add_core_later, quarters, summed, [keep, swap(away, 1, 0), other]))
+    plain[0], input_grad = lax.optimization_barrier((plain[0], input_grad))
     own, *sends = call(
         functools.partial(add_near, far),
         [(piece, F32)] + [(piece, BF)] * (far - 1),
@@ -717,7 +718,6 @@
         [*plain, other],
     )
     distant = [own] + [swap(one, 0, 2 * d) for d, one in zip(range(far - 1, 0, -1), sends, strict=True)]
-    distant[0], input_grad = lax.optimization_barrier((distant[0], input_grad))
     (done,) = call(add_far, [(piece, BF)], [], distant)
     distant = [done] + [swap(done, 0, 2 * d) for d in range(1, far)]
     (joined,) = call(join_far, [(quarter, BF)], [], distant)

time: 71.2 us -> 71.2 us (level)
  no operation moved by 1% of the time
where the time goes in v6:
time: 71.2 us; the launch traced here: 71 us
  starting transfers between devices  28.8 us (40%)
  waiting for transfers between devices  22.8 us (32%)
  Pallas kernels  18.3 us (26%)
  between operations  0.99 us (1%)
    ppermute x21, waiting for transfers between devices, swap(): return lax.ppermute(block, axes, route)  19.2 us
    ppermute x21, starting transfers between devices, swap(): return lax.ppermute(block, axes, route)  18.8 us
    pallas_call x13, Pallas kernels, call(): pl.pallas_call(body, in_specs=[here] * (count + len(stacked)) + [there] *...  18.3 us
    ppermute x6, starting transfers between devices, send(): return lax.ppermute(block, axes, route)  10.1 us
    ppermute x6, waiting for transfers between devices, send(): return lax.ppermute(block, axes, route)  3.66 us
  transfers between devices with their start and end apart: 27, of which 14 were waited for; matrix products, arithmetic and copies ran while one was open for 0% of the time, Pallas kernels for 11%

profile of v6, /device:TPU:0, one launch (start us, length us, event | category | flops | bytes accessed | tf_op | source)
XLA Modules:
  0.0 71.0 jit_solution(17431808508497191124)
XLA Ops:
  0.7 4.3 %shard_map.118 = (f32[2,4,16,192]{3,2,1,0:T(8,128)}, bf16[2,2,4,16,192]{4,3,2,1,0:T(8,128)(2,1)}, bf16[64,192]{1,0:T(8,128)(2,1)}, bf16[64,192]{1,0:T(8,128)(2,1)}) custom-call(bf16[2,8,16,192]{3,2,1,0:T(8,128)(2,1)} %refs_0_.3, bf16[2,8,16,192]{3,2,1,0:T(8,128)(2,1)} %refs_1_.3, f32[6,2,225]{2,1,0:T(2,128)} %bitcast.7, bf16[2,192,576]{2,1,0:T(8,128)(2,1)} %refs_4_.5, ...), custom_call_target="tpu_custom_call" | custom-call | flops 2529999872 | tf_op jit(solution)/shard_map/pallas_call | solution.py:598
  4.9 6.4 %collective-permute-start.1 = (bf16[64,192]{1,0:T(8,128)(2,1)}, bf16[64,192]{1,0:T(8,128)(2,1)S(1)}, u32[]{:S(2)}, u32[]{:S(2)}) collective-permute-start(bf16[64,192]{1,0:T(8,128)(2,1)} %get-tuple-element.63), channel_id=1, source_target_pairs={{0,31},{1,24},{2,25},{3,26},{4,27},{5,28},{6,29},{7,30},{8,7},{9,0... | collective-permute-start | bytes 73736 | tf_op jit(solution)/shard_map/ppermute | solution.py:627
  12.5 2.3 %shard_map.119 = (f32[384,128]{1,0:T(8,128)S(1)}, f32[768,256]{1,0:T(8,128)S(1)}, f32[192,256]{1,0:T(8,128)S(1)}, f32[1,256]{1,0:T(1,128)S(1)}, bf16[192,256]{1,...) custom-call(bf16[2,8,16,192]{3,2,1,0:T(8,128)(2,1)S(1)} %copy-done.4, ...), custom_call_target="tpu_custom_call" | custom-call | flops 2529999872 | tf_op jit(solution)/shard_map/pallas_call | solution.py:598
  14.8 0.7 collective-permute-done.2.refs_4_
  15.5 4.4 %shard_map.120 = (f32[2,4,16,192]{3,2,1,0:T(8,128)S(1)}, bf16[2,4,16,192]{3,2,1,0:T(8,128)(2,1)S(1)}, bf16[32,192]{1,0:T(8,128)(2,1)S(1)}, bf16[32,192]{1,0:T(8,...) custom-call(f32[2,4,16,192]{3,2,1,0:T(8,128)S(1)} %copy-done.7, ...), custom_call_target="tpu_custom_call" | custom-call | flops 5280000000 | tf_op jit(solution)/shard_map/pallas_call | solution.py:598
  20.4 1.2 %collective-permute-start.4 = (bf16[32,192]{1,0:T(8,128)(2,1)S(1)}, bf16[32,192]{1,0:T(8,128)(2,1)S(1)}, u32[]{:S(2)}, u32[]{:S(2)}) collective-permute-start(bf16[32,192]{1,0:T(8,128)(2,1)S(1)} %get-tuple-element.68), channel_id=1, source_target_pairs={{0,9},{1,10},{2,11},{3,12},{4,13},{5,14},{6,15},{7,8},{8,17},{9,18... | collective-permute-start | bytes 36872 | tf_op jit(solution)/shard_map/ppermute | solution.py:627
  22.0 1.0 %collective-permute-start.3 = (bf16[2,4,16,192]{3,2,1,0:T(8,128)(2,1)S(1)}, bf16[2,4,16,192]{3,2,1,0:T(8,128)(2,1)S(1)}, u32[]{:S(2)}, u32[]{:S(2)}) collective-permute-start(bf16[2,4,16,192]{3,2,1,0:T(8,128)(2,1)S(1)} %get-tuple-element.67), channel_id=1, source_target_pairs={{0,8},{1,9},{2,10},{3,11},{4,12},{5,13},{6,14},{7,15},{8,16},{9,17... | collective-permute-start | bytes 147464 | tf_op jit(solution)/shard_map/ppermute | solution.py:627
  23.7 1.5 %collective-permute-start.9 = (bf16[448,128]{1,0:T(8,128)(2,1)S(1)}, bf16[448,128]{1,0:T(8,128)(2,1)S(1)}, u32[]{:S(2)}, u32[]{:S(2)}) collective-permute-start(bf16[448,128]{1,0:T(8,128)(2,1)S(1)} %get-tuple-element.92), channel_id=1, source_target_pairs={{0,16},{1,17},{2,18},{3,19},{4,20},{5,21},{6,22},{7,23},{8,24},{9,... | collective-permute-start | bytes 344072 | tf_op jit(solution)/shard_map/ppermute | solution.py:633
  25.2 2.1 %collective-permute-done.4.refs_2_ = bf16[32,192]{1,0:T(8,128)(2,1)S(1)} collective-permute-done((bf16[32,192]{1,0:T(8,128)(2,1)S(1)}, bf16[32,192]{1,0:T(8,128)(2,1)S(1)}, u32[]{:S(2)}, u32[]{:S(2)}) %collective-permute-start.4) | collective-permute-done | bytes 12320 | tf_op jit(solution)/shard_map/ppermute | solution.py:627
  27.3 0.9 %collective-permute-done.5.refs_3_ = bf16[32,192]{1,0:T(8,128)(2,1)S(1)} collective-permute-done((bf16[32,192]{1,0:T(8,128)(2,1)S(1)}, bf16[32,192]{1,0:T(8,128)(2,1)S(1)}, u32[]{:S(2)}, u32[]{:S(2)}) %collective-permute-start.5) | collective-permute-done | bytes 12320 | tf_op jit(solution)/shard_map/ppermute | solution.py:627
  28.2 2.7 %shard_map.122 = (bf16[1792,128]{1,0:T(8,128)(2,1)S(1)}, bf16[1792,128]{1,0:T(8,128)(2,1)S(1)}, bf16[576,256]{1,0:T(8,128)(2,1)S(1)}, f32[192,256]{1,0:T(8,128)S(1)}) custom-call(f32[2,4,16,192]{3,2,1,0:T(8,128)S(1)} %get-tuple-element.66.refs_0_, bf16[2,4,16,192]{3,2,1,0:T(8,128)(2,1)S(1)} %collective-permute-done.3.refs_1_, ...), custom_call_target="tpu_custom_call" | custom-call | flops 3300000000 | tf_op jit(solution)/shard_map/pallas_call | solution.py:598
  31.1 1.9 %collective-permute-done.10.refs_3_ = bf16[448,128]{1,0:T(8,128)(2,1)S(1)} collective-permute-done((bf16[448,128]{1,0:T(8,128)(2,1)S(1)}, bf16[448,128]{1,0:T(8,128)(2,1)S(1)}, u32[]{:S(2)}, u32[]{:S(2)}) %collective-permute-start.10) | collective-permute-done | bytes 114720 | tf_op jit(solution)/shard_map/ppermute | solution.py:633
  33.3 1.9 %collective-permute-start.11 = (bf16[448,128]{1,0:T(8,128)(2,1)S(1)}, bf16[448,128]{1,0:T(8,128)(2,1)S(1)}, u32[]{:S(2)}, u32[]{:S(2)}) collective-permute-start(bf16[448,128]{1,0:T(8,128)(2,1)S(1)} %get-tuple-element.99), channel_id=1, source_target_pairs={{0,1},{1,0},{2,3},{3,2},{4,5},{5,4},{6,7},{7,6},{8,9},{9,8},{10,11... | collective-permute-start | bytes 344072 | tf_op jit(solution)/shard_map/ppermute | solution.py:633
  35.7 1.1 %collective-permute-start.13 = (bf16[448,128]{1,0:T(8,128)(2,1)S(1)}, bf16[448,128]{1,0:T(8,128)(2,1)S(1)}, u32[]{:S(2)}, u32[]{:S(2)}) collective-permute-start(bf16[448,128]{1,0:T(8,128)(2,1)S(1)} %get-tuple-element.101), channel_id=1, source_target_pairs={{0,17},{1,16},{2,19},{3,18},{4,21},{5,20},{6,23},{7,22},{8,25},{9,... | collective-permute-start | bytes 344072 | tf_op jit(solution)/shard_map/ppermute | solution.py:633
  36.8 1.1 %shard_map.125 = f32[2,8,16,192]{3,2,1,0:T(8,128)} custom-call(bf16[576,256]{1,0:T(8,128)(2,1)S(1)} %get-tuple-element.95.refs_0_, f32[192,256]{1,0:T(8,128)S(1)} %get-tuple-element.96.refs_1_, f32[192,256]{1,0:T(8,128)S(1)} %get-tuple-element.78.refs_5_.refs_2_, f32[1,256]{1,0:T(1,128)S(1)} %get-tuple-element.79.refs_6_.refs_3_, ...), custom_call_target="tpu_custom_call" | custom-call | flops 1100000000 | tf_op jit(solution)/shard_map/pallas_call | solution.py:598
  37.9 0.7 collective-permute-done.11.refs_1_
  38.6 2.6 %collective-permute-done.12.refs_2_ = bf16[448,128]{1,0:T(8,128)(2,1)S(1)} collective-permute-done((bf16[448,128]{1,0:T(8,128)(2,1)S(1)}, bf16[448,128]{1,0:T(8,128)(2,1)S(1)}, u32[]{:S(2)}, u32[]{:S(2)}) %collective-permute-start.12) | collective-permute-done | bytes 114720 | tf_op jit(solution)/shard_map/ppermute | solution.py:633
  41.2 1.1 %collective-permute-done.13.refs_3_ = bf16[448,128]{1,0:T(8,128)(2,1)S(1)} collective-permute-done((bf16[448,128]{1,0:T(8,128)(2,1)S(1)}, bf16[448,128]{1,0:T(8,128)(2,1)S(1)}, u32[]{:S(2)}, u32[]{:S(2)}) %collective-permute-start.13) | collective-permute-done | bytes 114720 | tf_op jit(solution)/shard_map/ppermute | solution.py:633
  42.4 2.2 %collective-permute-start.14 = (bf16[224,128]{1,0:T(8,128)(2,1)S(1)}, bf16[224,128]{1,0:T(8,128)(2,1)S(1)}, u32[]{:S(2)}, u32[]{:S(2)}) collective-permute-start(bf16[224,128]{1,0:T(8,128)(2,1)S(1)} %get-tuple-element.103), channel_id=1, source_target_pairs={{0,6},{1,7},{2,4},{3,5},{4,2},{5,3},{6,0},{7,1},{8,14},{9,15},{10,... | collective-permute-start | bytes 172040 | tf_op jit(solution)/shard_map/ppermute | solution.py:633
  44.6 2.3 %collective-permute-start.16 = (bf16[224,128]{1,0:T(8,128)(2,1)S(1)}, bf16[224,128]{1,0:T(8,128)(2,1)S(1)}, u32[]{:S(2)}, u32[]{:S(2)}) collective-permute-start(bf16[224,128]{1,0:T(8,128)(2,1)S(1)} %get-tuple-element.105), channel_id=1, source_target_pairs={{0,2},{1,3},{2,0},{3,1},{4,6},{5,7},{6,4},{7,5},{8,10},{9,11},{10,... | collective-permute-start | bytes 172040 | tf_op jit(solution)/shard_map/ppermute | solution.py:633
  46.8 1.7 %collective-permute-done.14.refs_1_ = bf16[224,128]{1,0:T(8,128)(2,1)S(1)} collective-permute-done((bf16[224,128]{1,0:T(8,128)(2,1)S(1)}, bf16[224,128]{1,0:T(8,128)(2,1)S(1)}, u32[]{:S(2)}, u32[]{:S(2)}) %collective-permute-start.14) | collective-permute-done | bytes 57376 | tf_op jit(solution)/shard_map/ppermute | solution.py:633
  48.6 1.2 %collective-permute-done.15.refs_2_ = bf16[224,128]{1,0:T(8,128)(2,1)S(1)} collective-permute-done((bf16[224,128]{1,0:T(8,128)(2,1)S(1)}, bf16[224,128]{1,0:T(8,128)(2,1)S(1)}, u32[]{:S(2)}, u32[]{:S(2)}) %collective-permute-start.15) | collective-permute-done | bytes 57376 | tf_op jit(solution)/shard_map/ppermute | solution.py:633
  49.8 2.5 %collective-permute-start.19 = (bf16[224,128]{1,0:T(8,128)(2,1)S(1)}, bf16[224,128]{1,0:T(8,128)(2,1)S(1)}, u32[]{:S(2)}, u32[]{:S(2)}) collective-permute-start(bf16[224,128]{1,0:T(8,128)(2,1)S(1)} %shard_map.127.refs_0_), channel_id=1, source_target_pairs={{0,6},{1,7},{2,4},{3,5},{4,2},{5,3},{6,0},{7,1},{8,14},{9,15},{10,... | collective-permute-start | bytes 172040 | tf_op jit(solution)/shard_map/ppermute | solution.py:633
  52.6 1.7 %collective-permute-start.17 = (bf16[224,128]{1,0:T(8,128)(2,1)S(1)}, bf16[224,128]{1,0:T(8,128)(2,1)S(1)}, u32[]{:S(2)}, u32[]{:S(2)}) collective-permute-start(bf16[224,128]{1,0:T(8,128)(2,1)S(1)} %shard_map.127.refs_0_), channel_id=1, source_target_pairs={{0,2},{1,3},{2,0},{3,1},{4,6},{5,7},{6,4},{7,5},{8,10},{9,11},{10,... | collective-permute-start | bytes 172040 | tf_op jit(solution)/shard_map/ppermute | solution.py:633
  54.3 1.6 %collective-permute-done.19.refs_3_ = bf16[224,128]{1,0:T(8,128)(2,1)S(1)} collective-permute-done((bf16[224,128]{1,0:T(8,128)(2,1)S(1)}, bf16[224,128]{1,0:T(8,128)(2,1)S(1)}, u32[]{:S(2)}, u32[]{:S(2)}) %collective-permute-start.19) | collective-permute-done | bytes 57376 | tf_op jit(solution)/shard_map/ppermute | solution.py:633
  55.9 1.6 %collective-permute-done.18.refs_2_ = bf16[224,128]{1,0:T(8,128)(2,1)S(1)} collective-permute-done((bf16[224,128]{1,0:T(8,128)(2,1)S(1)}, bf16[224,128]{1,0:T(8,128)(2,1)S(1)}, u32[]{:S(2)}, u32[]{:S(2)}) %collective-permute-start.18) | collective-permute-done | bytes 57376 | tf_op jit(solution)/shard_map/ppermute | solution.py:633
  57.5 1.6 %collective-permute-start.25 = (bf16[896,128]{1,0:T(8,128)(2,1)S(1)}, bf16[896,128]{1,0:T(8,128)(2,1)S(1)}, u32[]{:S(2)}, u32[]{:S(2)}) collective-permute-start(bf16[896,128]{1,0:T(8,128)(2,1)S(1)} %shard_map.128.refs_0_), channel_id=1, source_target_pairs={{0,17},{1,16},{2,19},{3,18},{4,21},{5,20},{6,23},{7,22},{8,25},{9,... | collective-permute-start | bytes 688136 | tf_op jit(solution)/shard_map/ppermute | solution.py:633
  59.1 1.5 %collective-permute-start.23 = (bf16[896,128]{1,0:T(8,128)(2,1)S(1)}, bf16[896,128]{1,0:T(8,128)(2,1)S(1)}, u32[]{:S(2)}, u32[]{:S(2)}) collective-permute-start(bf16[896,128]{1,0:T(8,128)(2,1)S(1)} %shard_map.128.refs_0_), channel_id=1, source_target_pairs={{0,16},{1,17},{2,18},{3,19},{4,20},{5,21},{6,22},{7,23},{8,24},{9,... | collective-permute-start | bytes 688136 | tf_op jit(solution)/shard_map/ppermute | solution.py:633
  61.0 4.5 %collective-permute-done.25.refs_3_ = bf16[896,128]{1,0:T(8,128)(2,1)S(1)} collective-permute-done((bf16[896,128]{1,0:T(8,128)(2,1)S(1)}, bf16[896,128]{1,0:T(8,128)(2,1)S(1)}, u32[]{:S(2)}, u32[]{:S(2)}) %collective-permute-start.25) | collective-permute-done | bytes 229408 | tf_op jit(solution)/shard_map/ppermute | solution.py:633
  65.5 1.9 %collective-permute-done.23.refs_2_ = bf16[896,128]{1,0:T(8,128)(2,1)S(1)} collective-permute-done((bf16[896,128]{1,0:T(8,128)(2,1)S(1)}, bf16[896,128]{1,0:T(8,128)(2,1)S(1)}, u32[]{:S(2)}, u32[]{:S(2)}) %collective-permute-start.23) | collective-permute-done | bytes 229408 | tf_op jit(solution)/shard_map/ppermute | solution.py:633
  67.9 1.5 %shard_map.129 = (f32[2,192,576]{2,1,0:T(8,128)}, f32[2,192,192]{2,1,0:T(8,128)}, f32[2,192,768]{2,1,0:T(8,128)}, f32[2,192,768]{2,1,0:T(8,128)}, f32[6,2,225]{2,1,0:T(2,128)}) custom-call(bf16[896,128]{1,0:T(8,128)(2,1)S(1)} %shard_map.128.refs_0_, bf16[896,128]{1,0:T(8,128)(2,1)S(1)} %collective-permute-done.21.refs_1_, ...), custom_call_target="tpu_custom_call" | custom-call | flops 1320000000 | tf_op jit(solution)/shard_map/pallas_call | solution.py:598
  69.4 1.5 %shard_map.130 = (f32[2,192,576]{2,1,0:T(8,128)}, f32[2,192,192]{2,1,0:T(8,128)}, f32[2,192,768]{2,1,0:T(8,128)}, f32[2,192,768]{2,1,0:T(8,128)}, f32[6,2,225]{2,1,0:T(2,128)}) custom-call(bf16[896,128]{1,0:T(8,128)(2,1)S(1)} %collective-permute-done.20.refs_0_, ...), custom_call_target="tpu_custom_call", output_to_operand_aliasing={{0}: (4, {}), {1}: (5, {}), {2}: (6, {}), {3}: (7, {}), {4}... | custom-call | flops 1320000000 | tf_op jit(solution)/shard_map/pallas_call | solution.py:598
  (51 shorter events, 5.1 us)
Async XLA Ops:
  0.6 11.8 %copy-start = (bf16[2,192,768]{2,1,0:T(8,128)(2,1)S(1)}, bf16[2,192,768]{2,1,0:T(8,128)(2,1)}, u32[]{:S(2)}) copy-start(bf16[2,192,768]{2,1,0:T(8,128)(2,1)} %refs_17_.1) | copy-start | bytes 1769476
  0.6 11.8 %copy-start.2 = (bf16[2,192,576]{2,1,0:T(8,128)(2,1)S(1)}, bf16[2,192,576]{2,1,0:T(8,128)(2,1)}, u32[]{:S(2)}) copy-start(bf16[2,192,576]{2,1,0:T(8,128)(2,1)} %refs_4_.5) | copy-start | bytes 1327108
  0.7 11.8 %copy-start.3 = (bf16[2,192,192]{2,1,0:T(8,128)(2,1)S(1)}, bf16[2,192,192]{2,1,0:T(8,128)(2,1)}, u32[]{:S(2)}) copy-start(bf16[2,192,192]{2,1,0:T(8,128)(2,1)} %refs_16_.1) | copy-start | bytes 442372
  0.7 11.8 %copy-start.4 = (bf16[2,8,16,192]{3,2,1,0:T(8,128)(2,1)S(1)}, bf16[2,8,16,192]{3,2,1,0:T(8,128)(2,1)}, u32[]{:S(2)}) copy-start(bf16[2,8,16,192]{3,2,1,0:T(8,128)(2,1)} %refs_0_.3) | copy-start | bytes 294916
  0.7 11.8 %copy-start.6 = (f32[2,6,225]{2,0,1:T(2,128)S(1)}, f32[2,6,225]{2,0,1:T(2,128)}, u32[]{:S(2)}) copy-start(f32[2,6,225]{2,0,1:T(2,128)} %param.13) | copy-start | bytes 32404
  4.9 9.9 %collective-permute-start.1 = (bf16[64,192]{1,0:T(8,128)(2,1)}, bf16[64,192]{1,0:T(8,128)(2,1)S(1)}, u32[]{:S(2)}, u32[]{:S(2)}) collective-permute-start(bf16[64,192]{1,0:T(8,128)(2,1)} %get-tuple-element.63), channel_id=1, source_target_pairs={{0,31},{1,24},{2,25},{3,26},{4,27},{5,28},{6,29},{7,30},{8,7},{9,0... | collective-permute-start | bytes 73736 | tf_op jit(solution)/shard_map/ppermute | solution.py:627
  11.4 4.1 %collective-permute-start.2 = (bf16[64,192]{1,0:T(8,128)(2,1)}, bf16[64,192]{1,0:T(8,128)(2,1)S(1)}, u32[]{:S(2)}, u32[]{:S(2)}) collective-permute-start(bf16[64,192]{1,0:T(8,128)(2,1)} %get-tuple-element.64), channel_id=1, source_target_pairs={{0,7},{1,0},{2,1},{3,2},{4,3},{5,4},{6,5},{7,6},{8,15},{9,8},{10,9... | collective-permute-start | bytes 73736 | tf_op jit(solution)/shard_map/ppermute | solution.py:627
  11.9 3.6 %collective-permute-start = (bf16[2,2,4,16,192]{4,3,2,1,0:T(8,128)(2,1)}, bf16[2,2,4,16,192]{4,3,2,1,0:T(8,128)(2,1)S(1)}, u32[]{:S(2)}, u32[]{:S(2)}) collective-permute-start(bf16[2,2,4,16,192]{4,3,2,1,0:T(8,128)(2,1)} %get-tuple-element.62), channel_id=1, source_target_pairs={{0,24},{1,25},{2,26},{3,27},{4,28},{5,29},{6,30},{7,31},{8,0},{9,1... | collective-permute-start | bytes 294920 | tf_op jit(solution)/shard_map/ppermute | solution.py:627
  19.9 3.1 %collective-permute-start.6 = (bf16[1792,128]{1,0:T(8,128)(2,1)S(1)}, bf16[1792,128]{1,0:T(8,128)(2,1)S(1)}, u32[]{:S(2)}, u32[]{:S(2)}) collective-permute-start(bf16[1792,128]{1,0:T(8,128)(2,1)S(1)} %get-tuple-element.72), channel_id=1, source_target_pairs={{0,8},{1,9},{2,10},{3,11},{4,12},{5,13},{6,14},{7,15},{8,0},{9,1},... | collective-permute-start | bytes 1376264 | tf_op jit(solution)/shard_map/ppermute | solution.py:633
  20.4 6.9 %collective-permute-start.4 = (bf16[32,192]{1,0:T(8,128)(2,1)S(1)}, bf16[32,192]{1,0:T(8,128)(2,1)S(1)}, u32[]{:S(2)}, u32[]{:S(2)}) collective-permute-start(bf16[32,192]{1,0:T(8,128)(2,1)S(1)} %get-tuple-element.68), channel_id=1, source_target_pairs={{0,9},{1,10},{2,11},{3,12},{4,13},{5,14},{6,15},{7,8},{8,17},{9,18... | collective-permute-start | bytes 36872 | tf_op jit(solution)/shard_map/ppermute | solution.py:627
  21.6 6.5 %collective-permute-start.5 = (bf16[32,192]{1,0:T(8,128)(2,1)S(1)}, bf16[32,192]{1,0:T(8,128)(2,1)S(1)}, u32[]{:S(2)}, u32[]{:S(2)}) collective-permute-start(bf16[32,192]{1,0:T(8,128)(2,1)S(1)} %get-tuple-element.69), channel_id=1, source_target_pairs={{0,1},{1,2},{2,3},{3,4},{4,5},{5,6},{6,7},{7,0},{8,9},{9,10},{10,1... | collective-permute-start | bytes 36872 | tf_op jit(solution)/shard_map/ppermute | solution.py:627
  22.0 6.2 %collective-permute-start.3 = (bf16[2,4,16,192]{3,2,1,0:T(8,128)(2,1)S(1)}, bf16[2,4,16,192]{3,2,1,0:T(8,128)(2,1)S(1)}, u32[]{:S(2)}, u32[]{:S(2)}) collective-permute-start(bf16[2,4,16,192]{3,2,1,0:T(8,128)(2,1)S(1)} %get-tuple-element.67), channel_id=1, source_target_pairs={{0,8},{1,9},{2,10},{3,11},{4,12},{5,13},{6,14},{7,15},{8,16},{9,17... | collective-permute-start | bytes 147464 | tf_op jit(solution)/shard_map/ppermute | solution.py:627
  23.2 7.9 %collective-permute-start.8 = (bf16[448,128]{1,0:T(8,128)(2,1)S(1)}, bf16[448,128]{1,0:T(8,128)(2,1)S(1)}, u32[]{:S(2)}, u32[]{:S(2)}) collective-permute-start(bf16[448,128]{1,0:T(8,128)(2,1)S(1)} %get-tuple-element.91), channel_id=1, source_target_pairs={{0,1},{1,0},{2,3},{3,2},{4,5},{5,4},{6,7},{7,6},{8,9},{9,8},{10,11... | collective-permute-start | bytes 344072 | tf_op jit(solution)/shard_map/ppermute | solution.py:633
  23.7 7.5 %collective-permute-start.9 = (bf16[448,128]{1,0:T(8,128)(2,1)S(1)}, bf16[448,128]{1,0:T(8,128)(2,1)S(1)}, u32[]{:S(2)}, u32[]{:S(2)}) collective-permute-start(bf16[448,128]{1,0:T(8,128)(2,1)S(1)} %get-tuple-element.92), channel_id=1, source_target_pairs={{0,16},{1,17},{2,18},{3,19},{4,20},{5,21},{6,22},{7,23},{8,24},{9,... | collective-permute-start | bytes 344072 | tf_op jit(solution)/shard_map/ppermute | solution.py:633
  27.3 5.7 %collective-permute-start.10 = (bf16[448,128]{1,0:T(8,128)(2,1)S(1)}, bf16[448,128]{1,0:T(8,128)(2,1)S(1)}, u32[]{:S(2)}, u32[]{:S(2)}) collective-permute-start(bf16[448,128]{1,0:T(8,128)(2,1)S(1)} %get-tuple-element.93), channel_id=1, source_target_pairs={{0,17},{1,16},{2,19},{3,18},{4,21},{5,20},{6,23},{7,22},{8,25},{9,... | collective-permute-start | bytes 344072 | tf_op jit(solution)/shard_map/ppermute | solution.py:633
  30.9 2.2 %collective-permute-start.7 = (bf16[1792,128]{1,0:T(8,128)(2,1)S(1)}, bf16[1792,128]{1,0:T(8,128)(2,1)S(1)}, u32[]{:S(2)}, u32[]{:S(2)}) collective-permute-start(bf16[1792,128]{1,0:T(8,128)(2,1)S(1)} %get-tuple-element.89), channel_id=1, source_target_pairs={{0,8},{1,9},{2,10},{3,11},{4,12},{5,13},{6,14},{7,15},{8,0},{9,1},... | collective-permute-start | bytes 1376264 | tf_op jit(solution)/shard_map/ppermute | solution.py:633
  33.3 5.3 %collective-permute-start.11 = (bf16[448,128]{1,0:T(8,128)(2,1)S(1)}, bf16[448,128]{1,0:T(8,128)(2,1)S(1)}, u32[]{:S(2)}, u32[]{:S(2)}) collective-permute-start(bf16[448,128]{1,0:T(8,128)(2,1)S(1)} %get-tuple-element.99), channel_id=1, source_target_pairs={{0,1},{1,0},{2,3},{3,2},{4,5},{5,4},{6,7},{7,6},{8,9},{9,8},{10,11... | collective-permute-start | bytes 344072 | tf_op jit(solution)/shard_map/ppermute | solution.py:633
  35.1 6.0 %collective-permute-start.12 = (bf16[448,128]{1,0:T(8,128)(2,1)S(1)}, bf16[448,128]{1,0:T(8,128)(2,1)S(1)}, u32[]{:S(2)}, u32[]{:S(2)}) collective-permute-start(bf16[448,128]{1,0:T(8,128)(2,1)S(1)} %get-tuple-element.100), channel_id=1, source_target_pairs={{0,16},{1,17},{2,18},{3,19},{4,20},{5,21},{6,22},{7,23},{8,24},{9,... | collective-permute-start | bytes 344072 | tf_op jit(solution)/shard_map/ppermute | solution.py:633
  35.7 6.6 %collective-permute-start.13 = (bf16[448,128]{1,0:T(8,128)(2,1)S(1)}, bf16[448,128]{1,0:T(8,128)(2,1)S(1)}, u32[]{:S(2)}, u32[]{:S(2)}) collective-permute-start(bf16[448,128]{1,0:T(8,128)(2,1)S(1)} %get-tuple-element.101), channel_id=1, source_target_pairs={{0,17},{1,16},{2,19},{3,18},{4,21},{5,20},{6,23},{7,22},{8,25},{9,... | collective-permute-start | bytes 344072 | tf_op jit(solution)/shard_map/ppermute | solution.py:633
  42.4 6.2 %collective-permute-start.14 = (bf16[224,128]{1,0:T(8,128)(2,1)S(1)}, bf16[224,128]{1,0:T(8,128)(2,1)S(1)}, u32[]{:S(2)}, u32[]{:S(2)}) collective-permute-start(bf16[224,128]{1,0:T(8,128)(2,1)S(1)} %get-tuple-element.103), channel_id=1, source_target_pairs={{0,6},{1,7},{2,4},{3,5},{4,2},{5,3},{6,0},{7,1},{8,14},{9,15},{10,... | collective-permute-start | bytes 172040 | tf_op jit(solution)/shard_map/ppermute | solution.py:633
  44.6 5.2 %collective-permute-start.15 = (bf16[224,128]{1,0:T(8,128)(2,1)S(1)}, bf16[224,128]{1,0:T(8,128)(2,1)S(1)}, u32[]{:S(2)}, u32[]{:S(2)}) collective-permute-start(bf16[224,128]{1,0:T(8,128)(2,1)S(1)} %get-tuple-element.104), channel_id=1, source_target_pairs={{0,4},{1,5},{2,6},{3,7},{4,0},{5,1},{6,2},{7,3},{8,12},{9,13},{10,... | collective-permute-start | bytes 172040 | tf_op jit(solution)/shard_map/ppermute | solution.py:633
  44.6 5.2 %collective-permute-start.16 = (bf16[224,128]{1,0:T(8,128)(2,1)S(1)}, bf16[224,128]{1,0:T(8,128)(2,1)S(1)}, u32[]{:S(2)}, u32[]{:S(2)}) collective-permute-start(bf16[224,128]{1,0:T(8,128)(2,1)S(1)} %get-tuple-element.105), channel_id=1, source_target_pairs={{0,2},{1,3},{2,0},{3,1},{4,6},{5,7},{6,4},{7,5},{8,10},{9,11},{10,... | collective-permute-start | bytes 172040 | tf_op jit(solution)/shard_map/ppermute | solution.py:633
  49.8 6.0 %collective-permute-start.19 = (bf16[224,128]{1,0:T(8,128)(2,1)S(1)}, bf16[224,128]{1,0:T(8,128)(2,1)S(1)}, u32[]{:S(2)}, u32[]{:S(2)}) collective-permute-start(bf16[224,128]{1,0:T(8,128)(2,1)S(1)} %shard_map.127.refs_0_), channel_id=1, source_target_pairs={{0,6},{1,7},{2,4},{3,5},{4,2},{5,3},{6,0},{7,1},{8,14},{9,15},{10,... | collective-permute-start | bytes 172040 | tf_op jit(solution)/shard_map/ppermute | solution.py:633
  52.3 5.2 %collective-permute-start.18 = (bf16[224,128]{1,0:T(8,128)(2,1)S(1)}, bf16[224,128]{1,0:T(8,128)(2,1)S(1)}, u32[]{:S(2)}, u32[]{:S(2)}) collective-permute-start(bf16[224,128]{1,0:T(8,128)(2,1)S(1)} %shard_map.127.refs_0_), channel_id=1, source_target_pairs={{0,4},{1,5},{2,6},{3,7},{4,0},{5,1},{6,2},{7,3},{8,12},{9,13},{10,... | collective-permute-start | bytes 172040 | tf_op jit(solution)/shard_map/ppermute | solution.py:633
  52.6 4.9 %collective-permute-start.17 = (bf16[224,128]{1,0:T(8,128)(2,1)S(1)}, bf16[224,128]{1,0:T(8,128)(2,1)S(1)}, u32[]{:S(2)}, u32[]{:S(2)}) collective-permute-start(bf16[224,128]{1,0:T(8,128)(2,1)S(1)} %shard_map.127.refs_0_), channel_id=1, source_target_pairs={{0,2},{1,3},{2,0},{3,1},{4,6},{5,7},{6,4},{7,5},{8,10},{9,11},{10,... | collective-permute-start | bytes 172040 | tf_op jit(solution)/shard_map/ppermute | solution.py:633
  57.5 8.0 %collective-permute-start.25 = (bf16[896,128]{1,0:T(8,128)(2,1)S(1)}, bf16[896,128]{1,0:T(8,128)(2,1)S(1)}, u32[]{:S(2)}, u32[]{:S(2)}) collective-permute-start(bf16[896,128]{1,0:T(8,128)(2,1)S(1)} %shard_map.128.refs_0_), channel_id=1, source_target_pairs={{0,17},{1,16},{2,19},{3,18},{4,21},{5,20},{6,23},{7,22},{8,25},{9,... | collective-permute-start | bytes 688136 | tf_op jit(solution)/shard_map/ppermute | solution.py:633
  59.1 8.3 %collective-permute-start.23 = (bf16[896,128]{1,0:T(8,128)(2,1)S(1)}, bf16[896,128]{1,0:T(8,128)(2,1)S(1)}, u32[]{:S(2)}, u32[]{:S(2)}) collective-permute-start(bf16[896,128]{1,0:T(8,128)(2,1)S(1)} %shard_map.128.refs_0_), channel_id=1, source_target_pairs={{0,16},{1,17},{2,18},{3,19},{4,20},{5,21},{6,22},{7,23},{8,24},{9,... | collective-permute-start | bytes 688136 | tf_op jit(solution)/shard_map/ppermute | solution.py:633
  60.6 7.2 %collective-permute-start.21 = (bf16[896,128]{1,0:T(8,128)(2,1)S(1)}, bf16[896,128]{1,0:T(8,128)(2,1)S(1)}, u32[]{:S(2)}, u32[]{:S(2)}) collective-permute-start(bf16[896,128]{1,0:T(8,128)(2,1)S(1)} %shard_map.128.refs_0_), channel_id=1, source_target_pairs={{0,1},{1,0},{2,3},{3,2},{4,5},{5,4},{6,7},{7,6},{8,9},{9,8},{10,11... | collective-permute-start | bytes 688136 | tf_op jit(solution)/shard_map/ppermute | solution.py:633
  61.0 8.3 %collective-permute-start.20 = (bf16[896,128]{1,0:T(8,128)(2,1)S(1)}, bf16[896,128]{1,0:T(8,128)(2,1)S(1)}, u32[]{:S(2)}, u32[]{:S(2)}) collective-permute-start(bf16[896,128]{1,0:T(8,128)(2,1)S(1)} %shard_map.128.refs_0_), channel_id=1, source_target_pairs={{0,8},{1,9},{2,10},{3,11},{4,12},{5,13},{6,14},{7,15},{8,0},{9,1},... | collective-permute-start | bytes 688136 | tf_op jit(solution)/shard_map/ppermute | solution.py:633
  65.5 3.9 %collective-permute-start.26 = (bf16[896,128]{1,0:T(8,128)(2,1)S(1)}, bf16[896,128]{1,0:T(8,128)(2,1)S(1)}, u32[]{:S(2)}, u32[]{:S(2)}) collective-permute-start(bf16[896,128]{1,0:T(8,128)(2,1)S(1)} %collective-permute-done.25.refs_3_), channel_id=1, source_target_pairs={{0,8},{1,9},{2,10},{3,11},{4,12},{5,13},{6,14},{7,15},{8,0},{9,1},... | collective-permute-start | bytes 688136 | tf_op jit(solution)/shard_map/ppermute | solution.py:633
  67.4 2.0 %collective-permute-start.24 = (bf16[896,128]{1,0:T(8,128)(2,1)S(1)}, bf16[896,128]{1,0:T(8,128)(2,1)S(1)}, u32[]{:S(2)}, u32[]{:S(2)}) collective-permute-start(bf16[896,128]{1,0:T(8,128)(2,1)S(1)} %collective-permute-done.23.refs_2_), channel_id=1, source_target_pairs={{0,8},{1,9},{2,10},{3,11},{4,12},{5,13},{6,14},{7,15},{8,0},{9,1},... | collective-permute-start | bytes 688136 | tf_op jit(solution)/shard_map/ppermute | solution.py:633
  67.9 1.5 %collective-permute-start.22 = (bf16[896,128]{1,0:T(8,128)(2,1)S(1)}, bf16[896,128]{1,0:T(8,128)(2,1)S(1)}, u32[]{:S(2)}, u32[]{:S(2)}) collective-permute-start(bf16[896,128]{1,0:T(8,128)(2,1)S(1)} %collective-permute-done.21.refs_1_), channel_id=1, source_target_pairs={{0,8},{1,9},{2,10},{3,11},{4,12},{5,13},{6,14},{7,15},{8,0},{9,1},... | collective-permute-start | bytes 688136 | tf_op jit(solution)/shard_map/ppermute | solution.py:633
  (3 other events, 10.9 us)

commit v7 on v6

--- a/solution.py
+++ b/solution.py
@@ -318,11 +318,13 @@
 def unpack_second(buffer, expand, reduce, sent, table, block, factor):
     take = Taker(buffer, factor)
     width = reduce.shape[0]
-    for which, one in enumerate((expand, reduce)):
+    for which, one in ((1, reduce), (0, expand)):
+        take.at = which * expand.shape[1] // 128 * width
         for n in range(one.shape[1] // 128):
             one[:, 128 * n : 128 * n + 128] = take(width)
         sent(which)
-    vectors = buffer[take.at : take.at + 16, :]
+    at = (expand.shape[1] + reduce.shape[1]) // 128 * width
+    vectors = buffer[at : at + 16, :]
     heads, _, entries = table.shape
     side = 2 * WIN - 1
     shape = (128, entries)

time: 71.2 us -> 71.2 us (level)
  no operation moved by 1% of the time
where the time goes in v7:
time: 71.2 us; the launch traced here: 71 us
  starting transfers between devices  28.8 us (40%)
  waiting for transfers between devices  22.8 us (32%)
  Pallas kernels  18.3 us (26%)
  between operations  0.99 us (1%)
    ppermute x21, waiting for transfers between devices, swap(): return lax.ppermute(block, axes, route)  19.2 us
    ppermute x21, starting transfers between devices, swap(): return lax.ppermute(block, axes, route)  18.8 us
    pallas_call x13, Pallas kernels, call(): pl.pallas_call(body, in_specs=[here] * (count + len(stacked)) + [there] *...  18.3 us
    ppermute x6, starting transfers between devices, send(): return lax.ppermute(block, axes, route)  10.1 us
    ppermute x6, waiting for transfers between devices, send(): return lax.ppermute(block, axes, route)  3.66 us
  transfers between devices with their start and end apart: 27, of which 14 were waited for; matrix products, arithmetic and copies ran while one was open for 0% of the time, Pallas kernels for 11%

profile of v7, /device:TPU:0, one launch (start us, length us, event | category | flops | bytes accessed | tf_op | source)
XLA Modules:
  0.0 71.0 jit_solution(15044095193562261677)
XLA Ops:
  0.7 4.3 %shard_map.118 = (f32[2,4,16,192]{3,2,1,0:T(8,128)}, bf16[2,2,4,16,192]{4,3,2,1,0:T(8,128)(2,1)}, bf16[64,192]{1,0:T(8,128)(2,1)}, bf16[64,192]{1,0:T(8,128)(2,1)}) custom-call(bf16[2,8,16,192]{3,2,1,0:T(8,128)(2,1)} %refs_0_.3, bf16[2,8,16,192]{3,2,1,0:T(8,128)(2,1)} %refs_1_.3, f32[6,2,225]{2,1,0:T(2,128)} %bitcast.7, bf16[2,192,576]{2,1,0:T(8,128)(2,1)} %refs_4_.5, ...), custom_call_target="tpu_custom_call" | custom-call | flops 2529999872 | tf_op jit(solution)/shard_map/pallas_call | solution.py:600
  4.9 6.4 %collective-permute-start.1 = (bf16[64,192]{1,0:T(8,128)(2,1)}, bf16[64,192]{1,0:T(8,128)(2,1)S(1)}, u32[]{:S(2)}, u32[]{:S(2)}) collective-permute-start(bf16[64,192]{1,0:T(8,128)(2,1)} %get-tuple-element.63), channel_id=1, source_target_pairs={{0,31},{1,24},{2,25},{3,26},{4,27},{5,28},{6,29},{7,30},{8,7},{9,0... | collective-permute-start | bytes 73736 | tf_op jit(solution)/shard_map/ppermute | solution.py:629
  12.5 2.3 %shard_map.119 = (f32[384,128]{1,0:T(8,128)S(1)}, f32[768,256]{1,0:T(8,128)S(1)}, f32[192,256]{1,0:T(8,128)S(1)}, f32[1,256]{1,0:T(1,128)S(1)}, bf16[192,256]{1,...) custom-call(bf16[2,8,16,192]{3,2,1,0:T(8,128)(2,1)S(1)} %copy-done.4, ...), custom_call_target="tpu_custom_call" | custom-call | flops 2529999872 | tf_op jit(solution)/shard_map/pallas_call | solution.py:600
  14.8 0.7 collective-permute-done.2.refs_4_
  15.5 4.4 %shard_map.120 = (f32[2,4,16,192]{3,2,1,0:T(8,128)S(1)}, bf16[2,4,16,192]{3,2,1,0:T(8,128)(2,1)S(1)}, bf16[32,192]{1,0:T(8,128)(2,1)S(1)}, bf16[32,192]{1,0:T(8,...) custom-call(f32[2,4,16,192]{3,2,1,0:T(8,128)S(1)} %copy-done.7, ...), custom_call_target="tpu_custom_call" | custom-call | flops 5280000000 | tf_op jit(solution)/shard_map/pallas_call | solution.py:600
  20.4 1.2 %collective-permute-start.4 = (bf16[32,192]{1,0:T(8,128)(2,1)S(1)}, bf16[32,192]{1,0:T(8,128)(2,1)S(1)}, u32[]{:S(2)}, u32[]{:S(2)}) collective-permute-start(bf16[32,192]{1,0:T(8,128)(2,1)S(1)} %get-tuple-element.68), channel_id=1, source_target_pairs={{0,9},{1,10},{2,11},{3,12},{4,13},{5,14},{6,15},{7,8},{8,17},{9,18... | collective-permute-start | bytes 36872 | tf_op jit(solution)/shard_map/ppermute | solution.py:629
  22.0 1.0 %collective-permute-start.3 = (bf16[2,4,16,192]{3,2,1,0:T(8,128)(2,1)S(1)}, bf16[2,4,16,192]{3,2,1,0:T(8,128)(2,1)S(1)}, u32[]{:S(2)}, u32[]{:S(2)}) collective-permute-start(bf16[2,4,16,192]{3,2,1,0:T(8,128)(2,1)S(1)} %get-tuple-element.67), channel_id=1, source_target_pairs={{0,8},{1,9},{2,10},{3,11},{4,12},{5,13},{6,14},{7,15},{8,16},{9,17... | collective-permute-start | bytes 147464 | tf_op jit(solution)/shard_map/ppermute | solution.py:629
  23.7 1.5 %collective-permute-start.9 = (bf16[448,128]{1,0:T(8,128)(2,1)S(1)}, bf16[448,128]{1,0:T(8,128)(2,1)S(1)}, u32[]{:S(2)}, u32[]{:S(2)}) collective-permute-start(bf16[448,128]{1,0:T(8,128)(2,1)S(1)} %get-tuple-element.92), channel_id=1, source_target_pairs={{0,16},{1,17},{2,18},{3,19},{4,20},{5,21},{6,22},{7,23},{8,24},{9,... | collective-permute-start | bytes 344072 | tf_op jit(solution)/shard_map/ppermute | solution.py:635
  25.2 2.1 %collective-permute-done.4.refs_2_ = bf16[32,192]{1,0:T(8,128)(2,1)S(1)} collective-permute-done((bf16[32,192]{1,0:T(8,128)(2,1)S(1)}, bf16[32,192]{1,0:T(8,128)(2,1)S(1)}, u32[]{:S(2)}, u32[]{:S(2)}) %collective-permute-start.4) | collective-permute-done | bytes 12320 | tf_op jit(solution)/shard_map/ppermute | solution.py:629
  27.3 0.9 %collective-permute-done.5.refs_3_ = bf16[32,192]{1,0:T(8,128)(2,1)S(1)} collective-permute-done((bf16[32,192]{1,0:T(8,128)(2,1)S(1)}, bf16[32,192]{1,0:T(8,128)(2,1)S(1)}, u32[]{:S(2)}, u32[]{:S(2)}) %collective-permute-start.5) | collective-permute-done | bytes 12320 | tf_op jit(solution)/shard_map/ppermute | solution.py:629
  28.2 2.7 %shard_map.122 = (bf16[1792,128]{1,0:T(8,128)(2,1)S(1)}, bf16[1792,128]{1,0:T(8,128)(2,1)S(1)}, bf16[576,256]{1,0:T(8,128)(2,1)S(1)}, f32[192,256]{1,0:T(8,128)S(1)}) custom-call(f32[2,4,16,192]{3,2,1,0:T(8,128)S(1)} %get-tuple-element.66.refs_0_, bf16[2,4,16,192]{3,2,1,0:T(8,128)(2,1)S(1)} %collective-permute-done.3.refs_1_, ...), custom_call_target="tpu_custom_call" | custom-call | flops 3300000000 | tf_op jit(solution)/shard_map/pallas_call | solution.py:600
  31.1 1.9 %collective-permute-done.10.refs_3_ = bf16[448,128]{1,0:T(8,128)(2,1)S(1)} collective-permute-done((bf16[448,128]{1,0:T(8,128)(2,1)S(1)}, bf16[448,128]{1,0:T(8,128)(2,1)S(1)}, u32[]{:S(2)}, u32[]{:S(2)}) %collective-permute-start.10) | collective-permute-done | bytes 114720 | tf_op jit(solution)/shard_map/ppermute | solution.py:635
  33.3 1.9 %collective-permute-start.11 = (bf16[448,128]{1,0:T(8,128)(2,1)S(1)}, bf16[448,128]{1,0:T(8,128)(2,1)S(1)}, u32[]{:S(2)}, u32[]{:S(2)}) collective-permute-start(bf16[448,128]{1,0:T(8,128)(2,1)S(1)} %get-tuple-element.99), channel_id=1, source_target_pairs={{0,1},{1,0},{2,3},{3,2},{4,5},{5,4},{6,7},{7,6},{8,9},{9,8},{10,11... | collective-permute-start | bytes 344072 | tf_op jit(solution)/shard_map/ppermute | solution.py:635
  35.7 1.1 %collective-permute-start.13 = (bf16[448,128]{1,0:T(8,128)(2,1)S(1)}, bf16[448,128]{1,0:T(8,128)(2,1)S(1)}, u32[]{:S(2)}, u32[]{:S(2)}) collective-permute-start(bf16[448,128]{1,0:T(8,128)(2,1)S(1)} %get-tuple-element.101), channel_id=1, source_target_pairs={{0,17},{1,16},{2,19},{3,18},{4,21},{5,20},{6,23},{7,22},{8,25},{9,... | collective-permute-start | bytes 344072 | tf_op jit(solution)/shard_map/ppermute | solution.py:635
  36.8 1.1 %shard_map.125 = f32[2,8,16,192]{3,2,1,0:T(8,128)} custom-call(bf16[576,256]{1,0:T(8,128)(2,1)S(1)} %get-tuple-element.95.refs_0_, f32[192,256]{1,0:T(8,128)S(1)} %get-tuple-element.96.refs_1_, f32[192,256]{1,0:T(8,128)S(1)} %get-tuple-element.78.refs_5_.refs_2_, f32[1,256]{1,0:T(1,128)S(1)} %get-tuple-element.79.refs_6_.refs_3_, ...), custom_call_target="tpu_custom_call" | custom-call | flops 1100000000 | tf_op jit(solution)/shard_map/pallas_call | solution.py:600
  37.9 0.7 collective-permute-done.11.refs_1_
  38.6 2.6 %collective-permute-done.12.refs_2_ = bf16[448,128]{1,0:T(8,128)(2,1)S(1)} collective-permute-done((bf16[448,128]{1,0:T(8,128)(2,1)S(1)}, bf16[448,128]{1,0:T(8,128)(2,1)S(1)}, u32[]{:S(2)}, u32[]{:S(2)}) %collective-permute-start.12) | collective-permute-done | bytes 114720 | tf_op jit(solution)/shard_map/ppermute | solution.py:635
  41.2 1.1 %collective-permute-done.13.refs_3_ = bf16[448,128]{1,0:T(8,128)(2,1)S(1)} collective-permute-done((bf16[448,128]{1,0:T(8,128)(2,1)S(1)}, bf16[448,128]{1,0:T(8,128)(2,1)S(1)}, u32[]{:S(2)}, u32[]{:S(2)}) %collective-permute-start.13) | collective-permute-done | bytes 114720 | tf_op jit(solution)/shard_map/ppermute | solution.py:635
  42.4 2.2 %collective-permute-start.14 = (bf16[224,128]{1,0:T(8,128)(2,1)S(1)}, bf16[224,128]{1,0:T(8,128)(2,1)S(1)}, u32[]{:S(2)}, u32[]{:S(2)}) collective-permute-start(bf16[224,128]{1,0:T(8,128)(2,1)S(1)} %get-tuple-element.103), channel_id=1, source_target_pairs={{0,6},{1,7},{2,4},{3,5},{4,2},{5,3},{6,0},{7,1},{8,14},{9,15},{10,... | collective-permute-start | bytes 172040 | tf_op jit(solution)/shard_map/ppermute | solution.py:635
  44.6 2.3 %collective-permute-start.16 = (bf16[224,128]{1,0:T(8,128)(2,1)S(1)}, bf16[224,128]{1,0:T(8,128)(2,1)S(1)}, u32[]{:S(2)}, u32[]{:S(2)}) collective-permute-start(bf16[224,128]{1,0:T(8,128)(2,1)S(1)} %get-tuple-element.105), channel_id=1, source_target_pairs={{0,2},{1,3},{2,0},{3,1},{4,6},{5,7},{6,4},{7,5},{8,10},{9,11},{10,... | collective-permute-start | bytes 172040 | tf_op jit(solution)/shard_map/ppermute | solution.py:635
  46.8 1.7 %collective-permute-done.14.refs_1_ = bf16[224,128]{1,0:T(8,128)(2,1)S(1)} collective-permute-done((bf16[224,128]{1,0:T(8,128)(2,1)S(1)}, bf16[224,128]{1,0:T(8,128)(2,1)S(1)}, u32[]{:S(2)}, u32[]{:S(2)}) %collective-permute-start.14) | collective-permute-done | bytes 57376 | tf_op jit(solution)/shard_map/ppermute | solution.py:635
  48.6 1.2 %collective-permute-done.15.refs_2_ = bf16[224,128]{1,0:T(8,128)(2,1)S(1)} collective-permute-done((bf16[224,128]{1,0:T(8,128)(2,1)S(1)}, bf16[224,128]{1,0:T(8,128)(2,1)S(1)}, u32[]{:S(2)}, u32[]{:S(2)}) %collective-permute-start.15) | collective-permute-done | bytes 57376 | tf_op jit(solution)/shard_map/ppermute | solution.py:635
  49.8 2.5 %collective-permute-start.19 = (bf16[224,128]{1,0:T(8,128)(2,1)S(1)}, bf16[224,128]{1,0:T(8,128)(2,1)S(1)}, u32[]{:S(2)}, u32[]{:S(2)}) collective-permute-start(bf16[224,128]{1,0:T(8,128)(2,1)S(1)} %shard_map.127.refs_0_), channel_id=1, source_target_pairs={{0,6},{1,7},{2,4},{3,5},{4,2},{5,3},{6,0},{7,1},{8,14},{9,15},{10,... | collective-permute-start | bytes 172040 | tf_op jit(solution)/shard_map/ppermute | solution.py:635
  52.6 1.7 %collective-permute-start.17 = (bf16[224,128]{1,0:T(8,128)(2,1)S(1)}, bf16[224,128]{1,0:T(8,128)(2,1)S(1)}, u32[]{:S(2)}, u32[]{:S(2)}) collective-permute-start(bf16[224,128]{1,0:T(8,128)(2,1)S(1)} %shard_map.127.refs_0_), channel_id=1, source_target_pairs={{0,2},{1,3},{2,0},{3,1},{4,6},{5,7},{6,4},{7,5},{8,10},{9,11},{10,... | collective-permute-start | bytes 172040 | tf_op jit(solution)/shard_map/ppermute | solution.py:635
  54.3 1.6 %collective-permute-done.19.refs_3_ = bf16[224,128]{1,0:T(8,128)(2,1)S(1)} collective-permute-done((bf16[224,128]{1,0:T(8,128)(2,1)S(1)}, bf16[224,128]{1,0:T(8,128)(2,1)S(1)}, u32[]{:S(2)}, u32[]{:S(2)}) %collective-permute-start.19) | collective-permute-done | bytes 57376 | tf_op jit(solution)/shard_map/ppermute | solution.py:635
  55.9 1.6 %collective-permute-done.18.refs_2_ = bf16[224,128]{1,0:T(8,128)(2,1)S(1)} collective-permute-done((bf16[224,128]{1,0:T(8,128)(2,1)S(1)}, bf16[224,128]{1,0:T(8,128)(2,1)S(1)}, u32[]{:S(2)}, u32[]{:S(2)}) %collective-permute-start.18) | collective-permute-done | bytes 57376 | tf_op jit(solution)/shard_map/ppermute | solution.py:635
  57.5 1.6 %collective-permute-start.25 = (bf16[896,128]{1,0:T(8,128)(2,1)S(1)}, bf16[896,128]{1,0:T(8,128)(2,1)S(1)}, u32[]{:S(2)}, u32[]{:S(2)}) collective-permute-start(bf16[896,128]{1,0:T(8,128)(2,1)S(1)} %shard_map.128.refs_0_), channel_id=1, source_target_pairs={{0,17},{1,16},{2,19},{3,18},{4,21},{5,20},{6,23},{7,22},{8,25},{9,... | collective-permute-start | bytes 688136 | tf_op jit(solution)/shard_map/ppermute | solution.py:635
  59.1 1.5 %collective-permute-start.23 = (bf16[896,128]{1,0:T(8,128)(2,1)S(1)}, bf16[896,128]{1,0:T(8,128)(2,1)S(1)}, u32[]{:S(2)}, u32[]{:S(2)}) collective-permute-start(bf16[896,128]{1,0:T(8,128)(2,1)S(1)} %shard_map.128.refs_0_), channel_id=1, source_target_pairs={{0,16},{1,17},{2,18},{3,19},{4,20},{5,21},{6,22},{7,23},{8,24},{9,... | collective-permute-start | bytes 688136 | tf_op jit(solution)/shard_map/ppermute | solution.py:635
  61.0 4.5 %collective-permute-done.25.refs_3_ = bf16[896,128]{1,0:T(8,128)(2,1)S(1)} collective-permute-done((bf16[896,128]{1,0:T(8,128)(2,1)S(1)}, bf16[896,128]{1,0:T(8,128)(2,1)S(1)}, u32[]{:S(2)}, u32[]{:S(2)}) %collective-permute-start.25) | collective-permute-done | bytes 229408 | tf_op jit(solution)/shard_map/ppermute | solution.py:635
  65.5 1.9 %collective-permute-done.23.refs_2_ = bf16[896,128]{1,0:T(8,128)(2,1)S(1)} collective-permute-done((bf16[896,128]{1,0:T(8,128)(2,1)S(1)}, bf16[896,128]{1,0:T(8,128)(2,1)S(1)}, u32[]{:S(2)}, u32[]{:S(2)}) %collective-permute-start.23) | collective-permute-done | bytes 229408 | tf_op jit(solution)/shard_map/ppermute | solution.py:635
  67.9 1.5 %shard_map.129 = (f32[2,192,576]{2,1,0:T(8,128)}, f32[2,192,192]{2,1,0:T(8,128)}, f32[2,192,768]{2,1,0:T(8,128)}, f32[2,192,768]{2,1,0:T(8,128)}, f32[6,2,225]{2,1,0:T(2,128)}) custom-call(bf16[896,128]{1,0:T(8,128)(2,1)S(1)} %shard_map.128.refs_0_, bf16[896,128]{1,0:T(8,128)(2,1)S(1)} %collective-permute-done.21.refs_1_, ...), custom_call_target="tpu_custom_call" | custom-call | flops 1320000000 | tf_op jit(solution)/shard_map/pallas_call | solution.py:600
  69.4 1.4 %shard_map.130 = (f32[2,192,576]{2,1,0:T(8,128)}, f32[2,192,192]{2,1,0:T(8,128)}, f32[2,192,768]{2,1,0:T(8,128)}, f32[2,192,768]{2,1,0:T(8,128)}, f32[6,2,225]{2,1,0:T(2,128)}) custom-call(bf16[896,128]{1,0:T(8,128)(2,1)S(1)} %collective-permute-done.20.refs_0_, ...), custom_call_target="tpu_custom_call", output_to_operand_aliasing={{0}: (4, {}), {1}: (5, {}), {2}: (6, {}), {3}: (7, {}), {4}... | custom-call | flops 1320000000 | tf_op jit(solution)/shard_map/pallas_call | solution.py:600
  (51 shorter events, 5.1 us)
Async XLA Ops:
  0.6 11.8 %copy-start = (bf16[2,192,768]{2,1,0:T(8,128)(2,1)S(1)}, bf16[2,192,768]{2,1,0:T(8,128)(2,1)}, u32[]{:S(2)}) copy-start(bf16[2,192,768]{2,1,0:T(8,128)(2,1)} %refs_17_.1) | copy-start | bytes 1769476
  0.6 11.8 %copy-start.2 = (bf16[2,192,576]{2,1,0:T(8,128)(2,1)S(1)}, bf16[2,192,576]{2,1,0:T(8,128)(2,1)}, u32[]{:S(2)}) copy-start(bf16[2,192,576]{2,1,0:T(8,128)(2,1)} %refs_4_.5) | copy-start | bytes 1327108
  0.7 11.8 %copy-start.3 = (bf16[2,192,192]{2,1,0:T(8,128)(2,1)S(1)}, bf16[2,192,192]{2,1,0:T(8,128)(2,1)}, u32[]{:S(2)}) copy-start(bf16[2,192,192]{2,1,0:T(8,128)(2,1)} %refs_16_.1) | copy-start | bytes 442372
  0.7 11.8 %copy-start.4 = (bf16[2,8,16,192]{3,2,1,0:T(8,128)(2,1)S(1)}, bf16[2,8,16,192]{3,2,1,0:T(8,128)(2,1)}, u32[]{:S(2)}) copy-start(bf16[2,8,16,192]{3,2,1,0:T(8,128)(2,1)} %refs_0_.3) | copy-start | bytes 294916
  0.7 11.8 %copy-start.6 = (f32[2,6,225]{2,0,1:T(2,128)S(1)}, f32[2,6,225]{2,0,1:T(2,128)}, u32[]{:S(2)}) copy-start(f32[2,6,225]{2,0,1:T(2,128)} %param.13) | copy-start | bytes 32404
  4.9 9.9 %collective-permute-start.1 = (bf16[64,192]{1,0:T(8,128)(2,1)}, bf16[64,192]{1,0:T(8,128)(2,1)S(1)}, u32[]{:S(2)}, u32[]{:S(2)}) collective-permute-start(bf16[64,192]{1,0:T(8,128)(2,1)} %get-tuple-element.63), channel_id=1, source_target_pairs={{0,31},{1,24},{2,25},{3,26},{4,27},{5,28},{6,29},{7,30},{8,7},{9,0... | collective-permute-start | bytes 73736 | tf_op jit(solution)/shard_map/ppermute | solution.py:629
  11.4 4.1 %collective-permute-start.2 = (bf16[64,192]{1,0:T(8,128)(2,1)}, bf16[64,192]{1,0:T(8,128)(2,1)S(1)}, u32[]{:S(2)}, u32[]{:S(2)}) collective-permute-start(bf16[64,192]{1,0:T(8,128)(2,1)} %get-tuple-element.64), channel_id=1, source_target_pairs={{0,7},{1,0},{2,1},{3,2},{4,3},{5,4},{6,5},{7,6},{8,15},{9,8},{10,9... | collective-permute-start | bytes 73736 | tf_op jit(solution)/shard_map/ppermute | solution.py:629
  11.9 3.6 %collective-permute-start = (bf16[2,2,4,16,192]{4,3,2,1,0:T(8,128)(2,1)}, bf16[2,2,4,16,192]{4,3,2,1,0:T(8,128)(2,1)S(1)}, u32[]{:S(2)}, u32[]{:S(2)}) collective-permute-start(bf16[2,2,4,16,192]{4,3,2,1,0:T(8,128)(2,1)} %get-tuple-element.62), channel_id=1, source_target_pairs={{0,24},{1,25},{2,26},{3,27},{4,28},{5,29},{6,30},{7,31},{8,0},{9,1... | collective-permute-start | bytes 294920 | tf_op jit(solution)/shard_map/ppermute | solution.py:629
  19.9 3.1 %collective-permute-start.6 = (bf16[1792,128]{1,0:T(8,128)(2,1)S(1)}, bf16[1792,128]{1,0:T(8,128)(2,1)S(1)}, u32[]{:S(2)}, u32[]{:S(2)}) collective-permute-start(bf16[1792,128]{1,0:T(8,128)(2,1)S(1)} %get-tuple-element.72), channel_id=1, source_target_pairs={{0,8},{1,9},{2,10},{3,11},{4,12},{5,13},{6,14},{7,15},{8,0},{9,1},... | collective-permute-start | bytes 1376264 | tf_op jit(solution)/shard_map/ppermute | solution.py:635
  20.4 6.9 %collective-permute-start.4 = (bf16[32,192]{1,0:T(8,128)(2,1)S(1)}, bf16[32,192]{1,0:T(8,128)(2,1)S(1)}, u32[]{:S(2)}, u32[]{:S(2)}) collective-permute-start(bf16[32,192]{1,0:T(8,128)(2,1)S(1)} %get-tuple-element.68), channel_id=1, source_target_pairs={{0,9},{1,10},{2,11},{3,12},{4,13},{5,14},{6,15},{7,8},{8,17},{9,18... | collective-permute-start | bytes 36872 | tf_op jit(solution)/shard_map/ppermute | solution.py:629
  21.6 6.5 %collective-permute-start.5 = (bf16[32,192]{1,0:T(8,128)(2,1)S(1)}, bf16[32,192]{1,0:T(8,128)(2,1)S(1)}, u32[]{:S(2)}, u32[]{:S(2)}) collective-permute-start(bf16[32,192]{1,0:T(8,128)(2,1)S(1)} %get-tuple-element.69), channel_id=1, source_target_pairs={{0,1},{1,2},{2,3},{3,4},{4,5},{5,6},{6,7},{7,0},{8,9},{9,10},{10,1... | collective-permute-start | bytes 36872 | tf_op jit(solution)/shard_map/ppermute | solution.py:629
  22.0 6.2 %collective-permute-start.3 = (bf16[2,4,16,192]{3,2,1,0:T(8,128)(2,1)S(1)}, bf16[2,4,16,192]{3,2,1,0:T(8,128)(2,1)S(1)}, u32[]{:S(2)}, u32[]{:S(2)}) collective-permute-start(bf16[2,4,16,192]{3,2,1,0:T(8,128)(2,1)S(1)} %get-tuple-element.67), channel_id=1, source_target_pairs={{0,8},{1,9},{2,10},{3,11},{4,12},{5,13},{6,14},{7,15},{8,16},{9,17... | collective-permute-start | bytes 147464 | tf_op jit(solution)/shard_map/ppermute | solution.py:629
  23.2 7.9 %collective-permute-start.8 = (bf16[448,128]{1,0:T(8,128)(2,1)S(1)}, bf16[448,128]{1,0:T(8,128)(2,1)S(1)}, u32[]{:S(2)}, u32[]{:S(2)}) collective-permute-start(bf16[448,128]{1,0:T(8,128)(2,1)S(1)} %get-tuple-element.91), channel_id=1, source_target_pairs={{0,1},{1,0},{2,3},{3,2},{4,5},{5,4},{6,7},{7,6},{8,9},{9,8},{10,11... | collective-permute-start | bytes 344072 | tf_op jit(solution)/shard_map/ppermute | solution.py:635
  23.7 7.5 %collective-permute-start.9 = (bf16[448,128]{1,0:T(8,128)(2,1)S(1)}, bf16[448,128]{1,0:T(8,128)(2,1)S(1)}, u32[]{:S(2)}, u32[]{:S(2)}) collective-permute-start(bf16[448,128]{1,0:T(8,128)(2,1)S(1)} %get-tuple-element.92), channel_id=1, source_target_pairs={{0,16},{1,17},{2,18},{3,19},{4,20},{5,21},{6,22},{7,23},{8,24},{9,... | collective-permute-start | bytes 344072 | tf_op jit(solution)/shard_map/ppermute | solution.py:635
  27.3 5.7 %collective-permute-start.10 = (bf16[448,128]{1,0:T(8,128)(2,1)S(1)}, bf16[448,128]{1,0:T(8,128)(2,1)S(1)}, u32[]{:S(2)}, u32[]{:S(2)}) collective-permute-start(bf16[448,128]{1,0:T(8,128)(2,1)S(1)} %get-tuple-element.93), channel_id=1, source_target_pairs={{0,17},{1,16},{2,19},{3,18},{4,21},{5,20},{6,23},{7,22},{8,25},{9,... | collective-permute-start | bytes 344072 | tf_op jit(solution)/shard_map/ppermute | solution.py:635
  30.9 2.2 %collective-permute-start.7 = (bf16[1792,128]{1,0:T(8,128)(2,1)S(1)}, bf16[1792,128]{1,0:T(8,128)(2,1)S(1)}, u32[]{:S(2)}, u32[]{:S(2)}) collective-permute-start(bf16[1792,128]{1,0:T(8,128)(2,1)S(1)} %get-tuple-element.89), channel_id=1, source_target_pairs={{0,8},{1,9},{2,10},{3,11},{4,12},{5,13},{6,14},{7,15},{8,0},{9,1},... | collective-permute-start | bytes 1376264 | tf_op jit(solution)/shard_map/ppermute | solution.py:635
  33.3 5.3 %collective-permute-start.11 = (bf16[448,128]{1,0:T(8,128)(2,1)S(1)}, bf16[448,128]{1,0:T(8,128)(2,1)S(1)}, u32[]{:S(2)}, u32[]{:S(2)}) collective-permute-start(bf16[448,128]{1,0:T(8,128)(2,1)S(1)} %get-tuple-element.99), channel_id=1, source_target_pairs={{0,1},{1,0},{2,3},{3,2},{4,5},{5,4},{6,7},{7,6},{8,9},{9,8},{10,11... | collective-permute-start | bytes 344072 | tf_op jit(solution)/shard_map/ppermute | solution.py:635
  35.1 6.0 %collective-permute-start.12 = (bf16[448,128]{1,0:T(8,128)(2,1)S(1)}, bf16[448,128]{1,0:T(8,128)(2,1)S(1)}, u32[]{:S(2)}, u32[]{:S(2)}) collective-permute-start(bf16[448,128]{1,0:T(8,128)(2,1)S(1)} %get-tuple-element.100), channel_id=1, source_target_pairs={{0,16},{1,17},{2,18},{3,19},{4,20},{5,21},{6,22},{7,23},{8,24},{9,... | collective-permute-start | bytes 344072 | tf_op jit(solution)/shard_map/ppermute | solution.py:635
  35.7 6.6 %collective-permute-start.13 = (bf16[448,128]{1,0:T(8,128)(2,1)S(1)}, bf16[448,128]{1,0:T(8,128)(2,1)S(1)}, u32[]{:S(2)}, u32[]{:S(2)}) collective-permute-start(bf16[448,128]{1,0:T(8,128)(2,1)S(1)} %get-tuple-element.101), channel_id=1, source_target_pairs={{0,17},{1,16},{2,19},{3,18},{4,21},{5,20},{6,23},{7,22},{8,25},{9,... | collective-permute-start | bytes 344072 | tf_op jit(solution)/shard_map/ppermute | solution.py:635
  42.4 6.2 %collective-permute-start.14 = (bf16[224,128]{1,0:T(8,128)(2,1)S(1)}, bf16[224,128]{1,0:T(8,128)(2,1)S(1)}, u32[]{:S(2)}, u32[]{:S(2)}) collective-permute-start(bf16[224,128]{1,0:T(8,128)(2,1)S(1)} %get-tuple-element.103), channel_id=1, source_target_pairs={{0,6},{1,7},{2,4},{3,5},{4,2},{5,3},{6,0},{7,1},{8,14},{9,15},{10,... | collective-permute-start | bytes 172040 | tf_op jit(solution)/shard_map/ppermute | solution.py:635
  44.6 5.2 %collective-permute-start.15 = (bf16[224,128]{1,0:T(8,128)(2,1)S(1)}, bf16[224,128]{1,0:T(8,128)(2,1)S(1)}, u32[]{:S(2)}, u32[]{:S(2)}) collective-permute-start(bf16[224,128]{1,0:T(8,128)(2,1)S(1)} %get-tuple-element.104), channel_id=1, source_target_pairs={{0,4},{1,5},{2,6},{3,7},{4,0},{5,1},{6,2},{7,3},{8,12},{9,13},{10,... | collective-permute-start | bytes 172040 | tf_op jit(solution)/shard_map/ppermute | solution.py:635
  44.6 5.2 %collective-permute-start.16 = (bf16[224,128]{1,0:T(8,128)(2,1)S(1)}, bf16[224,128]{1,0:T(8,128)(2,1)S(1)}, u32[]{:S(2)}, u32[]{:S(2)}) collective-permute-start(bf16[224,128]{1,0:T(8,128)(2,1)S(1)} %get-tuple-element.105), channel_id=1, source_target_pairs={{0,2},{1,3},{2,0},{3,1},{4,6},{5,7},{6,4},{7,5},{8,10},{9,11},{10,... | collective-permute-start | bytes 172040 | tf_op jit(solution)/shard_map/ppermute | solution.py:635
  49.8 6.0 %collective-permute-start.19 = (bf16[224,128]{1,0:T(8,128)(2,1)S(1)}, bf16[224,128]{1,0:T(8,128)(2,1)S(1)}, u32[]{:S(2)}, u32[]{:S(2)}) collective-permute-start(bf16[224,128]{1,0:T(8,128)(2,1)S(1)} %shard_map.127.refs_0_), channel_id=1, source_target_pairs={{0,6},{1,7},{2,4},{3,5},{4,2},{5,3},{6,0},{7,1},{8,14},{9,15},{10,... | collective-permute-start | bytes 172040 | tf_op jit(solution)/shard_map/ppermute | solution.py:635
  52.3 5.2 %collective-permute-start.18 = (bf16[224,128]{1,0:T(8,128)(2,1)S(1)}, bf16[224,128]{1,0:T(8,128)(2,1)S(1)}, u32[]{:S(2)}, u32[]{:S(2)}) collective-permute-start(bf16[224,128]{1,0:T(8,128)(2,1)S(1)} %shard_map.127.refs_0_), channel_id=1, source_target_pairs={{0,4},{1,5},{2,6},{3,7},{4,0},{5,1},{6,2},{7,3},{8,12},{9,13},{10,... | collective-permute-start | bytes 172040 | tf_op jit(solution)/shard_map/ppermute | solution.py:635
  52.6 4.9 %collective-permute-start.17 = (bf16[224,128]{1,0:T(8,128)(2,1)S(1)}, bf16[224,128]{1,0:T(8,128)(2,1)S(1)}, u32[]{:S(2)}, u32[]{:S(2)}) collective-permute-start(bf16[224,128]{1,0:T(8,128)(2,1)S(1)} %shard_map.127.refs_0_), channel_id=1, source_target_pairs={{0,2},{1,3},{2,0},{3,1},{4,6},{5,7},{6,4},{7,5},{8,10},{9,11},{10,... | collective-permute-start | bytes 172040 | tf_op jit(solution)/shard_map/ppermute | solution.py:635
  57.5 8.0 %collective-permute-start.25 = (bf16[896,128]{1,0:T(8,128)(2,1)S(1)}, bf16[896,128]{1,0:T(8,128)(2,1)S(1)}, u32[]{:S(2)}, u32[]{:S(2)}) collective-permute-start(bf16[896,128]{1,0:T(8,128)(2,1)S(1)} %shard_map.128.refs_0_), channel_id=1, source_target_pairs={{0,17},{1,16},{2,19},{3,18},{4,21},{5,20},{6,23},{7,22},{8,25},{9,... | collective-permute-start | bytes 688136 | tf_op jit(solution)/shard_map/ppermute | solution.py:635
  59.1 8.3 %collective-permute-start.23 = (bf16[896,128]{1,0:T(8,128)(2,1)S(1)}, bf16[896,128]{1,0:T(8,128)(2,1)S(1)}, u32[]{:S(2)}, u32[]{:S(2)}) collective-permute-start(bf16[896,128]{1,0:T(8,128)(2,1)S(1)} %shard_map.128.refs_0_), channel_id=1, source_target_pairs={{0,16},{1,17},{2,18},{3,19},{4,20},{5,21},{6,22},{7,23},{8,24},{9,... | collective-permute-start | bytes 688136 | tf_op jit(solution)/shard_map/ppermute | solution.py:635
  60.6 7.2 %collective-permute-start.21 = (bf16[896,128]{1,0:T(8,128)(2,1)S(1)}, bf16[896,128]{1,0:T(8,128)(2,1)S(1)}, u32[]{:S(2)}, u32[]{:S(2)}) collective-permute-start(bf16[896,128]{1,0:T(8,128)(2,1)S(1)} %shard_map.128.refs_0_), channel_id=1, source_target_pairs={{0,1},{1,0},{2,3},{3,2},{4,5},{5,4},{6,7},{7,6},{8,9},{9,8},{10,11... | collective-permute-start | bytes 688136 | tf_op jit(solution)/shard_map/ppermute | solution.py:635
  61.0 8.3 %collective-permute-start.20 = (bf16[896,128]{1,0:T(8,128)(2,1)S(1)}, bf16[896,128]{1,0:T(8,128)(2,1)S(1)}, u32[]{:S(2)}, u32[]{:S(2)}) collective-permute-start(bf16[896,128]{1,0:T(8,128)(2,1)S(1)} %shard_map.128.refs_0_), channel_id=1, source_target_pairs={{0,8},{1,9},{2,10},{3,11},{4,12},{5,13},{6,14},{7,15},{8,0},{9,1},... | collective-permute-start | bytes 688136 | tf_op jit(solution)/shard_map/ppermute | solution.py:635
  65.5 3.9 %collective-permute-start.26 = (bf16[896,128]{1,0:T(8,128)(2,1)S(1)}, bf16[896,128]{1,0:T(8,128)(2,1)S(1)}, u32[]{:S(2)}, u32[]{:S(2)}) collective-permute-start(bf16[896,128]{1,0:T(8,128)(2,1)S(1)} %collective-permute-done.25.refs_3_), channel_id=1, source_target_pairs={{0,8},{1,9},{2,10},{3,11},{4,12},{5,13},{6,14},{7,15},{8,0},{9,1},... | collective-permute-start | bytes 688136 | tf_op jit(solution)/shard_map/ppermute | solution.py:635
  67.4 2.0 %collective-permute-start.24 = (bf16[896,128]{1,0:T(8,128)(2,1)S(1)}, bf16[896,128]{1,0:T(8,128)(2,1)S(1)}, u32[]{:S(2)}, u32[]{:S(2)}) collective-permute-start(bf16[896,128]{1,0:T(8,128)(2,1)S(1)} %collective-permute-done.23.refs_2_), channel_id=1, source_target_pairs={{0,8},{1,9},{2,10},{3,11},{4,12},{5,13},{6,14},{7,15},{8,0},{9,1},... | collective-permute-start | bytes 688136 | tf_op jit(solution)/shard_map/ppermute | solution.py:635
  67.9 1.5 %collective-permute-start.22 = (bf16[896,128]{1,0:T(8,128)(2,1)S(1)}, bf16[896,128]{1,0:T(8,128)(2,1)S(1)}, u32[]{:S(2)}, u32[]{:S(2)}) collective-permute-start(bf16[896,128]{1,0:T(8,128)(2,1)S(1)} %collective-permute-done.21.refs_1_), channel_id=1, source_target_pairs={{0,8},{1,9},{2,10},{3,11},{4,12},{5,13},{6,14},{7,15},{8,0},{9,1},... | collective-permute-start | bytes 688136 | tf_op jit(solution)/shard_map/ppermute | solution.py:635
  (3 other events, 10.9 us)
